TPU v7x, 768 devices: a whole 4x8x12 slice. The times are simulated.
768 devices in a mesh: outer: 192 (over z_lo, x, y, core), inner: 4 (over z_hi).
Axes of the slice: x: 4, y: 8, z: 12 (z_hi: 4, z_lo: 3; z = z_hi * 3 + z_lo), core: 2. Of those that a mesh axis runs over, the one named last changes fastest.
Arguments:
- images: bfloat16 [196608, 1152], P(('outer', 'inner')), may hold values from -0.625 to 0.625
- texts: bfloat16 [196608, 1152], P(('outer', 'inner')), may hold values from -0.625 to 0.625
- positive: int32 [196608], P(('outer', 'inner')), may hold values from 0 to 196607, as said below
- logit_scale: float32 [1], replicated, may hold values from 8 to 12
- logit_bias: float32 [1], replicated, may hold values from -8 to -5
Outputs:
- loss_rows: float32 [196608], P(('outer', 'inner'))
- image_grad: bfloat16 [196608, 1152], P(('outer', 'inner'))
- text_grad: bfloat16 [196608, 1152], P(('outer', 'inner'))
Inputs may be any that keep to these rules, and one draw needn't show every extreme that they name: positive[i] lies in the window W(i) of image i: a text of its own group or of the group before it, cyclically; group size 1024.
All inputs are finite; a program needn't handle non-finite values.
Results may differ from a plain program's by a relative error of at most 0.0039.
Values may be sent and summed in bfloat16 or wider, within the bound.
No kernel may reach another device: no remote copies, remote signals or barrier semaphores. Data moves between devices by JAX's collectives and lax.ppermute only.
A program may use at most 64 MiB of HBM per device.

v0:
```python
import jax
import jax.numpy as jnp
from jax import lax
from jax.sharding import PartitionSpec as P


def from_behind(block, axis, distance):
    devices = range(lax.axis_size(axis))
    route = [((i - distance) % len(devices), i) for i in devices]
    return lax.ppermute(block, axis, route)


def per_device(images, texts, positive, logit_scale, logit_bias):
    scale = logit_scale[0]
    bias = logit_bias[0]
    rows = texts.shape[0]
    width = rows * lax.axis_size("inner")
    count = lax.axis_size("outer")
    where_outer = lax.axis_index("outer")
    group = lax.all_gather(texts, "inner", axis=0, tiled=True)
    prior = from_behind(group, "outer", 1)
    window = jnp.concatenate([group, prior], axis=0)
    cols = jnp.arange(width, dtype=jnp.int32)
    ids = jnp.concatenate(
        [where_outer * width + cols, (where_outer - 1 + count) % count * width + cols]
    )
    hits = positive[:, None] == ids[None, :]
    logits = (
        scale
        * lax.dot_general(
            images, window, (((1,), (1,)), ((), ())), preferred_element_type=jnp.float32
        )
        + bias
    )
    signs = jnp.where(hits, 1.0, -1.0).astype(jnp.float32)
    loss_rows = jnp.sum(jax.nn.softplus(-signs * logits), axis=1)
    weights = (jax.nn.sigmoid(logits) - hits.astype(jnp.float32)).astype(jnp.bfloat16)
    image_grad = (scale * jnp.dot(weights, window, preferred_element_type=jnp.float32)).astype(
        jnp.bfloat16
    )
    parts = lax.dot_general(
        weights, images, (((0,), (0,)), ((), ())), preferred_element_type=jnp.float32
    )
    own_part = parts[:width]
    prior_part = parts[width:]
    returned = from_behind(prior_part, "outer", -1)
    summed = lax.psum_scatter(own_part + returned, "inner", scatter_dimension=0, tiled=True)
    text_grad = (scale * summed).astype(jnp.bfloat16)
    return (loss_rows, image_grad, text_grad)


def solution(mesh):
    return jax.shard_map(
        per_device,
        mesh=mesh,
        in_specs=(
            P(("outer", "inner"), None),
            P(("outer", "inner"), None),
            P(("outer", "inner")),
            P(),
            P(),
        ),
        out_specs=(P(("outer", "inner")), P(("outer", "inner"), None), P(("outer", "inner"), None)),
        check_vma=False,
    )
```

profile of v0, /device:TPU:67, one launch (start us, length us, event | category | flops | bytes accessed | tf_op | source)
XLA Modules:
  0.0 342.2 jit_solution(16715334778825475922)
XLA Ops:
  7.2 0.0 copy-start
  7.2 0.0 all-gather.2.cloned.1.call-start
  7.2 0.7 all-gather.2.cloned.1.call-update
  7.9 0.0 reduce-scatter.2.cloned.1.call-start
  8.0 90.2 %all-gather.2.cloned.1.call-done = bf16[1024,1152]{1,0:T(8,128)(2,1)} async-done(((bf16[256,1152]{1,0:T(8,128)(2,1)}), bf16[1024,1152]{1,0:T(8,128)(2,1)}) %all-gather.2.cloned.1.call-update) | async-done | bytes 2359312 | tf_op jit(solution)/shard_map/all_gather | solution.py:20
  98.2 3.7 %collective-permute-start = (bf16[1024,1152]{1,0:T(8,128)(2,1)}, bf16[1024,1152]{1,0:T(8,128)(2,1)S(1)}, u32[]{:S(2)}, u32[]{:S(2)}) collective-permute-start(bf16[1024,1152]{1,0:T(8,128)(2,1)} %all-gather.2.cloned.1.call-done), channel_id=1, source_target_pairs={{764,0},{0,4},{4,8},{8,12},{12,16},{16,20},{20,24},{24,28},{28,32}... | collective-permute-start | bytes 7077896 | tf_op jit(solution)/shard_map/ppermute | solution.py:10
  103.2 1.8 constant_dynamic-update-slice_fusion.1
  105.1 0.0 copy-start.2
  105.1 22.9 %collective-permute-done = bf16[1024,1152]{1,0:T(8,128)(2,1)S(1)} collective-permute-done((bf16[1024,1152]{1,0:T(8,128)(2,1)}, bf16[1024,1152]{1,0:T(8,128)(2,1)S(1)}, u32[]{:S(2)}, u32[]{:S(2)}) %collective-permute-start) | collective-permute-done | bytes 2359328 | tf_op jit(solution)/shard_map/ppermute | solution.py:10
  128.0 0.4 constant_dynamic-update-slice_fusion
  128.3 0.0 copy-start.1
  128.3 0.0 copy-done
  128.3 0.0 copy-done.2
  128.3 3.3 fusion.7
  131.7 0.0 copy-done.1
  131.7 1.8 fusion.8
  133.5 0.3 slice.9
  133.8 5.3 %collective-permute-start.1 = (f32[1024,1152]{1,0:T(8,128)S(1)}, f32[1024,1152]{1,0:T(8,128)S(1)}, u32[]{:S(2)}, u32[]{:S(2)}) collective-permute-start(f32[1024,1152]{1,0:T(8,128)S(1)} %slice.9), channel_id=1, source_target_pairs={{4,0},{8,4},{12,8},{16,12},{20,16},{24,20},{28,24},{32,28},{36,32}... | collective-permute-start | bytes 14155784 | tf_op jit(solution)/shard_map/ppermute | solution.py:10
  139.1 50.8 %collective-permute-done.1 = f32[1024,1152]{1,0:T(8,128)S(1)} collective-permute-done((f32[1024,1152]{1,0:T(8,128)S(1)}, f32[1024,1152]{1,0:T(8,128)S(1)}, u32[]{:S(2)}, u32[]{:S(2)}) %collective-permute-start.1) | collective-permute-done | bytes 4718624 | tf_op jit(solution)/shard_map/ppermute | solution.py:10
  189.9 2.6 slice_add_fusion
  192.5 0.0 reduce-scatter.2.cloned.1.call-update
  192.6 4.8 %fusion.2 = bf16[256,1152]{1,0:T(8,128)(2,1)} fusion(bf16[2048,1152]{1,0:T(8,128)(2,1)} %copy-done.1, f32[]{:T(128)} %bitcast.9, f32[256,2048]{0,1:T(8,128)S(1)} %get-tuple-element.4, s32[256]{0:T(256)S(1)} %copy-done.2, s32[2048]{0:T(1024)S(1)} %pad_add_fusion), kind=kOutput, calls=%fused_computation.8 | convolution fusion | flops 1212219392 | bytes 7414788 | tf_op jit(solution)/shard_map/dot_general | solution.py:38
  197.4 135.8 %reduce-scatter.2.cloned.1.call-done = f32[256,1152]{1,0:T(8,128)} async-done(((f32[1024,1152]{1,0:T(8,128)}), f32[256,1152]{1,0:T(8,128)}) %reduce-scatter.2.cloned.1.call-update) | async-done | bytes 1179664 | tf_op jit(solution)/shard_map/reduce_scatter | solution.py:47
  333.2 2.2 multiply_convert_fusion
  (2 shorter events, 0.0 us)
Async XLA Ops:
  7.2 121.2 %copy-start = (bf16[256,1152]{1,0:T(8,128)(2,1)S(1)}, bf16[256,1152]{1,0:T(8,128)(2,1)}, u32[]{:S(2)}) copy-start(bf16[256,1152]{1,0:T(8,128)(2,1)} %param.5) | copy-start | bytes 1769476
  7.2 91.0 %all-gather.2.cloned.1.call-start = ((), (), s32[]{:S(2)}) async-start(), calls=%async_computation.1 | async-start | bytes 2949120 | tf_op jit(solution)/shard_map/all_gather | solution.py:20
  7.9 325.3 %reduce-scatter.2.cloned.1.call-start = ((), (), s32[]{:S(2)}) async-start(), calls=%async_computation.2 | async-start | bytes 5898240 | tf_op jit(solution)/shard_map/reduce_scatter | solution.py:47
  98.2 29.8 %collective-permute-start = (bf16[1024,1152]{1,0:T(8,128)(2,1)}, bf16[1024,1152]{1,0:T(8,128)(2,1)S(1)}, u32[]{:S(2)}, u32[]{:S(2)}) collective-permute-start(bf16[1024,1152]{1,0:T(8,128)(2,1)} %all-gather.2.cloned.1.call-done), channel_id=1, source_target_pairs={{764,0},{0,4},{4,8},{8,12},{12,16},{16,20},{20,24},{24,28},{28,32}... | collective-permute-start | bytes 7077896 | tf_op jit(solution)/shard_map/ppermute | solution.py:10
  105.1 23.3 %copy-start.2 = (s32[256]{0:T(256)S(1)}, s32[256]{0:T(256)}, u32[]{:S(2)}) copy-start(s32[256]{0:T(256)} %param.7) | copy-start | bytes 3076
  128.3 3.3 copy-start.1
  133.8 56.1 %collective-permute-start.1 = (f32[1024,1152]{1,0:T(8,128)S(1)}, f32[1024,1152]{1,0:T(8,128)S(1)}, u32[]{:S(2)}, u32[]{:S(2)}) collective-permute-start(f32[1024,1152]{1,0:T(8,128)S(1)} %slice.9), channel_id=1, source_target_pairs={{4,0},{8,4},{12,8},{16,12},{20,16},{24,20},{28,24},{32,28},{36,32}... | collective-permute-start | bytes 14155784 | tf_op jit(solution)/shard_map/ppermute | solution.py:10
Sparse Core Ops, SparseCore 0:
  10.4 87.7 all-gather.1
  192.7 140.4 reduce-scatter.1
where the time goes:
time: 342 us
  waiting for transfers between devices  300 us (88%)
  between operations  15.4 us (5%)
  matrix products  9.95 us (3%)
  starting transfers between devices  9.04 us (3%)
  other arithmetic  4.8 us (1%)
    reduce_scatter x1, waiting for transfers between devices, per_device(): lax.psum_scatter(own_part + returned, 'inner', scatter_dimension=0, tiled...  136 us
    all_gather x1, waiting for transfers between devices, per_device(): group = lax.all_gather(texts, 'inner', axis=0, tiled=True)  90.2 us
    ppermute x2, waiting for transfers between devices, from_behind(): return lax.ppermute(block, axis, route)  73.7 us
    ppermute x2, starting transfers between devices, from_behind(): return lax.ppermute(block, axis, route)  8.96 us
  transfers between devices with their start and end apart: 4, of which 4 were waited for; matrix products, arithmetic and copies ran while one was open for 2% of the time, Pallas kernels for 0%

commit v1 on v0

v1 whole, which is shorter than its diff:
```python
import jax
import jax.numpy as jnp
from jax import lax
from jax.sharding import PartitionSpec as P

IMAGE_PAIRS = [(0, 1), (1, 0), (2, 3), (3, 2)]
TEXT_PAIRS = [(1, 2), (2, 1), (3, 0), (0, 3)]


def from_behind(block, distance):
    count = lax.axis_size("outer")
    return lax.ppermute(block, "outer", [((i - distance) % count, i) for i in range(count)])


def per_device(images, texts, positive, logit_scale, logit_bias):
    scale = logit_scale[0]
    bias = logit_bias[0]
    rows = texts.shape[0]
    count = lax.axis_size("outer")
    group = lax.axis_index("outer")
    me = lax.axis_index("inner")
    other = 3 - me
    there = lax.ppermute(positive, "inner", IMAGE_PAIRS)
    texts_there = lax.ppermute(texts, "inner", TEXT_PAIRS)
    images_there = lax.ppermute(images, "inner", IMAGE_PAIRS)
    prior = from_behind(texts, 1)
    prior_there = from_behind(texts_there, 1)

    image_pair = jnp.concatenate([images, images_there], axis=0)
    window = jnp.concatenate([texts, texts_there, prior, prior_there], axis=0)
    positives = jnp.concatenate([positive, there])
    width = 4 * rows
    before = (group - 1 + count) % count
    cols = jnp.arange(rows, dtype=jnp.int32)
    ids = jnp.concatenate(
        [
            group * width + me * rows + cols,
            group * width + other * rows + cols,
            before * width + me * rows + cols,
            before * width + other * rows + cols,
        ]
    )
    hits = positives[:, None] == ids[None, :]
    logits = (
        scale
        * lax.dot_general(
            image_pair, window, (((1,), (1,)), ((), ())), preferred_element_type=jnp.float32
        )
        + bias
    )
    signs = jnp.where(hits, 1.0, -1.0).astype(jnp.float32)
    losses = jnp.sum(jax.nn.softplus(-signs * logits), axis=1)
    weights = (jax.nn.sigmoid(logits) - hits.astype(jnp.float32)).astype(jnp.bfloat16)

    text_parts = lax.dot_general(
        weights, image_pair, (((0,), (0,)), ((), ())), preferred_element_type=jnp.float32
    )
    returned = from_behind(text_parts[2 * rows :].astype(jnp.bfloat16), -1)
    image_parts = jnp.dot(weights, window, preferred_element_type=jnp.float32)
    image_back = lax.ppermute(image_parts[rows:].astype(jnp.bfloat16), "inner", IMAGE_PAIRS)
    loss_back = lax.ppermute(losses[rows:], "inner", IMAGE_PAIRS)
    text_sum = text_parts[: 2 * rows] + returned.astype(jnp.float32)
    text_back = lax.ppermute(text_sum[rows:].astype(jnp.bfloat16), "inner", TEXT_PAIRS)

    loss_rows = losses[:rows] + loss_back
    image_grad = (scale * (image_parts[:rows] + image_back.astype(jnp.float32))).astype(jnp.bfloat16)
    text_grad = (scale * (text_sum[:rows] + text_back.astype(jnp.float32))).astype(jnp.bfloat16)
    return (loss_rows, image_grad, text_grad)


def solution(mesh):
    return jax.shard_map(
        per_device,
        mesh=mesh,
        in_specs=(
            P(("outer", "inner"), None),
            P(("outer", "inner"), None),
            P(("outer", "inner")),
            P(),
            P(),
        ),
        out_specs=(P(("outer", "inner")), P(("outer", "inner"), None), P(("outer", "inner"), None)),
        check_vma=False,
    )
```

time: 342 us -> 145 us (0.42)
  the two profiles are of different devices: /device:TPU:67 before, /device:TPU:128 now
where the time goes in v1:
time: 145 us
  waiting for transfers between devices  87.3 us (60%)
  starting transfers between devices  38.4 us (26%)
  matrix products  8.17 us (6%)
  local copies, waits for them, and re-layouts  5.95 us (4%)
  other arithmetic  2.7 us (2%)
  between operations  2.13 us (1%)
    ppermute x3, waiting for transfers between devices, from_behind(): lax.ppermute(block, 'outer', [((i - distance) % count, i) for i in range(...  42 us
    ppermute x1, waiting for transfers between devices, per_device(): texts_there = lax.ppermute(texts, 'inner', TEXT_PAIRS)  23.8 us
    ppermute x1, starting transfers between devices, per_device(): texts_there = lax.ppermute(texts, 'inner', TEXT_PAIRS)  12.8 us
    ppermute x1, waiting for transfers between devices, per_device(): lax.ppermute(image_parts[rows:].astype(jnp.bfloat16), 'inner', IMAGE_PAIRS)  7.26 us
    ppermute x1, waiting for transfers between devices, per_device(): lax.ppermute(text_sum[rows:].astype(jnp.bfloat16), 'inner', TEXT_PAIRS)  7.24 us
    ppermute x1, waiting for transfers between devices, per_device(): images_there = lax.ppermute(images, 'inner', IMAGE_PAIRS)  7.01 us
    ppermute x1, starting transfers between devices, per_device(): lax.ppermute(image_parts[rows:].astype(jnp.bfloat16), 'inner', IMAGE_PAIRS)  6.93 us
    ppermute x3, starting transfers between devices, from_behind(): lax.ppermute(block, 'outer', [((i - distance) % count, i) for i in range(...  5.98 us
  transfers between devices with their start and end apart: 9, of which 6 were waited for; matrix products, arithmetic and copies ran while one was open for 6% of the time, Pallas kernels for 0%

profile of v1, /device:TPU:128, one launch (start us, length us, event | category | flops | bytes accessed | tf_op | source)
XLA Modules:
  0.0 144.6 jit_solution(12885910713729638652)
XLA Ops:
  0.6 0.0 copy-start.1
  0.6 12.8 %collective-permute-start.2 = (bf16[256,1152]{1,0:T(8,128)(2,1)}, bf16[256,1152]{1,0:T(8,128)(2,1)S(1)}, u32[]{:S(2)}, u32[]{:S(2)}) collective-permute-start(bf16[256,1152]{1,0:T(8,128)(2,1)} %param.6), channel_id=1, source_target_pairs={{1,2},{2,1},{3,0},{0,3},{5,6},{6,5},{7,4},{4,7},{9,10},{10,9},{11,... | collective-permute-start | bytes 1769480 | tf_op jit(solution)/shard_map/ppermute | solution.py:24
  13.4 1.9 %collective-permute-start.3 = (bf16[256,1152]{1,0:T(8,128)(2,1)}, bf16[256,1152]{1,0:T(8,128)(2,1)S(1)}, u32[]{:S(2)}, u32[]{:S(2)}) collective-permute-start(bf16[256,1152]{1,0:T(8,128)(2,1)} %param.6), channel_id=1, source_target_pairs={{764,0},{0,4},{4,8},{8,12},{12,16},{16,20},{20,24},{24,28},{28,32}... | collective-permute-start | bytes 1769480 | tf_op jit(solution)/shard_map/ppermute | solution.py:12
  15.3 3.0 %collective-permute-start = (s32[256]{0:T(256)}, s32[256]{0:T(256)S(1)}, u32[]{:S(2)}, u32[]{:S(2)}) collective-permute-start(s32[256]{0:T(256)} %param.7), channel_id=1, source_target_pairs={{0,1},{1,0},{2,3},{3,2},{4,5},{5,4},{6,7},{7,6},{8,9},{9,8},{10,11... | collective-permute-start | bytes 3080 | tf_op jit(solution)/shard_map/ppermute | solution.py:23
  18.4 5.8 %collective-permute-start.1 = (bf16[256,1152]{1,0:T(8,128)(2,1)}, bf16[256,1152]{1,0:T(8,128)(2,1)S(1)}, u32[]{:S(2)}, u32[]{:S(2)}) collective-permute-start(bf16[256,1152]{1,0:T(8,128)(2,1)} %param.5), channel_id=1, source_target_pairs={{0,1},{1,0},{2,3},{3,2},{4,5},{5,4},{6,7},{7,6},{8,9},{9,8},{10,11... | collective-permute-start | bytes 1769480 | tf_op jit(solution)/shard_map/ppermute | solution.py:25
  24.2 1.1 constant_dynamic-update-slice_fusion.1
  25.4 1.9 %constant_dynamic-update-slice_fusion.5 = bf16[1024,1152]{1,0:T(8,128)(2,1)} fusion(bf16[256,1152]{1,0:T(8,128)(2,1)} %param.6), kind=kLoop, calls=%fused_computation.24 | loop fusion | bytes 1179648
  28.6 23.8 %collective-permute-done.2 = bf16[256,1152]{1,0:T(8,128)(2,1)S(1)} collective-permute-done((bf16[256,1152]{1,0:T(8,128)(2,1)}, bf16[256,1152]{1,0:T(8,128)(2,1)S(1)}, u32[]{:S(2)}, u32[]{:S(2)}) %collective-permute-start.2) | collective-permute-done | bytes 589856 | tf_op jit(solution)/shard_map/ppermute | solution.py:24
  52.4 1.9 %collective-permute-start.4 = (bf16[256,1152]{1,0:T(8,128)(2,1)S(1)}, bf16[256,1152]{1,0:T(8,128)(2,1)S(1)}, u32[]{:S(2)}, u32[]{:S(2)}) collective-permute-start(bf16[256,1152]{1,0:T(8,128)(2,1)S(1)} %collective-permute-done.2), channel_id=1, source_target_pairs={{764,0},{0,4},{4,8},{8,12},{12,16},{16,20},{20,24},{24,28},{28,32}... | collective-permute-start | bytes 1769480 | tf_op jit(solution)/shard_map/ppermute | solution.py:12
  54.3 0.0 collective-permute-done
  54.3 0.0 copy-done.1
  54.3 0.9 constant_dynamic-update-slice_fusion.4
  55.2 0.0 collective-permute-done.3
  55.2 0.9 constant_dynamic-update-slice_fusion.3
  56.1 7.0 %collective-permute-done.1 = bf16[256,1152]{1,0:T(8,128)(2,1)S(1)} collective-permute-done((bf16[256,1152]{1,0:T(8,128)(2,1)}, bf16[256,1152]{1,0:T(8,128)(2,1)S(1)}, u32[]{:S(2)}, u32[]{:S(2)}) %collective-permute-start.1) | collective-permute-done | bytes 589856 | tf_op jit(solution)/shard_map/ppermute | solution.py:25
  63.1 10.9 %collective-permute-done.4 = bf16[256,1152]{1,0:T(8,128)(2,1)S(1)} collective-permute-done((bf16[256,1152]{1,0:T(8,128)(2,1)S(1)}, bf16[256,1152]{1,0:T(8,128)(2,1)S(1)}, u32[]{:S(2)}, u32[]{:S(2)}) %collective-permute-start.4) | collective-permute-done | bytes 589856 | tf_op jit(solution)/shard_map/ppermute | solution.py:12
  73.9 0.9 constant_dynamic-update-slice_fusion
  74.8 4.4 %fusion.4 = (f32[512]{0:T(512)S(1)}, f32[512,1024]{1,0:T(8,128)S(1)}) fusion(f32[]{:T(128)} %bitcast.11, f32[]{:T(128)} %bitcast.6, s32[1024]{0:T(1024)S(1)} %pad_add_fusion, s32[512]{0:T(512)S(1)} %pad_add_fusion.1, bf16[512,1152]{1,0:T(8,128)(2,1)S(1)} %get-tuple-element.9, bf16[1024,1152]{1,0:T(8,128)(2,1)} %get-tuple-element.10), kind=kOutput, calls=%fused_computation.9 | convolution fusion | flops 1214774784 | bytes 5644296 | tf_op jit(solution)/shard_map/dot_general | solution.py:46
  79.3 1.8 %fusion.9 = f32[1024,1152]{1,0:T(8,128)S(1)} fusion(bf16[512,1152]{1,0:T(8,128)(2,1)S(1)} %get-tuple-element.9, f32[512,1024]{1,0:T(8,128)S(1)} %get-tuple-element.4, f32[]{:T(128)} %bitcast.13, f32[]{:T(128)} %bitcast.10, s32[1024]{0:T(1024)S(1)} %pad_add_fusion, s32[512]{0:T(512)S(1)} %pad_add_fusion.1), kind=kOutput, calls=%fused_computation.32 | convolution fusion | flops 1212678144 | bytes 8001544 | tf_op jit(solution)/shard_map/dot_general | solution.py:55
  81.1 0.0 copy-start
  81.1 0.1 slice.56
  81.2 2.1 %collective-permute-start.7 = (bf16[512,1152]{1,0:T(8,128)(2,1)S(1)}, bf16[512,1152]{1,0:T(8,128)(2,1)S(1)}, u32[]{:S(2)}, u32[]{:S(2)}) collective-permute-start(bf16[512,1152]{1,0:T(8,128)(2,1)S(1)} %slice.56), channel_id=1, source_target_pairs={{4,0},{8,4},{12,8},{16,12},{20,16},{24,20},{28,24},{32,28},{36,32}... | collective-permute-start | bytes 3538952 | tf_op jit(solution)/shard_map/ppermute | solution.py:12
  83.4 1.9 %collective-permute-start.5 = (f32[256]{0:T(256)S(1)}, f32[256]{0:T(256)S(1)}, u32[]{:S(2)}, u32[]{:S(2)}) collective-permute-start(f32[256]{0:T(256)S(1)} %slice.28), channel_id=1, source_target_pairs={{0,1},{1,0},{2,3},{3,2},{4,5},{5,4},{6,7},{7,6},{8,9},{9,8},{10,11... | collective-permute-start | bytes 3080 | tf_op jit(solution)/shard_map/ppermute | solution.py:61
  85.3 0.0 copy-done
  85.3 1.9 %fusion.11 = f32[512,1152]{1,0:T(8,128)S(1)} fusion(bf16[1024,1152]{1,0:T(8,128)(2,1)S(1)} %copy-done, f32[512,1024]{1,0:T(8,128)S(1)} %get-tuple-element.4, f32[]{:T(128)} %bitcast.12, f32[]{:T(128)} %bitcast.8, s32[1024]{0:T(1024)S(1)} %pad_add_fusion, s32[512]{0:T(512)S(1)} %pad_add_fusion.1), kind=kOutput, calls=%fused_computation.33 | convolution fusion | flops 1212678144 | bytes 6821896 | tf_op jit(solution)/shard_map/dot_general | solution.py:59
  87.3 0.1 slice.58
  87.3 6.9 %collective-permute-start.6 = (bf16[256,1152]{1,0:T(8,128)(2,1)S(1)}, bf16[256,1152]{1,0:T(8,128)(2,1)S(1)}, u32[]{:S(2)}, u32[]{:S(2)}) collective-permute-start(bf16[256,1152]{1,0:T(8,128)(2,1)S(1)} %slice.58), channel_id=1, source_target_pairs={{0,1},{1,0},{2,3},{3,2},{4,5},{5,4},{6,7},{7,6},{8,9},{9,8},{10,11... | collective-permute-start | bytes 1769480 | tf_op jit(solution)/shard_map/ppermute | solution.py:60
  94.3 31.1 %collective-permute-done.7 = bf16[512,1152]{1,0:T(8,128)(2,1)S(1)} collective-permute-done((bf16[512,1152]{1,0:T(8,128)(2,1)S(1)}, bf16[512,1152]{1,0:T(8,128)(2,1)S(1)}, u32[]{:S(2)}, u32[]{:S(2)}) %collective-permute-start.7) | collective-permute-done | bytes 1179680 | tf_op jit(solution)/shard_map/ppermute | solution.py:12
  125.4 0.2 slice_add_fusion
  125.6 0.1 slice.57
  125.7 1.9 %collective-permute-start.8 = (bf16[256,1152]{1,0:T(8,128)(2,1)S(1)}, bf16[256,1152]{1,0:T(8,128)(2,1)S(1)}, u32[]{:S(2)}, u32[]{:S(2)}) collective-permute-start(bf16[256,1152]{1,0:T(8,128)(2,1)S(1)} %slice.57), channel_id=1, source_target_pairs={{1,2},{2,1},{3,0},{0,3},{5,6},{6,5},{7,4},{4,7},{9,10},{10,9},{11,... | collective-permute-start | bytes 1769480 | tf_op jit(solution)/shard_map/ppermute | solution.py:63
  127.6 0.0 collective-permute-done.5
  127.6 0.6 slice_add_fusion.3
  128.2 7.3 %collective-permute-done.6 = bf16[256,1152]{1,0:T(8,128)(2,1)S(1)} collective-permute-done((bf16[256,1152]{1,0:T(8,128)(2,1)S(1)}, bf16[256,1152]{1,0:T(8,128)(2,1)S(1)}, u32[]{:S(2)}, u32[]{:S(2)}) %collective-permute-start.6) | collective-permute-done | bytes 589856 | tf_op jit(solution)/shard_map/ppermute | solution.py:60
  135.4 1.0 fusion.8
  136.4 7.2 %collective-permute-done.8 = bf16[256,1152]{1,0:T(8,128)(2,1)S(1)} collective-permute-done((bf16[256,1152]{1,0:T(8,128)(2,1)S(1)}, bf16[256,1152]{1,0:T(8,128)(2,1)S(1)}, u32[]{:S(2)}, u32[]{:S(2)}) %collective-permute-start.8) | collective-permute-done | bytes 589856 | tf_op jit(solution)/shard_map/ppermute | solution.py:63
  143.6 1.0 fusion.6
  (5 shorter events, 0.0 us)
Async XLA Ops:
  0.6 53.7 %copy-start.1 = (s32[256]{0:T(256)S(1)}, s32[256]{0:T(256)}, u32[]{:S(2)}) copy-start(s32[256]{0:T(256)} %param.7) | copy-start | bytes 3076
  0.6 51.8 %collective-permute-start.2 = (bf16[256,1152]{1,0:T(8,128)(2,1)}, bf16[256,1152]{1,0:T(8,128)(2,1)S(1)}, u32[]{:S(2)}, u32[]{:S(2)}) collective-permute-start(bf16[256,1152]{1,0:T(8,128)(2,1)} %param.6), channel_id=1, source_target_pairs={{1,2},{2,1},{3,0},{0,3},{5,6},{6,5},{7,4},{4,7},{9,10},{10,9},{11,... | collective-permute-start | bytes 1769480 | tf_op jit(solution)/shard_map/ppermute | solution.py:24
  13.4 41.8 %collective-permute-start.3 = (bf16[256,1152]{1,0:T(8,128)(2,1)}, bf16[256,1152]{1,0:T(8,128)(2,1)S(1)}, u32[]{:S(2)}, u32[]{:S(2)}) collective-permute-start(bf16[256,1152]{1,0:T(8,128)(2,1)} %param.6), channel_id=1, source_target_pairs={{764,0},{0,4},{4,8},{8,12},{12,16},{16,20},{20,24},{24,28},{28,32}... | collective-permute-start | bytes 1769480 | tf_op jit(solution)/shard_map/ppermute | solution.py:12
  15.3 39.0 %collective-permute-start = (s32[256]{0:T(256)}, s32[256]{0:T(256)S(1)}, u32[]{:S(2)}, u32[]{:S(2)}) collective-permute-start(s32[256]{0:T(256)} %param.7), channel_id=1, source_target_pairs={{0,1},{1,0},{2,3},{3,2},{4,5},{5,4},{6,7},{7,6},{8,9},{9,8},{10,11... | collective-permute-start | bytes 3080 | tf_op jit(solution)/shard_map/ppermute | solution.py:23
  18.4 44.7 %collective-permute-start.1 = (bf16[256,1152]{1,0:T(8,128)(2,1)}, bf16[256,1152]{1,0:T(8,128)(2,1)S(1)}, u32[]{:S(2)}, u32[]{:S(2)}) collective-permute-start(bf16[256,1152]{1,0:T(8,128)(2,1)} %param.5), channel_id=1, source_target_pairs={{0,1},{1,0},{2,3},{3,2},{4,5},{5,4},{6,7},{7,6},{8,9},{9,8},{10,11... | collective-permute-start | bytes 1769480 | tf_op jit(solution)/shard_map/ppermute | solution.py:25
  52.4 21.6 %collective-permute-start.4 = (bf16[256,1152]{1,0:T(8,128)(2,1)S(1)}, bf16[256,1152]{1,0:T(8,128)(2,1)S(1)}, u32[]{:S(2)}, u32[]{:S(2)}) collective-permute-start(bf16[256,1152]{1,0:T(8,128)(2,1)S(1)} %collective-permute-done.2), channel_id=1, source_target_pairs={{764,0},{0,4},{4,8},{8,12},{12,16},{16,20},{20,24},{24,28},{28,32}... | collective-permute-start | bytes 1769480 | tf_op jit(solution)/shard_map/ppermute | solution.py:12
  81.1 4.2 %copy-start = (bf16[1024,1152]{1,0:T(8,128)(2,1)S(1)}, bf16[1024,1152]{1,0:T(8,128)(2,1)}, u32[]{:S(2)}) copy-start(bf16[1024,1152]{1,0:T(8,128)(2,1)} %get-tuple-element.10) | copy-start | bytes 7077892
  81.2 44.2 %collective-permute-start.7 = (bf16[512,1152]{1,0:T(8,128)(2,1)S(1)}, bf16[512,1152]{1,0:T(8,128)(2,1)S(1)}, u32[]{:S(2)}, u32[]{:S(2)}) collective-permute-start(bf16[512,1152]{1,0:T(8,128)(2,1)S(1)} %slice.56), channel_id=1, source_target_pairs={{4,0},{8,4},{12,8},{16,12},{20,16},{24,20},{28,24},{32,28},{36,32}... | collective-permute-start | bytes 3538952 | tf_op jit(solution)/shard_map/ppermute | solution.py:12
  83.4 44.2 %collective-permute-start.5 = (f32[256]{0:T(256)S(1)}, f32[256]{0:T(256)S(1)}, u32[]{:S(2)}, u32[]{:S(2)}) collective-permute-start(f32[256]{0:T(256)S(1)} %slice.28), channel_id=1, source_target_pairs={{0,1},{1,0},{2,3},{3,2},{4,5},{5,4},{6,7},{7,6},{8,9},{9,8},{10,11... | collective-permute-start | bytes 3080 | tf_op jit(solution)/shard_map/ppermute | solution.py:61
  87.3 48.1 %collective-permute-start.6 = (bf16[256,1152]{1,0:T(8,128)(2,1)S(1)}, bf16[256,1152]{1,0:T(8,128)(2,1)S(1)}, u32[]{:S(2)}, u32[]{:S(2)}) collective-permute-start(bf16[256,1152]{1,0:T(8,128)(2,1)S(1)} %slice.58), channel_id=1, source_target_pairs={{0,1},{1,0},{2,3},{3,2},{4,5},{5,4},{6,7},{7,6},{8,9},{9,8},{10,11... | collective-permute-start | bytes 1769480 | tf_op jit(solution)/shard_map/ppermute | solution.py:60
  125.7 18.0 %collective-permute-start.8 = (bf16[256,1152]{1,0:T(8,128)(2,1)S(1)}, bf16[256,1152]{1,0:T(8,128)(2,1)S(1)}, u32[]{:S(2)}, u32[]{:S(2)}) collective-permute-start(bf16[256,1152]{1,0:T(8,128)(2,1)S(1)} %slice.57), channel_id=1, source_target_pairs={{1,2},{2,1},{3,0},{0,3},{5,6},{6,5},{7,4},{4,7},{9,10},{10,9},{11,... | collective-permute-start | bytes 1769480 | tf_op jit(solution)/shard_map/ppermute | solution.py:63

commit v2 on v0

v2 whole, which is shorter than its diff:
```python
import jax
import jax.numpy as jnp
from jax import lax
from jax.experimental import pallas as pl
from jax.experimental.pallas import tpu as pltpu
from jax.sharding import PartitionSpec as P

IMAGE_PAIRS = [(0, 1), (1, 0), (2, 3), (3, 2)]
TEXT_PAIRS = [(1, 2), (2, 1), (3, 0), (0, 3)]

VMEM = pl.BlockSpec(memory_space=pltpu.VMEM)
SMEM = pl.BlockSpec(memory_space=pltpu.SMEM)
LIMIT = 40 * 1024 * 1024


def from_behind(block, distance):
    count = lax.axis_size("outer")
    return lax.ppermute(block, "outer", [((i - distance) % count, i) for i in range(count)])


def over_last(x, y):
    return lax.dot_general(x, y, (((1,), (1,)), ((), ())), preferred_element_type=jnp.float32)


def over_first(x, y):
    return lax.dot_general(x, y, (((0,), (0,)), ((), ())), preferred_element_type=jnp.float32)


def block_logits(texts, images, positive, first, scale, bias):
    logits = scale * over_last(texts, images) + bias
    row = lax.broadcasted_iota(jnp.int32, logits.shape, 0)
    return logits, row == positive - first


def block_weights(logits, hits):
    decay = jnp.exp(-jnp.abs(logits))
    share = 1.0 / (1.0 + decay)
    sigmoid = jnp.where(logits >= 0.0, share, decay * share)
    weights = (sigmoid - hits.astype(jnp.float32)).astype(jnp.bfloat16)
    return weights, decay


def block_loss(logits, hits, decay):
    signed = jnp.where(hits, -logits, logits)
    return jnp.sum(jnp.maximum(signed, 0.0) + jnp.log1p(decay), axis=0, keepdims=True)


def hold_kernel(images, texts, positive, images_out, texts_out, positive_out):
    images_out[...] = images[...]
    texts_out[...] = texts[...]
    positive_out[...] = positive[...]


def first_kernel(
    firsts, reals, image_0, image_1, text_0, text_1, prior, after, near, far, image_part, text_part, loss
):
    scale, bias = reals[0], reals[1]
    rows = image_0.shape[0]
    images, texts = (image_0, image_1), (text_0, text_1)
    for j in range(2):
        losses = jnp.zeros((1, rows), jnp.float32)
        total = None
        for k, text in enumerate((text_0, text_1, prior)):
            logits, hits = block_logits(
                text[...], images[j][...], near[pl.ds(j, 1), :], firsts[k], scale, bias
            )
            weights, decay = block_weights(logits, hits)
            losses += block_loss(logits, hits, decay)
            part = over_first(weights, text[...])
            total = part if total is None else total + part
            if k < 2:
                half = pl.ds(k * rows, rows)
                added = jnp.dot(weights, images[j][...], preferred_element_type=jnp.float32)
                text_part[half, :] = added if j == 0 else text_part[half, :] + added
        image_part[pl.ds(j * rows, rows), :] = total
        loss[pl.ds(j, 1), :] = losses
    for k in range(2):
        logits, hits = block_logits(texts[k][...], after[...], far[...], firsts[k], scale, bias)
        weights, _ = block_weights(logits, hits)
        text_part[pl.ds(k * rows, rows), :] += jnp.dot(
            weights, after[...], preferred_element_type=jnp.float32
        )


def image_kernel(
    firsts, reals, image_0, image_1, prior, near, image_part, loss, image_own, image_send, loss_own, loss_send
):
    scale, bias = reals[0], reals[1]
    rows = image_0.shape[0]
    for j, image in ((1, image_1), (0, image_0)):
        logits, hits = block_logits(
            prior[...], image[...], near[pl.ds(j, 1), :], firsts[3], scale, bias
        )
        weights, decay = block_weights(logits, hits)
        losses = loss[pl.ds(j, 1), :] + block_loss(logits, hits, decay)
        total = image_part[pl.ds(j * rows, rows), :] + over_first(weights, prior[...])
        if j == 1:
            image_send[...] = total.astype(jnp.bfloat16)
            loss_send[...] = losses
        else:
            image_own[...] = total
            loss_own[...] = losses


def text_kernel(firsts, reals, text_0, text_1, after, far, text_part, text_own, text_send):
    scale, bias = reals[0], reals[1]
    rows = text_0.shape[0]
    for k, text in ((1, text_1), (0, text_0)):
        logits, hits = block_logits(text[...], after[...], far[...], firsts[k], scale, bias)
        weights, _ = block_weights(logits, hits)
        total = text_part[pl.ds(k * rows, rows), :] + jnp.dot(
            weights, after[...], preferred_element_type=jnp.float32
        )
        if k == 1:
            text_send[...] = total.astype(jnp.bfloat16)
        else:
            text_own[...] = total


def call(kernel, name, in_specs, outs, blocks):
    return pl.pallas_call(
        kernel,
        name=name,
        out_shape=outs,
        in_specs=in_specs,
        out_specs=[VMEM] * len(outs),
        compiler_params=pltpu.CompilerParams(vmem_limit_bytes=LIMIT),
        cost_estimate=pl.CostEstimate(
            flops=2 * blocks * 256 * 256 * 1152, bytes_accessed=1 << 20, transcendentals=0
        ),
    )


def per_device(images, texts, positive, logit_scale, logit_bias):
    rows, width = texts.shape
    count = lax.axis_size("outer")
    group = lax.axis_index("outer")
    me = lax.axis_index("inner")
    whole = lax.axis_size("inner") * rows
    before = (group - 1 + count) % count
    firsts = jnp.stack(
        [
            group * whole + me * rows,
            group * whole + (3 - me) * rows,
            before * whole + me * rows,
            before * whole + (3 - me) * rows,
        ]
    ).astype(jnp.int32)
    reals = jnp.concatenate([logit_scale, logit_bias])
    shard = jax.ShapeDtypeStruct((rows, width), jnp.bfloat16)
    real_shard = jax.ShapeDtypeStruct((rows, width), jnp.float32)
    real_pair = jax.ShapeDtypeStruct((2 * rows, width), jnp.float32)
    line = jax.ShapeDtypeStruct((1, rows), jnp.float32)
    lines = jax.ShapeDtypeStruct((2, rows), jnp.float32)

    text_1 = lax.ppermute(texts, "inner", TEXT_PAIRS)
    image_1 = lax.ppermute(images, "inner", IMAGE_PAIRS)
    images_later, texts_later, mine = call(
        hold_kernel,
        "hold",
        [VMEM] * 3,
        [shard, shard, jax.ShapeDtypeStruct((1, rows), jnp.int32)],
        1,
    )(images, texts, positive[None, :])
    near = jnp.concatenate([mine, lax.ppermute(mine, "inner", IMAGE_PAIRS)])
    prior_0 = from_behind(texts_later, 1)
    after_0 = from_behind(images_later, -1)
    far = from_behind(near, -1)
    prior_1 = from_behind(text_1, 1)
    after_1 = from_behind(image_1, -1)

    image_part, text_part, loss = call(
        first_kernel, "first", [SMEM] * 2 + [VMEM] * 8, [real_pair, real_pair, lines], 20
    )(firsts, reals, images, image_1, texts, text_1, prior_0, after_0, near, far[:1])
    image_own, image_send, loss_own, loss_send = call(
        image_kernel, "image", [SMEM] * 2 + [VMEM] * 6, [real_shard, shard, line, line], 4
    )(firsts, reals, images, image_1, prior_1, near, image_part, loss)
    text_own, text_send = call(
        text_kernel, "text", [SMEM] * 2 + [VMEM] * 5, [real_shard, shard], 4
    )(firsts, reals, texts, text_1, after_1, far[1:], text_part)

    image_back = lax.ppermute(image_send, "inner", IMAGE_PAIRS)
    text_back = lax.ppermute(text_send, "inner", TEXT_PAIRS)
    loss_back = lax.ppermute(loss_send, "inner", IMAGE_PAIRS)
    scale = logit_scale[0]
    loss_rows = (loss_own + loss_back)[0]
    image_grad = (scale * (image_own + image_back.astype(jnp.float32))).astype(jnp.bfloat16)
    text_grad = (scale * (text_own + text_back.astype(jnp.float32))).astype(jnp.bfloat16)
    return (loss_rows, image_grad, text_grad)


def solution(mesh):
    return jax.shard_map(
        per_device,
        mesh=mesh,
        in_specs=(
            P(("outer", "inner"), None),
            P(("outer", "inner"), None),
            P(("outer", "inner")),
            P(),
            P(),
        ),
        out_specs=(P(("outer", "inner")), P(("outer", "inner"), None), P(("outer", "inner"), None)),
        check_vma=False,
    )
```

time: 342 us -> 135 us (0.39)
  the two profiles are of different devices: /device:TPU:67 before, /device:TPU:62 now
where the time goes in v2:
time: 135 us; the launch traced here: 134 us
  starting transfers between devices  69.4 us (51%)
  waiting for transfers between devices  44.3 us (33%)
  Pallas kernels  13.1 us (10%)
  local copies, waits for them, and re-layouts  2.82 us (2%)
  other arithmetic  2.67 us (2%)
  between operations  2.12 us (2%)
    ppermute x1, waiting for transfers between devices, per_device(): loss_back = lax.ppermute(loss_send, 'inner', IMAGE_PAIRS)  34.2 us
    ppermute x5, starting transfers between devices, from_behind(): lax.ppermute(block, 'outer', [((i - distance) % count, i) for i in range(...  27 us
    ppermute x1, starting transfers between devices, per_device(): text_back = lax.ppermute(text_send, 'inner', TEXT_PAIRS)  11.9 us
    ppermute x1, starting transfers between devices, per_device(): text_1 = lax.ppermute(texts, 'inner', TEXT_PAIRS)  9.71 us
    ppermute x1, starting transfers between devices, per_device(): image_1 = lax.ppermute(images, 'inner', IMAGE_PAIRS)  7.9 us
    pallas_call x1, Pallas kernels, per_device(): call(first_kernel, 'first', [SMEM] * 2 + [VMEM] * 8, [real_pair, real_pai...  7 us
    ppermute x1, waiting for transfers between devices, per_device(): near = jnp.concatenate([mine, lax.ppermute(mine, 'inner', IMAGE_PAIRS)])  5.74 us
    ppermute x1, starting transfers between devices, per_device(): loss_back = lax.ppermute(loss_send, 'inner', IMAGE_PAIRS)  5.72 us
  transfers between devices with their start and end apart: 11, of which 3 were waited for; matrix products, arithmetic and copies ran while one was open for 1% of the time, Pallas kernels for 10%

profile of v2, /device:TPU:62, one launch (start us, length us, event | category | flops | bytes accessed | tf_op | source)
XLA Modules:
  0.0 134.4 jit_solution(17332524590777722643)
XLA Ops:
  0.6 7.9 %collective-permute-start = (bf16[256,1152]{1,0:T(8,128)(2,1)}, bf16[256,1152]{1,0:T(8,128)(2,1)S(1)}, u32[]{:S(2)}, u32[]{:S(2)}) collective-permute-start(bf16[256,1152]{1,0:T(8,128)(2,1)} %image_0.3), channel_id=1, source_target_pairs={{0,1},{1,0},{2,3},{3,2},{4,5},{5,4},{6,7},{7,6},{8,9},{9,8},{10,11... | collective-permute-start | bytes 1769480 | tf_op jit(solution)/shard_map/ppermute | solution.py:157
  8.5 9.7 %collective-permute-start.1 = (bf16[256,1152]{1,0:T(8,128)(2,1)}, bf16[256,1152]{1,0:T(8,128)(2,1)S(1)}, u32[]{:S(2)}, u32[]{:S(2)}) collective-permute-start(bf16[256,1152]{1,0:T(8,128)(2,1)} %text_0.3), channel_id=1, source_target_pairs={{1,2},{2,1},{3,0},{0,3},{5,6},{6,5},{7,4},{4,7},{9,10},{10,9},{11,... | collective-permute-start | bytes 1769480 | tf_op jit(solution)/shard_map/ppermute | solution.py:156
  18.3 0.0 copy-start
  18.3 1.1 copy-done
  19.3 0.0 copy-start.2
  19.3 1.1 copy-done.2
  20.4 0.0 copy-start.4
  20.4 0.7 copy-done.4
  21.1 0.0 copy-start.1
  21.1 0.0 copy-start.3
  21.1 1.1 hold.1
  22.2 1.9 %collective-permute-start.4 = (bf16[256,1152]{1,0:T(8,128)(2,1)}, bf16[256,1152]{1,0:T(8,128)(2,1)S(1)}, u32[]{:S(2)}, u32[]{:S(2)}) collective-permute-start(bf16[256,1152]{1,0:T(8,128)(2,1)} %get-tuple-element.16), channel_id=1, source_target_pairs={{764,0},{0,4},{4,8},{8,12},{12,16},{16,20},{20,24},{24,28},{28,32}... | collective-permute-start | bytes 1769480 | tf_op jit(solution)/shard_map/ppermute | solution.py:18
  24.1 3.6 %collective-permute-start.5 = (bf16[256,1152]{1,0:T(8,128)(2,1)}, bf16[256,1152]{1,0:T(8,128)(2,1)S(1)}, u32[]{:S(2)}, u32[]{:S(2)}) collective-permute-start(bf16[256,1152]{1,0:T(8,128)(2,1)} %get-tuple-element.17), channel_id=1, source_target_pairs={{4,0},{8,4},{12,8},{16,12},{20,16},{24,20},{28,24},{32,28},{36,32}... | collective-permute-start | bytes 1769480 | tf_op jit(solution)/shard_map/ppermute | solution.py:18
  27.7 5.2 %collective-permute-start.3 = (s32[1,256]{1,0:T(1,128)S(1)}, s32[1,256]{1,0:T(1,128)S(1)}, u32[]{:S(2)}, u32[]{:S(2)}) collective-permute-start(s32[1,256]{1,0:T(1,128)S(1)} %get-tuple-element.15), channel_id=1, source_target_pairs={{0,1},{1,0},{2,3},{3,2},{4,5},{5,4},{6,7},{7,6},{8,9},{9,8},{10,11... | collective-permute-start | bytes 3080 | tf_op jit(solution)/shard_map/ppermute | solution.py:165
  34.3 0.1 pad_maximum_fusion.reals
  34.3 5.7 %collective-permute-done.3 = s32[1,256]{1,0:T(1,128)S(1)} collective-permute-done((s32[1,256]{1,0:T(1,128)S(1)}, s32[1,256]{1,0:T(1,128)S(1)}, u32[]{:S(2)}, u32[]{:S(2)}) %collective-permute-start.3) | collective-permute-done | bytes 1056 | tf_op jit(solution)/shard_map/ppermute | solution.py:165
  40.1 9.8 %collective-permute-start.6 = (s32[2,256]{1,0:T(2,128)S(1)}, s32[2,256]{1,0:T(2,128)S(1)}, u32[]{:S(2)}, u32[]{:S(2)}) collective-permute-start(s32[2,256]{1,0:T(2,128)S(1)} %pad_add_fusion.near), channel_id=1, source_target_pairs={{4,0},{8,4},{12,8},{16,12},{20,16},{24,20},{28,24},{32,28},{36,32}... | collective-permute-start | bytes 6152 | tf_op jit(solution)/shard_map/ppermute | solution.py:18
  49.9 0.0 collective-permute-done.image_1
  49.9 3.2 %collective-permute-start.9 = (bf16[256,1152]{1,0:T(8,128)(2,1)S(1)}, bf16[256,1152]{1,0:T(8,128)(2,1)S(1)}, u32[]{:S(2)}, u32[]{:S(2)}) collective-permute-start(bf16[256,1152]{1,0:T(8,128)(2,1)S(1)} %collective-permute-done.image_1), channel_id=1, source_target_pairs={{4,0},{8,4},{12,8},{16,12},{20,16},{24,20},{28,24},{32,28},{36,32}... | collective-permute-start | bytes 1769480 | tf_op jit(solution)/shard_map/ppermute | solution.py:18
  53.1 0.1 pad_add_fusion.1.firsts
  53.2 4.3 %collective-permute-done.6 = s32[2,256]{1,0:T(2,128)S(1)} collective-permute-done((s32[2,256]{1,0:T(2,128)S(1)}, s32[2,256]{1,0:T(2,128)S(1)}, u32[]{:S(2)}, u32[]{:S(2)}) %collective-permute-start.6) | collective-permute-done | bytes 2080 | tf_op jit(solution)/shard_map/ppermute | solution.py:18
  57.5 0.0 collective-permute-done.1.text_1
  57.5 8.5 %collective-permute-start.2 = (bf16[256,1152]{1,0:T(8,128)(2,1)S(1)}, bf16[256,1152]{1,0:T(8,128)(2,1)S(1)}, u32[]{:S(2)}, u32[]{:S(2)}) collective-permute-start(bf16[256,1152]{1,0:T(8,128)(2,1)S(1)} %collective-permute-done.1.text_1), channel_id=1, source_target_pairs={{764,0},{0,4},{4,8},{8,12},{12,16},{16,20},{20,24},{24,28},{28,32}... | collective-permute-start | bytes 1769480 | tf_op jit(solution)/shard_map/ppermute | solution.py:18
  66.0 0.0 collective-permute-done.4.prior
  66.0 0.0 collective-permute-done.5.after
  66.0 0.0 copy-done.1
  66.0 0.0 copy-done.3
  66.0 7.0 %first.1 = (f32[512,1152]{1,0:T(8,128)S(1)}, f32[512,1152]{1,0:T(8,128)S(1)}, f32[2,256]{1,0:T(2,128)S(1)}) custom-call(s32[4]{0:T(128)S(1)} %pad_add_fusion.1.firsts, f32[2]{0:T(128)S(1)} %pad_maximum_fusion.reals, bf16[256,1152]{1,0:T(8,128)(2,1)S(1)} %copy-done.3, bf16[256,1152]{1,0:T(8,128)(2,1)S(1)} %collective-permute-done.image_1, ...), custom_call_target="tpu_custom_call" | custom-call | flops 3019898880 | bytes 1048576 | tf_op jit(solution)/shard_map/first/pallas_call | solution.py:172
  73.1 0.0 collective-permute-done.9.after
  73.1 2.3 %text.1 = (f32[256,1152]{1,0:T(8,128)S(1)}, bf16[256,1152]{1,0:T(8,128)(2,1)S(1)}) custom-call(s32[4]{0:T(128)S(1)} %pad_add_fusion.1.firsts, f32[2]{0:T(128)S(1)} %pad_maximum_fusion.reals, bf16[256,1152]{1,0:T(8,128)(2,1)S(1)} %copy-done.1, bf16[256,1152]{1,0:T(8,128)(2,1)S(1)} %collective-permute-done.1.text_1, ...), custom_call_target="tpu_custom_call" | custom-call | flops 603979776 | bytes 1048576 | tf_op jit(solution)/shard_map/text/pallas_call | solution.py:178
  75.4 11.9 %collective-permute-start.10 = (bf16[256,1152]{1,0:T(8,128)(2,1)S(1)}, bf16[256,1152]{1,0:T(8,128)(2,1)S(1)}, u32[]{:S(2)}, u32[]{:S(2)}) collective-permute-start(bf16[256,1152]{1,0:T(8,128)(2,1)S(1)} %get-tuple-element.26), channel_id=1, source_target_pairs={{1,2},{2,1},{3,0},{0,3},{5,6},{6,5},{7,4},{4,7},{9,10},{10,9},{11,... | collective-permute-start | bytes 1769480 | tf_op jit(solution)/shard_map/ppermute | solution.py:183
  87.3 0.0 collective-permute-done.2.prior
  87.3 2.7 %image.1 = (f32[256,1152]{1,0:T(8,128)S(1)}, bf16[256,1152]{1,0:T(8,128)(2,1)S(1)}, f32[1,256]{1,0:T(1,128)S(1)}, f32[1,256]{1,0:T(1,128)S(1)}) custom-call(s32[4]{0:T(128)S(1)} %pad_add_fusion.1.firsts, f32[2]{0:T(128)S(1)} %pad_maximum_fusion.reals, bf16[256,1152]{1,0:T(8,128)(2,1)S(1)} %copy-done.3, bf16[256,1152]{1,0:T(8,128)(2,1)S(1)} %collective-permute-done.image_1, ...), custom_call_target="tpu_custom_call" | custom-call | flops 603979776 | bytes 1048576 | tf_op jit(solution)/shard_map/image/pallas_call | solution.py:175
  90.0 1.9 %collective-permute-start.8 = (bf16[256,1152]{1,0:T(8,128)(2,1)S(1)}, bf16[256,1152]{1,0:T(8,128)(2,1)S(1)}, u32[]{:S(2)}, u32[]{:S(2)}) collective-permute-start(bf16[256,1152]{1,0:T(8,128)(2,1)S(1)} %get-tuple-element.23), channel_id=1, source_target_pairs={{0,1},{1,0},{2,3},{3,2},{4,5},{5,4},{6,7},{7,6},{8,9},{9,8},{10,11... | collective-permute-start | bytes 1769480 | tf_op jit(solution)/shard_map/ppermute | solution.py:182
  91.9 5.7 %collective-permute-start.7 = (f32[1,256]{1,0:T(1,128)S(1)}, f32[1,256]{1,0:T(1,128)S(1)}, u32[]{:S(2)}, u32[]{:S(2)}) collective-permute-start(f32[1,256]{1,0:T(1,128)S(1)} %get-tuple-element.21), channel_id=1, source_target_pairs={{0,1},{1,0},{2,3},{3,2},{4,5},{5,4},{6,7},{7,6},{8,9},{9,8},{10,11... | collective-permute-start | bytes 3080 | tf_op jit(solution)/shard_map/ppermute | solution.py:184
  97.6 34.2 %collective-permute-done.7 = f32[1,256]{1,0:T(1,128)S(1)} collective-permute-done((f32[1,256]{1,0:T(1,128)S(1)}, f32[1,256]{1,0:T(1,128)S(1)}, u32[]{:S(2)}, u32[]{:S(2)}) %collective-permute-start.7) | collective-permute-done | bytes 1056 | tf_op jit(solution)/shard_map/ppermute | solution.py:184
  131.8 0.6 add.37
  132.4 0.0 collective-permute-done.10
  132.4 1.0 multiply_convert_fusion
  133.4 0.0 collective-permute-done.8
  133.4 1.0 multiply_convert_fusion.1
  (2 shorter events, 0.0 us)
Async XLA Ops:
  0.6 49.2 %collective-permute-start = (bf16[256,1152]{1,0:T(8,128)(2,1)}, bf16[256,1152]{1,0:T(8,128)(2,1)S(1)}, u32[]{:S(2)}, u32[]{:S(2)}) collective-permute-start(bf16[256,1152]{1,0:T(8,128)(2,1)} %image_0.3), channel_id=1, source_target_pairs={{0,1},{1,0},{2,3},{3,2},{4,5},{5,4},{6,7},{7,6},{8,9},{9,8},{10,11... | collective-permute-start | bytes 1769480 | tf_op jit(solution)/shard_map/ppermute | solution.py:157
  8.5 49.0 %collective-permute-start.1 = (bf16[256,1152]{1,0:T(8,128)(2,1)}, bf16[256,1152]{1,0:T(8,128)(2,1)S(1)}, u32[]{:S(2)}, u32[]{:S(2)}) collective-permute-start(bf16[256,1152]{1,0:T(8,128)(2,1)} %text_0.3), channel_id=1, source_target_pairs={{1,2},{2,1},{3,0},{0,3},{5,6},{6,5},{7,4},{4,7},{9,10},{10,9},{11,... | collective-permute-start | bytes 1769480 | tf_op jit(solution)/shard_map/ppermute | solution.py:156
  18.3 1.1 copy-start
  19.3 1.1 copy-start.2
  20.4 0.7 copy-start.4
  21.1 45.0 %copy-start.1 = (bf16[256,1152]{1,0:T(8,128)(2,1)S(1)}, bf16[256,1152]{1,0:T(8,128)(2,1)}, u32[]{:S(2)}) copy-start(bf16[256,1152]{1,0:T(8,128)(2,1)} %text_0.3) | copy-start | bytes 1769476
  21.1 45.0 %copy-start.3 = (bf16[256,1152]{1,0:T(8,128)(2,1)S(1)}, bf16[256,1152]{1,0:T(8,128)(2,1)}, u32[]{:S(2)}) copy-start(bf16[256,1152]{1,0:T(8,128)(2,1)} %image_0.3) | copy-start | bytes 1769476
  22.2 43.8 %collective-permute-start.4 = (bf16[256,1152]{1,0:T(8,128)(2,1)}, bf16[256,1152]{1,0:T(8,128)(2,1)S(1)}, u32[]{:S(2)}, u32[]{:S(2)}) collective-permute-start(bf16[256,1152]{1,0:T(8,128)(2,1)} %get-tuple-element.16), channel_id=1, source_target_pairs={{764,0},{0,4},{4,8},{8,12},{12,16},{16,20},{20,24},{24,28},{28,32}... | collective-permute-start | bytes 1769480 | tf_op jit(solution)/shard_map/ppermute | solution.py:18
  24.1 41.9 %collective-permute-start.5 = (bf16[256,1152]{1,0:T(8,128)(2,1)}, bf16[256,1152]{1,0:T(8,128)(2,1)S(1)}, u32[]{:S(2)}, u32[]{:S(2)}) collective-permute-start(bf16[256,1152]{1,0:T(8,128)(2,1)} %get-tuple-element.17), channel_id=1, source_target_pairs={{4,0},{8,4},{12,8},{16,12},{20,16},{24,20},{28,24},{32,28},{36,32}... | collective-permute-start | bytes 1769480 | tf_op jit(solution)/shard_map/ppermute | solution.py:18
  27.7 12.3 %collective-permute-start.3 = (s32[1,256]{1,0:T(1,128)S(1)}, s32[1,256]{1,0:T(1,128)S(1)}, u32[]{:S(2)}, u32[]{:S(2)}) collective-permute-start(s32[1,256]{1,0:T(1,128)S(1)} %get-tuple-element.15), channel_id=1, source_target_pairs={{0,1},{1,0},{2,3},{3,2},{4,5},{5,4},{6,7},{7,6},{8,9},{9,8},{10,11... | collective-permute-start | bytes 3080 | tf_op jit(solution)/shard_map/ppermute | solution.py:165
  40.1 17.4 %collective-permute-start.6 = (s32[2,256]{1,0:T(2,128)S(1)}, s32[2,256]{1,0:T(2,128)S(1)}, u32[]{:S(2)}, u32[]{:S(2)}) collective-permute-start(s32[2,256]{1,0:T(2,128)S(1)} %pad_add_fusion.near), channel_id=1, source_target_pairs={{4,0},{8,4},{12,8},{16,12},{20,16},{24,20},{28,24},{32,28},{36,32}... | collective-permute-start | bytes 6152 | tf_op jit(solution)/shard_map/ppermute | solution.py:18
  49.9 23.2 %collective-permute-start.9 = (bf16[256,1152]{1,0:T(8,128)(2,1)S(1)}, bf16[256,1152]{1,0:T(8,128)(2,1)S(1)}, u32[]{:S(2)}, u32[]{:S(2)}) collective-permute-start(bf16[256,1152]{1,0:T(8,128)(2,1)S(1)} %collective-permute-done.image_1), channel_id=1, source_target_pairs={{4,0},{8,4},{12,8},{16,12},{20,16},{24,20},{28,24},{32,28},{36,32}... | collective-permute-start | bytes 1769480 | tf_op jit(solution)/shard_map/ppermute | solution.py:18
  57.5 29.8 %collective-permute-start.2 = (bf16[256,1152]{1,0:T(8,128)(2,1)S(1)}, bf16[256,1152]{1,0:T(8,128)(2,1)S(1)}, u32[]{:S(2)}, u32[]{:S(2)}) collective-permute-start(bf16[256,1152]{1,0:T(8,128)(2,1)S(1)} %collective-permute-done.1.text_1), channel_id=1, source_target_pairs={{764,0},{0,4},{4,8},{8,12},{12,16},{16,20},{20,24},{24,28},{28,32}... | collective-permute-start | bytes 1769480 | tf_op jit(solution)/shard_map/ppermute | solution.py:18
  75.4 57.1 %collective-permute-start.10 = (bf16[256,1152]{1,0:T(8,128)(2,1)S(1)}, bf16[256,1152]{1,0:T(8,128)(2,1)S(1)}, u32[]{:S(2)}, u32[]{:S(2)}) collective-permute-start(bf16[256,1152]{1,0:T(8,128)(2,1)S(1)} %get-tuple-element.26), channel_id=1, source_target_pairs={{1,2},{2,1},{3,0},{0,3},{5,6},{6,5},{7,4},{4,7},{9,10},{10,9},{11,... | collective-permute-start | bytes 1769480 | tf_op jit(solution)/shard_map/ppermute | solution.py:183
  90.0 43.4 %collective-permute-start.8 = (bf16[256,1152]{1,0:T(8,128)(2,1)S(1)}, bf16[256,1152]{1,0:T(8,128)(2,1)S(1)}, u32[]{:S(2)}, u32[]{:S(2)}) collective-permute-start(bf16[256,1152]{1,0:T(8,128)(2,1)S(1)} %get-tuple-element.23), channel_id=1, source_target_pairs={{0,1},{1,0},{2,3},{3,2},{4,5},{5,4},{6,7},{7,6},{8,9},{9,8},{10,11... | collective-permute-start | bytes 1769480 | tf_op jit(solution)/shard_map/ppermute | solution.py:182
  91.9 39.9 %collective-permute-start.7 = (f32[1,256]{1,0:T(1,128)S(1)}, f32[1,256]{1,0:T(1,128)S(1)}, u32[]{:S(2)}, u32[]{:S(2)}) collective-permute-start(f32[1,256]{1,0:T(1,128)S(1)} %get-tuple-element.21), channel_id=1, source_target_pairs={{0,1},{1,0},{2,3},{3,2},{4,5},{5,4},{6,7},{7,6},{8,9},{9,8},{10,11... | collective-permute-start | bytes 3080 | tf_op jit(solution)/shard_map/ppermute | solution.py:184

commit v3 on v2

v3 whole, which is shorter than its diff:
```python
import jax
import jax.numpy as jnp
from jax import lax
from jax.experimental import pallas as pl
from jax.experimental.pallas import tpu as pltpu
from jax.sharding import PartitionSpec as P

IMAGE_PAIRS = [(0, 1), (1, 0), (2, 3), (3, 2)]
TEXT_PAIRS = [(1, 2), (2, 1), (3, 0), (0, 3)]
PLANES = 3

SHIFTS = (0, 8, 16)
TAIL = 16

VMEM = pl.BlockSpec(memory_space=pltpu.VMEM)
SMEM = pl.BlockSpec(memory_space=pltpu.SMEM)
LIMIT = 40 * 1024 * 1024


def outer_pairs(distance, edge):
    count = lax.axis_size("outer")
    plane = count // PLANES
    pairs = [((i - distance) % count, i) for i in range(count)]
    return [(i, j) for i, j in pairs if (i // plane != j // plane) == edge]


def from_behind(block, distance):
    pairs = outer_pairs(distance, False) + outer_pairs(distance, True)
    return lax.ppermute(block, "outer", pairs)


def within_from_behind(block, distance):
    return lax.ppermute(block, "outer", outer_pairs(distance, False))


def over_last(x, y):
    return lax.dot_general(x, y, (((1,), (1,)), ((), ())), preferred_element_type=jnp.float32)


def over_first(x, y):
    return lax.dot_general(x, y, (((0,), (0,)), ((), ())), preferred_element_type=jnp.float32)


def hold_kernel(flags, images, texts, positive, images_out, texts_out, positive_out, edge_out):
    rows = images.shape[0]
    images_out[pl.ds(0, rows), :] = images[...]
    images_out[pl.ds(rows, TAIL), :] = jnp.zeros((TAIL, images.shape[1]), jnp.bfloat16)
    digits = [(positive[...] >> shift) & 255 for shift in SHIFTS]
    digits = jnp.concatenate(digits + [jnp.zeros((TAIL - len(SHIFTS), rows), jnp.int32)])
    images_out[pl.ds(rows, TAIL), pl.ds(0, rows)] = digits.astype(jnp.float32).astype(jnp.bfloat16)
    texts_out[...] = texts[...]
    positive_out[...] = positive[...]


    @pl.when(flags[1] == 1)
    def _():
        edge_out[pl.ds(0, rows), :] = texts[...]

    @pl.when(flags[1] == 0)
    def _():
        edge_out[...] = images_out[...]


def gate_kernel(*refs):
    pass


def gate(array, *tokens):
    anywhere = pl.BlockSpec(memory_space=pl.ANY)
    return pl.pallas_call(
        gate_kernel,
        name="gate",
        out_shape=jax.ShapeDtypeStruct(array.shape, array.dtype),
        in_specs=[anywhere] * (1 + len(tokens)),
        out_specs=anywhere,
        input_output_aliases={0: 0},
    )(array, *tokens)


class Blocks:
    def __init__(self, firsts, reals):
        self.firsts, self.scale, self.bias = firsts, reals[0], reals[1]

    def logits(self, text, image, positive, first):
        logits = self.scale * over_last(text, image) + self.bias
        row = lax.broadcasted_iota(jnp.int32, logits.shape, 0)
        return logits, row == positive - self.firsts[first]

    def __call__(self, text, image, positive, first):
        logits, hits = self.logits(text, image, positive, first)
        decay = jnp.exp(-jnp.abs(logits))
        share = 1.0 / (1.0 + decay)
        sigmoid = jnp.where(logits >= 0.0, share, decay * share)
        weights = (sigmoid - hits.astype(jnp.float32)).astype(jnp.bfloat16)

        def loss():
            signed = jnp.where(hits, -logits, logits)
            return jnp.sum(jnp.maximum(signed, 0.0) + jnp.log1p(decay), axis=0, keepdims=True)

        return weights, loss


def read_after(after):
    rows = after.shape[0] - TAIL
    digits = after[pl.ds(rows, TAIL), pl.ds(0, rows)].astype(jnp.float32).astype(jnp.int32)
    far = sum(digits[k : k + 1, :] << shift for k, shift in enumerate(SHIFTS))
    return after[pl.ds(0, rows), :], far


def by_image(weights, image):
    return jnp.dot(weights, image, preferred_element_type=jnp.float32)


def early_kernel(firsts, reals, images, texts, near, image_part, text_part, loss):
    block = Blocks(firsts, reals)
    weights, losses = block(texts[...], images[...], near[...], 0)
    loss[...] = losses()
    image_part[...] = over_first(weights, texts[...])
    text_part[...] = by_image(weights, images[...])


def first_kernel(
    firsts,
    reals,
    flags,
    image_0,
    image_1,
    text_0,
    text_1,
    prior,
    after,
    near,
    near_1,
    image_early,
    text_early,
    loss_early,
    image_part,
    text_part,
    loss,
):
    block = Blocks(firsts, reals)
    rows = image_0.shape[0]
    own, other = pl.ds(0, rows), pl.ds(rows, rows)

    weights, losses = block(text_1[...], image_0[...], near[...], 1)
    loss[pl.ds(0, 1), :] = loss_early[...] + losses()
    image_part[own, :] = image_early[...] + over_first(weights, text_1[...])
    text_part[other, :] = by_image(weights, image_0[...])

    weights, losses = block(text_0[...], image_1[...], near_1[...], 0)
    total = losses()
    image_part[other, :] = over_first(weights, text_0[...])
    text_part[own, :] = text_early[...] + by_image(weights, image_1[...])

    weights, losses = block(text_1[...], image_1[...], near_1[...], 1)
    loss[pl.ds(1, 1), :] = total + losses()
    image_part[other, :] += over_first(weights, text_1[...])
    text_part[other, :] += by_image(weights, image_1[...])

    @pl.when(flags[0] == 0)
    def _():
        for j, image, positive in ((0, image_0, near), (1, image_1, near_1)):
            weights, losses = block(prior[...], image[...], positive[...], 2)
            loss[pl.ds(j, 1), :] += losses()
            image_part[pl.ds(j * rows, rows), :] += over_first(weights, prior[...])

    @pl.when(flags[1] == 0)
    def _():
        image, far = read_after(after)
        for k, text in ((0, text_0), (1, text_1)):
            weights, _ = block(text[...], image, far, k)
            text_part[pl.ds(k * rows, rows), :] += by_image(weights, image)


def image_kernel(
    firsts,
    reals,
    flags,
    image_0,
    image_1,
    prior,
    edge,
    near,
    near_1,
    image_part,
    loss,
    image_own,
    image_send,
    loss_own,
    loss_send,
):
    block = Blocks(firsts, reals)
    rows = image_0.shape[0]
    for j, image, positive in ((1, image_1, near_1), (0, image_0, near)):
        part = pl.ds(j * rows, rows)
        weights, losses = block(prior[...], image[...], positive[...], 3)
        losses = loss[pl.ds(j, 1), :] + losses()
        total = image_part[part, :] + over_first(weights, prior[...])
        loss_out, image_out = (loss_send, image_send) if j == 1 else (loss_own, image_own)
        loss_out[...] = losses
        image_out[...] = total.astype(image_out.dtype)

        @pl.when(flags[0] == 1)
        def _():
            edge_text = edge[pl.ds(0, rows), :]
            weights, losses = block(prior[...], image[...], positive[...], 3)
            more, more_losses = block(edge_text, image[...], positive[...], 2)
            total = image_part[part, :] + over_first(weights, prior[...])
            total += over_first(more, edge_text)
            loss_out[...] = loss[pl.ds(j, 1), :] + losses() + more_losses()
            image_out[...] = total.astype(image_out.dtype)


def text_kernel(
    firsts, reals, flags, text_0, text_1, after, edge, far_1, text_part, text_own, text_send
):
    block = Blocks(firsts, reals)
    rows = text_0.shape[0]
    for k, text, text_out in ((1, text_1, text_send), (0, text_0, text_own)):
        part = pl.ds(k * rows, rows)
        weights, _ = block(text[...], after[...], far_1[...], k)
        total = text_part[part, :] + by_image(weights, after[...])
        text_out[...] = total.astype(text_out.dtype)

        @pl.when(flags[1] == 1)
        def _():
            weights, _ = block(text[...], after[...], far_1[...], k)
            edge_image, far = read_after(edge)
            more, _ = block(text[...], edge_image, far, k)
            total = text_part[part, :] + by_image(weights, after[...])
            text_out[...] = (total + by_image(more, edge_image)).astype(text_out.dtype)


def call(kernel, name, in_specs, outs, blocks):
    return pl.pallas_call(
        kernel,
        name=name,
        out_shape=outs,
        in_specs=in_specs,
        out_specs=[VMEM] * len(outs),
        compiler_params=pltpu.CompilerParams(vmem_limit_bytes=LIMIT),
        cost_estimate=pl.CostEstimate(
            flops=2 * blocks * 256 * 256 * 1152, bytes_accessed=1 << 20, transcendentals=0
        ),
    )


def per_device(images, texts, positive, logit_scale, logit_bias):
    rows, width = texts.shape
    count = lax.axis_size("outer")
    group = lax.axis_index("outer")
    me = lax.axis_index("inner")
    whole = lax.axis_size("inner") * rows
    before = (group - 1 + count) % count
    firsts = jnp.stack(
        [
            group * whole + me * rows,
            group * whole + (3 - me) * rows,
            before * whole + me * rows,
            before * whole + (3 - me) * rows,
        ]
    ).astype(jnp.int32)
    reals = jnp.concatenate([logit_scale, logit_bias])
    shard = jax.ShapeDtypeStruct((rows, width), jnp.bfloat16)
    long_shard = jax.ShapeDtypeStruct((rows + TAIL, width), jnp.bfloat16)
    real_shard = jax.ShapeDtypeStruct((rows, width), jnp.float32)
    real_pair = jax.ShapeDtypeStruct((2 * rows, width), jnp.float32)
    line = jax.ShapeDtypeStruct((1, rows), jnp.float32)
    lines = jax.ShapeDtypeStruct((2, rows), jnp.float32)

    plane = count // PLANES
    flags = jnp.stack([group % plane == 0, group % plane == plane - 1]).astype(jnp.int32)

    text_1 = lax.ppermute(texts, "inner", TEXT_PAIRS)
    image_1 = lax.ppermute(images, "inner", IMAGE_PAIRS)
    images_later, texts_later, near, edge_out = call(
        hold_kernel,
        "hold",
        [SMEM] + [VMEM] * 3,
        [long_shard, shard, jax.ShapeDtypeStruct((1, rows), jnp.int32), long_shard],
        1,
    )(flags, images, texts, positive[None, :])
    prior_0 = within_from_behind(texts_later, 1)
    after_0 = within_from_behind(images_later, -1)
    image_early, text_early, loss_early = call(
        early_kernel, "early", [SMEM] * 2 + [VMEM] * 3, [real_shard, real_shard, line], 3
    )(firsts, reals, images, texts, near)
    near_1 = lax.ppermute(positive[None, :], "inner", IMAGE_PAIRS)
    image_1 = gate(image_1, near_1, loss_early)
    after_1 = from_behind(image_1, -1)
    text_1 = gate(text_1, near_1, loss_early)
    prior_1 = from_behind(text_1, 1)
    far_1 = from_behind(near_1, -1)
    edge = lax.ppermute(gate(edge_out, text_1, image_1), "outer", outer_pairs(1, True) + outer_pairs(-1, True))

    image_part, text_part, loss = call(
        first_kernel, "first", [SMEM] * 3 + [VMEM] * 11, [real_pair, real_pair, lines], 17
    )(
        firsts,
        reals,
        flags,
        images,
        image_1,
        texts,
        text_1,
        prior_0,
        after_0,
        near,
        near_1,
        image_early,
        text_early,
        loss_early,
    )
    text_own, text_send = call(
        text_kernel, "text", [SMEM] * 3 + [VMEM] * 6, [real_shard, shard], 4
    )(firsts, reals, flags, texts, text_1, after_1, edge, far_1, text_part)
    image_own, image_send, loss_own, loss_send = call(
        image_kernel, "image", [SMEM] * 3 + [VMEM] * 8, [real_shard, shard, line, line], 4
    )(firsts, reals, flags, images, image_1, prior_1, edge, near, near_1, image_part, loss)

    image_back = lax.ppermute(image_send, "inner", IMAGE_PAIRS)
    text_back = lax.ppermute(text_send, "inner", TEXT_PAIRS)
    loss_back = lax.ppermute(loss_send, "inner", IMAGE_PAIRS)
    scale = logit_scale[0]
    loss_rows = (loss_own + loss_back)[0]
    image_grad = (scale * (image_own + image_back.astype(jnp.float32))).astype(jnp.bfloat16)
    text_grad = (scale * (text_own + text_back.astype(jnp.float32))).astype(jnp.bfloat16)
    return (loss_rows, image_grad, text_grad)


def solution(mesh):
    return jax.shard_map(
        per_device,
        mesh=mesh,
        in_specs=(
            P(("outer", "inner"), None),
            P(("outer", "inner"), None),
            P(("outer", "inner")),
            P(),
            P(),
        ),
        out_specs=(P(("outer", "inner")), P(("outer", "inner"), None), P(("outer", "inner"), None)),
        check_vma=False,
    )
```

time: 135 us -> 143 us (1.059)
  the two profiles are of different devices: /device:TPU:62 before, /device:TPU:129 now
where the time goes in v3:
time: 143 us; the launch traced here: 142 us
  starting transfers between devices  56.8 us (40%)
  waiting for transfers between devices  51.8 us (36%)
  Pallas kernels  17.7 us (12%)
  local copies, waits for them, and re-layouts  10.7 us (7%)
  other arithmetic  2.73 us (2%)
  between operations  2.18 us (2%)
    ppermute x1, waiting for transfers between devices, per_device(): loss_back = lax.ppermute(loss_send, 'inner', IMAGE_PAIRS)  36.7 us
    ppermute x3, starting transfers between devices, from_behind(): return lax.ppermute(block, 'outer', pairs)  16 us
    ppermute x1, waiting for transfers between devices, per_device(): near_1 = lax.ppermute(positive[None, :], 'inner', IMAGE_PAIRS)  15.1 us
    ppermute x1, starting transfers between devices, per_device(): text_1 = lax.ppermute(texts, 'inner', TEXT_PAIRS)  12.5 us
    unnamed x36, local copies, waits for them, and re-layouts  10.7 us
    pallas_call x1, Pallas kernels, per_device(): call(first_kernel, 'first', [SMEM] * 3 + [VMEM] * 11, [real_pair, real_pa...  8.48 us
    ppermute x2, starting transfers between devices, within_from_behind(): return lax.ppermute(block, 'outer', outer_pairs(distance, False))  6.51 us
    ppermute x1, starting transfers between devices, per_device(): near_1 = lax.ppermute(positive[None, :], 'inner', IMAGE_PAIRS)  5.53 us
  transfers between devices with their start and end apart: 12, of which 2 were waited for; matrix products, arithmetic and copies ran while one was open for 1% of the time, Pallas kernels for 12%

profile of v3, /device:TPU:129, one launch (start us, length us, event | category | flops | bytes accessed | tf_op | source)
XLA Modules:
  0.0 141.9 jit_solution(9977975923241410566)
XLA Ops:
  0.6 12.5 %collective-permute-start.2 = (bf16[256,1152]{1,0:T(8,128)(2,1)}, bf16[256,1152]{1,0:T(8,128)(2,1)S(1)}, u32[]{:S(2)}, u32[]{:S(2)}) collective-permute-start(bf16[256,1152]{1,0:T(8,128)(2,1)} %text_0.3), channel_id=1, source_target_pairs={{1,2},{2,1},{3,0},{0,3},{5,6},{6,5},{7,4},{4,7},{9,10},{10,9},{11,... | collective-permute-start | bytes 1769480 | tf_op jit(solution)/shard_map/ppermute | solution.py:274
  13.1 2.8 %collective-permute-start = (bf16[256,1152]{1,0:T(8,128)(2,1)}, bf16[256,1152]{1,0:T(8,128)(2,1)S(1)}, u32[]{:S(2)}, u32[]{:S(2)}) collective-permute-start(bf16[256,1152]{1,0:T(8,128)(2,1)} %image_0.3), channel_id=1, source_target_pairs={{0,1},{1,0},{2,3},{3,2},{4,5},{5,4},{6,7},{7,6},{8,9},{9,8},{10,11... | collective-permute-start | bytes 1769480 | tf_op jit(solution)/shard_map/ppermute | solution.py:275
  15.9 5.5 %collective-permute-start.1 = (s32[1,256]{1,0:T(1,128)}, s32[1,256]{1,0:T(1,128)S(1)}, u32[]{:S(2)}, u32[]{:S(2)}) collective-permute-start(s32[1,256]{1,0:T(1,128)} %bitcast.11), channel_id=1, source_target_pairs={{0,1},{1,0},{2,3},{3,2},{4,5},{5,4},{6,7},{7,6},{8,9},{9,8},{10,11... | collective-permute-start | bytes 3080 | tf_op jit(solution)/shard_map/ppermute | solution.py:288
  21.5 0.1 add_convert_fusion.flags
  21.5 0.0 copy-start.4
  21.5 1.1 copy-done.4
  22.6 0.0 copy-start.6
  22.6 1.1 copy-done.6
  23.7 0.0 copy-start.13
  23.7 0.7 copy-done.13
  24.3 0.0 copy-start.5
  24.3 0.0 copy-start.7
  24.3 1.7 %hold.1 = (bf16[272,1152]{1,0:T(8,128)(2,1)}, bf16[256,1152]{1,0:T(8,128)(2,1)}, s32[1,256]{1,0:T(1,128)S(1)}, bf16[272,1152]{1,0:T(8,128)(2,1)S(1)}) custom-call(s32[2]{0:T(128)S(1)} %add_convert_fusion.flags, bf16[256,1152]{1,0:T(8,128)(2,1)S(1)} %copy-done.6, bf16[256,1152]{1,0:T(8,128)(2,1)S(1)} %copy-done.4, s32[1,256]{1,0:T(1,128)S(1)} %bitcast.12), custom_call_target="tpu_custom_call" | custom-call | flops 150994944 | bytes 1048576 | tf_op jit(solution)/shard_map/hold/pallas_call | solution.py:276
  26.0 0.0 copy-start.8
  26.0 0.8 copy-done.8
  26.9 3.4 %collective-permute-start.6 = (bf16[272,1152]{1,0:T(8,128)(2,1)}, bf16[272,1152]{1,0:T(8,128)(2,1)S(1)}, u32[]{:S(2)}, u32[]{:S(2)}) collective-permute-start(bf16[272,1152]{1,0:T(8,128)(2,1)} %get-tuple-element.23), channel_id=1, source_target_pairs={{4,0},{8,4},{12,8},{16,12},{20,16},{24,20},{28,24},{32,28},{36,32}... | collective-permute-start | bytes 1880072 | tf_op jit(solution)/shard_map/ppermute | solution.py:33
  30.3 3.1 %collective-permute-start.5 = (bf16[256,1152]{1,0:T(8,128)(2,1)}, bf16[256,1152]{1,0:T(8,128)(2,1)}, u32[]{:S(2)}, u32[]{:S(2)}) collective-permute-start(bf16[256,1152]{1,0:T(8,128)(2,1)} %get-tuple-element.22), channel_id=1, source_target_pairs={{0,4},{4,8},{8,12},{12,16},{16,20},{20,24},{24,28},{28,32},{32,36}... | collective-permute-start | bytes 1769480 | tf_op jit(solution)/shard_map/ppermute | solution.py:33
  34.7 0.1 pad_maximum_fusion.reals
  34.8 0.1 pad_add_fusion.firsts
  34.9 0.0 copy-done.5
  34.9 0.0 copy-done.7
  34.9 1.9 %early.1 = (f32[256,1152]{1,0:T(8,128)S(1)}, f32[256,1152]{1,0:T(8,128)S(1)}, f32[1,256]{1,0:T(1,128)S(1)}) custom-call(s32[4]{0:T(128)S(1)} %pad_add_fusion.firsts, f32[2]{0:T(128)S(1)} %pad_maximum_fusion.reals, bf16[256,1152]{1,0:T(8,128)(2,1)S(1)} %copy-done.7, bf16[256,1152]{1,0:T(8,128)(2,1)S(1)} %copy-done.5, s32[1,256]{1,0:T(1,128)S(1)} %get-tuple-element.19.near), custom_call_target="tpu_custom_call" | custom-call | flops 452984832 | bytes 1048576 | tf_op jit(solution)/shard_map/early/pallas_call | solution.py:285
  36.8 0.0 copy-start.11
  36.8 0.6 copy-done.11
  37.4 0.0 copy-start.14
  37.4 1.0 copy-done.14
  38.4 0.0 copy-start.16
  38.4 1.0 copy-done.16
  39.5 15.1 %collective-permute-done.1.refs_1_.near_1 = s32[1,256]{1,0:T(1,128)S(1)} collective-permute-done((s32[1,256]{1,0:T(1,128)}, s32[1,256]{1,0:T(1,128)S(1)}, u32[]{:S(2)}, u32[]{:S(2)}) %collective-permute-start.1) | collective-permute-done | bytes 1056 | tf_op jit(solution)/shard_map/ppermute | solution.py:288
  54.5 0.0 copy-start.9
  54.5 0.0 collective-permute-done.2.refs_0_
  54.5 0.6 copy-done.9
  55.1 0.3 copy-done.2
  55.3 0.0 collective-permute-done.refs_0_
  55.3 0.8 copy-done
  56.2 0.8 collective-permute-start.4
  57.0 0.2 copy-done.1
  57.2 10.5 %collective-permute-start.9 = (bf16[256,1152]{1,0:T(8,128)(2,1)S(1)}, bf16[256,1152]{1,0:T(8,128)(2,1)S(1)}, u32[]{:S(2)}, u32[]{:S(2)}) collective-permute-start(bf16[256,1152]{1,0:T(8,128)(2,1)S(1)} %copy-done.1), channel_id=1, source_target_pairs={{4,0},{8,4},{12,8},{16,12},{20,16},{24,20},{28,24},{32,28},{36,32}... | collective-permute-start | bytes 1769480 | tf_op jit(solution)/shard_map/ppermute | solution.py:29
  67.7 0.0 copy-done.10
  67.7 1.9 %collective-permute-start.10 = (s32[1,256]{1,0:T(1,128)S(1)}, s32[1,256]{1,0:T(1,128)S(1)}, u32[]{:S(2)}, u32[]{:S(2)}) collective-permute-start(s32[1,256]{1,0:T(1,128)S(1)} %copy-done.10), channel_id=1, source_target_pairs={{4,0},{8,4},{12,8},{16,12},{20,16},{24,20},{28,24},{32,28},{36,32}... | collective-permute-start | bytes 3080 | tf_op jit(solution)/shard_map/ppermute | solution.py:29
  69.7 0.0 collective-permute-done.5.prior
  69.7 0.0 copy-done.3
  69.7 3.6 %collective-permute-start.3 = (bf16[256,1152]{1,0:T(8,128)(2,1)S(1)}, bf16[256,1152]{1,0:T(8,128)(2,1)S(1)}, u32[]{:S(2)}, u32[]{:S(2)}) collective-permute-start(bf16[256,1152]{1,0:T(8,128)(2,1)S(1)} %copy-done.3), channel_id=1, source_target_pairs={{0,4},{4,8},{8,12},{12,16},{16,20},{20,24},{24,28},{28,32},{32,36}... | collective-permute-start | bytes 1769480 | tf_op jit(solution)/shard_map/ppermute | solution.py:29
  73.3 0.0 collective-permute-done.6.after
  73.3 0.0 copy-done.12
  73.3 0.0 copy-start.15
  73.4 1.3 copy-done.15
  74.6 1.3 copy-done.17
  75.9 8.5 %first.1 = (f32[512,1152]{1,0:T(8,128)S(1)}, f32[512,1152]{1,0:T(8,128)S(1)}, f32[2,256]{1,0:T(2,128)S(1)}) custom-call(s32[4]{0:T(128)S(1)} %pad_add_fusion.firsts, f32[2]{0:T(128)S(1)} %pad_maximum_fusion.reals, s32[2]{0:T(128)S(1)} %add_convert_fusion.flags, bf16[256,1152]{1,0:T(8,128)(2,1)S(1)} %copy-done.7, bf16[256,1152]{1,0:T(8,128)(2,1)S(1)} %copy-done.1, ...), custom_call_target="tpu_custom_call" | custom-call | flops 2566914048 | bytes 1048576 | tf_op jit(solution)/shard_map/first/pallas_call | solution.py:296
  84.4 0.0 collective-permute-done.10.far_1
  84.4 0.0 collective-permute-done.9.after
  84.4 0.0 collective-permute-done.4.edge
  84.4 2.5 %text.1 = (f32[256,1152]{1,0:T(8,128)S(1)}, bf16[256,1152]{1,0:T(8,128)(2,1)S(1)}) custom-call(s32[4]{0:T(128)S(1)} %pad_add_fusion.firsts, f32[2]{0:T(128)S(1)} %pad_maximum_fusion.reals, s32[2]{0:T(128)S(1)} %add_convert_fusion.flags, bf16[256,1152]{1,0:T(8,128)(2,1)S(1)} %copy-done.5, bf16[256,1152]{1,0:T(8,128)(2,1)S(1)} %copy-done.3, ...), custom_call_target="tpu_custom_call" | custom-call | flops 603979776 | bytes 1048576 | tf_op jit(solution)/shard_map/text/pallas_call | solution.py:314
  86.9 4.4 %collective-permute-start.11 = (bf16[256,1152]{1,0:T(8,128)(2,1)S(1)}, bf16[256,1152]{1,0:T(8,128)(2,1)S(1)}, u32[]{:S(2)}, u32[]{:S(2)}) collective-permute-start(bf16[256,1152]{1,0:T(8,128)(2,1)S(1)} %get-tuple-element.34), channel_id=1, source_target_pairs={{1,2},{2,1},{3,0},{0,3},{5,6},{6,5},{7,4},{4,7},{9,10},{10,9},{11,... | collective-permute-start | bytes 1769480 | tf_op jit(solution)/shard_map/ppermute | solution.py:322
  91.3 0.0 collective-permute-done.3.prior
  91.3 3.1 %image.1 = (f32[256,1152]{1,0:T(8,128)S(1)}, bf16[256,1152]{1,0:T(8,128)(2,1)S(1)}, f32[1,256]{1,0:T(1,128)S(1)}, f32[1,256]{1,0:T(1,128)S(1)}) custom-call(s32[4]{0:T(128)S(1)} %pad_add_fusion.firsts, f32[2]{0:T(128)S(1)} %pad_maximum_fusion.reals, s32[2]{0:T(128)S(1)} %add_convert_fusion.flags, bf16[256,1152]{1,0:T(8,128)(2,1)S(1)} %copy-done.7, ...), custom_call_target="tpu_custom_call" | custom-call | flops 603979776 | bytes 1048576 | tf_op jit(solution)/shard_map/image/pallas_call | solution.py:317
  94.4 3.7 %collective-permute-start.8 = (bf16[256,1152]{1,0:T(8,128)(2,1)S(1)}, bf16[256,1152]{1,0:T(8,128)(2,1)S(1)}, u32[]{:S(2)}, u32[]{:S(2)}) collective-permute-start(bf16[256,1152]{1,0:T(8,128)(2,1)S(1)} %get-tuple-element.31), channel_id=1, source_target_pairs={{0,1},{1,0},{2,3},{3,2},{4,5},{5,4},{6,7},{7,6},{8,9},{9,8},{10,11... | collective-permute-start | bytes 1769480 | tf_op jit(solution)/shard_map/ppermute | solution.py:321
  98.1 4.5 %collective-permute-start.7 = (f32[1,256]{1,0:T(1,128)S(1)}, f32[1,256]{1,0:T(1,128)S(1)}, u32[]{:S(2)}, u32[]{:S(2)}) collective-permute-start(f32[1,256]{1,0:T(1,128)S(1)} %get-tuple-element.29), channel_id=1, source_target_pairs={{0,1},{1,0},{2,3},{3,2},{4,5},{5,4},{6,7},{7,6},{8,9},{9,8},{10,11... | collective-permute-start | bytes 3080 | tf_op jit(solution)/shard_map/ppermute | solution.py:323
  102.7 36.7 %collective-permute-done.7 = f32[1,256]{1,0:T(1,128)S(1)} collective-permute-done((f32[1,256]{1,0:T(1,128)S(1)}, f32[1,256]{1,0:T(1,128)S(1)}, u32[]{:S(2)}, u32[]{:S(2)}) %collective-permute-start.7) | collective-permute-done | bytes 1056 | tf_op jit(solution)/shard_map/ppermute | solution.py:323
  139.4 0.6 add.42
  139.9 0.0 collective-permute-done.11
  139.9 1.0 multiply_convert_fusion
  140.9 0.0 collective-permute-done.8
  140.9 1.0 multiply_convert_fusion.1
  (10 shorter events, 0.0 us)
Async XLA Ops:
  0.6 53.9 %collective-permute-start.2 = (bf16[256,1152]{1,0:T(8,128)(2,1)}, bf16[256,1152]{1,0:T(8,128)(2,1)S(1)}, u32[]{:S(2)}, u32[]{:S(2)}) collective-permute-start(bf16[256,1152]{1,0:T(8,128)(2,1)} %text_0.3), channel_id=1, source_target_pairs={{1,2},{2,1},{3,0},{0,3},{5,6},{6,5},{7,4},{4,7},{9,10},{10,9},{11,... | collective-permute-start | bytes 1769480 | tf_op jit(solution)/shard_map/ppermute | solution.py:274
  13.1 42.2 %collective-permute-start = (bf16[256,1152]{1,0:T(8,128)(2,1)}, bf16[256,1152]{1,0:T(8,128)(2,1)S(1)}, u32[]{:S(2)}, u32[]{:S(2)}) collective-permute-start(bf16[256,1152]{1,0:T(8,128)(2,1)} %image_0.3), channel_id=1, source_target_pairs={{0,1},{1,0},{2,3},{3,2},{4,5},{5,4},{6,7},{7,6},{8,9},{9,8},{10,11... | collective-permute-start | bytes 1769480 | tf_op jit(solution)/shard_map/ppermute | solution.py:275
  15.9 38.6 %collective-permute-start.1 = (s32[1,256]{1,0:T(1,128)}, s32[1,256]{1,0:T(1,128)S(1)}, u32[]{:S(2)}, u32[]{:S(2)}) collective-permute-start(s32[1,256]{1,0:T(1,128)} %bitcast.11), channel_id=1, source_target_pairs={{0,1},{1,0},{2,3},{3,2},{4,5},{5,4},{6,7},{7,6},{8,9},{9,8},{10,11... | collective-permute-start | bytes 3080 | tf_op jit(solution)/shard_map/ppermute | solution.py:288
  21.5 1.1 copy-start.4
  22.6 1.1 copy-start.6
  23.7 0.7 copy-start.13
  24.3 10.5 %copy-start.5 = (bf16[256,1152]{1,0:T(8,128)(2,1)S(1)}, bf16[256,1152]{1,0:T(8,128)(2,1)}, u32[]{:S(2)}) copy-start(bf16[256,1152]{1,0:T(8,128)(2,1)} %text_0.3) | copy-start | bytes 1769476
  24.3 10.5 %copy-start.7 = (bf16[256,1152]{1,0:T(8,128)(2,1)S(1)}, bf16[256,1152]{1,0:T(8,128)(2,1)}, u32[]{:S(2)}) copy-start(bf16[256,1152]{1,0:T(8,128)(2,1)} %image_0.3) | copy-start | bytes 1769476
  26.0 0.8 copy-start.8
  26.9 46.4 %collective-permute-start.6 = (bf16[272,1152]{1,0:T(8,128)(2,1)}, bf16[272,1152]{1,0:T(8,128)(2,1)S(1)}, u32[]{:S(2)}, u32[]{:S(2)}) collective-permute-start(bf16[272,1152]{1,0:T(8,128)(2,1)} %get-tuple-element.23), channel_id=1, source_target_pairs={{4,0},{8,4},{12,8},{16,12},{20,16},{24,20},{28,24},{32,28},{36,32}... | collective-permute-start | bytes 1880072 | tf_op jit(solution)/shard_map/ppermute | solution.py:33
  30.3 39.4 %collective-permute-start.5 = (bf16[256,1152]{1,0:T(8,128)(2,1)}, bf16[256,1152]{1,0:T(8,128)(2,1)}, u32[]{:S(2)}, u32[]{:S(2)}) collective-permute-start(bf16[256,1152]{1,0:T(8,128)(2,1)} %get-tuple-element.22), channel_id=1, source_target_pairs={{0,4},{4,8},{8,12},{12,16},{16,20},{20,24},{24,28},{28,32},{32,36}... | collective-permute-start | bytes 1769480 | tf_op jit(solution)/shard_map/ppermute | solution.py:33
  36.8 0.6 copy-start.11
  37.4 1.0 copy-start.14
  38.4 1.0 copy-start.16
  54.5 0.6 copy-start.9
  54.5 0.8 copy-start.2
  55.3 0.8 copy-start
  56.2 1.1 copy-start.1
  56.2 11.6 %copy-start.10 = (s32[1,256]{1,0:T(1,128)S(1)}, s32[1,256]{1,0:T(1,128)}, u32[]{:S(2)}) copy-start(s32[1,256]{1,0:T(1,128)} %copy-done.9) | copy-start | bytes 3076
  56.2 13.5 %copy-start.3 = (bf16[256,1152]{1,0:T(8,128)(2,1)S(1)}, bf16[256,1152]{1,0:T(8,128)(2,1)}, u32[]{:S(2)}) copy-start(bf16[256,1152]{1,0:T(8,128)(2,1)} %gate.4.refs_1_.text_1) | copy-start | bytes 1769476
  56.2 17.2 %copy-start.12 = (f32[1,256]{1,0:T(1,128)S(1)}, f32[1,256]{1,0:T(1,128)}, u32[]{:S(2)}) copy-start(f32[1,256]{1,0:T(1,128)} %copy-done.11) | copy-start | bytes 3076
  56.2 28.2 %collective-permute-start.4 = (bf16[272,1152]{1,0:T(8,128)(2,1)}, bf16[272,1152]{1,0:T(8,128)(2,1)S(1)}, u32[]{:S(2)}, u32[]{:S(2)}) collective-permute-start(bf16[272,1152]{1,0:T(8,128)(2,1)} %gate.5), channel_id=1, source_target_pairs={{764,0},{252,256},{508,512},{256,252},{512,508},{0,764},{765,1},{2... | collective-permute-start | bytes 1880072 | tf_op jit(solution)/shard_map/ppermute | solution.py:294
  57.2 27.2 %collective-permute-start.9 = (bf16[256,1152]{1,0:T(8,128)(2,1)S(1)}, bf16[256,1152]{1,0:T(8,128)(2,1)S(1)}, u32[]{:S(2)}, u32[]{:S(2)}) collective-permute-start(bf16[256,1152]{1,0:T(8,128)(2,1)S(1)} %copy-done.1), channel_id=1, source_target_pairs={{4,0},{8,4},{12,8},{16,12},{20,16},{24,20},{28,24},{32,28},{36,32}... | collective-permute-start | bytes 1769480 | tf_op jit(solution)/shard_map/ppermute | solution.py:29
  67.7 16.7 %collective-permute-start.10 = (s32[1,256]{1,0:T(1,128)S(1)}, s32[1,256]{1,0:T(1,128)S(1)}, u32[]{:S(2)}, u32[]{:S(2)}) collective-permute-start(s32[1,256]{1,0:T(1,128)S(1)} %copy-done.10), channel_id=1, source_target_pairs={{4,0},{8,4},{12,8},{16,12},{20,16},{24,20},{28,24},{32,28},{36,32}... | collective-permute-start | bytes 3080 | tf_op jit(solution)/shard_map/ppermute | solution.py:29
  69.7 21.6 %collective-permute-start.3 = (bf16[256,1152]{1,0:T(8,128)(2,1)S(1)}, bf16[256,1152]{1,0:T(8,128)(2,1)S(1)}, u32[]{:S(2)}, u32[]{:S(2)}) collective-permute-start(bf16[256,1152]{1,0:T(8,128)(2,1)S(1)} %copy-done.3), channel_id=1, source_target_pairs={{0,4},{4,8},{8,12},{12,16},{16,20},{20,24},{24,28},{28,32},{32,36}... | collective-permute-start | bytes 1769480 | tf_op jit(solution)/shard_map/ppermute | solution.py:29
  73.3 1.3 copy-start.15
  74.6 1.3 copy-start.17
  86.9 53.0 %collective-permute-start.11 = (bf16[256,1152]{1,0:T(8,128)(2,1)S(1)}, bf16[256,1152]{1,0:T(8,128)(2,1)S(1)}, u32[]{:S(2)}, u32[]{:S(2)}) collective-permute-start(bf16[256,1152]{1,0:T(8,128)(2,1)S(1)} %get-tuple-element.34), channel_id=1, source_target_pairs={{1,2},{2,1},{3,0},{0,3},{5,6},{6,5},{7,4},{4,7},{9,10},{10,9},{11,... | collective-permute-start | bytes 1769480 | tf_op jit(solution)/shard_map/ppermute | solution.py:322
  94.4 46.5 %collective-permute-start.8 = (bf16[256,1152]{1,0:T(8,128)(2,1)S(1)}, bf16[256,1152]{1,0:T(8,128)(2,1)S(1)}, u32[]{:S(2)}, u32[]{:S(2)}) collective-permute-start(bf16[256,1152]{1,0:T(8,128)(2,1)S(1)} %get-tuple-element.31), channel_id=1, source_target_pairs={{0,1},{1,0},{2,3},{3,2},{4,5},{5,4},{6,7},{7,6},{8,9},{9,8},{10,11... | collective-permute-start | bytes 1769480 | tf_op jit(solution)/shard_map/ppermute | solution.py:321
  98.1 41.3 %collective-permute-start.7 = (f32[1,256]{1,0:T(1,128)S(1)}, f32[1,256]{1,0:T(1,128)S(1)}, u32[]{:S(2)}, u32[]{:S(2)}) collective-permute-start(f32[1,256]{1,0:T(1,128)S(1)} %get-tuple-element.29), channel_id=1, source_target_pairs={{0,1},{1,0},{2,3},{3,2},{4,5},{5,4},{6,7},{7,6},{8,9},{9,8},{10,11... | collective-permute-start | bytes 3080 | tf_op jit(solution)/shard_map/ppermute | solution.py:323

commit v4 on v3

v4 whole, which is shorter than its diff:
```python
import jax
import jax.numpy as jnp
from jax import lax
from jax.experimental import pallas as pl
from jax.experimental.pallas import tpu as pltpu
from jax.sharding import PartitionSpec as P

IMAGE_PAIRS = [(0, 1), (1, 0), (2, 3), (3, 2)]
TEXT_PAIRS = [(1, 2), (2, 1), (3, 0), (0, 3)]

SHIFTS = (0, 8, 16)
TAIL = 16

VMEM = pl.BlockSpec(memory_space=pltpu.VMEM)
SMEM = pl.BlockSpec(memory_space=pltpu.SMEM)
LIMIT = 40 * 1024 * 1024


def from_behind(block, distance):
    count = lax.axis_size("outer")
    return lax.ppermute(block, "outer", [((i - distance) % count, i) for i in range(count)])


def over_last(x, y):
    return lax.dot_general(x, y, (((1,), (1,)), ((), ())), preferred_element_type=jnp.float32)


def over_first(x, y):
    return lax.dot_general(x, y, (((0,), (0,)), ((), ())), preferred_element_type=jnp.float32)


def hold_kernel(images, texts, positive, images_out, texts_out):
    rows = images.shape[0]
    images_out[pl.ds(0, rows), :] = images[...]
    images_out[pl.ds(rows, TAIL), :] = jnp.zeros((TAIL, images.shape[1]), jnp.bfloat16)
    digits = [(positive[...] >> shift) & 255 for shift in SHIFTS]
    digits = jnp.concatenate(digits + [jnp.zeros((TAIL - len(SHIFTS), rows), jnp.int32)])
    images_out[pl.ds(rows, TAIL), pl.ds(0, rows)] = digits.astype(jnp.float32).astype(jnp.bfloat16)
    texts_out[...] = texts[...]


class Blocks:
    def __init__(self, firsts, reals):
        self.firsts, self.scale, self.bias = firsts, reals[0], reals[1]

    def logits(self, text, image, positive, first):
        logits = self.scale * over_last(text, image) + self.bias
        row = lax.broadcasted_iota(jnp.int32, logits.shape, 0)
        return logits, row == positive - self.firsts[first]

    def __call__(self, text, image, positive, first):
        logits, hits = self.logits(text, image, positive, first)
        decay = jnp.exp(-jnp.abs(logits))
        share = 1.0 / (1.0 + decay)
        sigmoid = jnp.where(logits >= 0.0, share, decay * share)
        weights = (sigmoid - hits.astype(jnp.float32)).astype(jnp.bfloat16)

        def loss():
            signed = jnp.where(hits, -logits, logits)
            return jnp.sum(jnp.maximum(signed, 0.0) + jnp.log1p(decay), axis=0, keepdims=True)

        return weights, loss


def read_after(after):
    rows = after.shape[0] - TAIL
    digits = after[pl.ds(rows, TAIL), pl.ds(0, rows)].astype(jnp.float32).astype(jnp.int32)
    far = sum(digits[k : k + 1, :] << shift for k, shift in enumerate(SHIFTS))
    return after[pl.ds(0, rows), :], far


def by_image(weights, image):
    return jnp.dot(weights, image, preferred_element_type=jnp.float32)


def gate_kernel(*refs):
    pass


def gate(array, *tokens):
    anywhere = pl.BlockSpec(memory_space=pl.ANY)
    return pl.pallas_call(
        gate_kernel,
        name="gate",
        out_shape=pltpu.VMEM(array.shape, array.dtype),
        in_specs=[anywhere] * (1 + len(tokens)),
        out_specs=anywhere,
        input_output_aliases={0: 0},
    )(pltpu.with_memory_space_constraint(array, pltpu.VMEM), *tokens)


def first_kernel(
    firsts,
    reals,
    image_0,
    image_1,
    text_0,
    text_1,
    prior_0,
    after_0,
    near_0,
    near_1,
    image_part,
    text_part,
    loss_part,
):
    block = Blocks(firsts, reals)
    weights, losses = block(text_1[...], image_1[...], near_1[...], 1)
    image_part[...] = over_first(weights, text_1[...])
    text_part[...] = by_image(weights, image_1[...])
    loss_part[...] = losses()
    weights, losses = block(text_0[...], image_1[...], near_1[...], 0)
    image_part[...] += over_first(weights, text_0[...])
    loss_part[...] += losses()
    weights, losses = block(prior_0[...], image_1[...], near_1[...], 2)
    image_part[...] += over_first(weights, prior_0[...])
    loss_part[...] += losses()
    weights, _ = block(text_1[...], image_0[...], near_0[...], 1)
    text_part[...] += by_image(weights, image_0[...])
    image, far = read_after(after_0)
    weights, _ = block(text_1[...], image, far, 1)
    text_part[...] += by_image(weights, image)


def text_kernel(firsts, reals, text_1, after_1, far_1, text_part, text_send):
    weights, _ = Blocks(firsts, reals)(text_1[...], after_1[...], far_1[...], 1)
    total = text_part[...] + by_image(weights, after_1[...])
    text_send[...] = total.astype(text_send.dtype)


def image_kernel(
    firsts, reals, image_1, prior_1, near_1, image_part, loss_part, sent, image_send, loss_send
):
    weights, losses = Blocks(firsts, reals)(prior_1[...], image_1[...], near_1[...], 3)
    total = image_part[...] + over_first(weights, prior_1[...])
    image_send[...] = total.astype(image_send.dtype)
    loss_send[...] = loss_part[...] + losses()


def late_kernel(
    firsts,
    reals,
    image_0,
    image_1,
    text_0,
    text_1,
    prior_0,
    prior_1,
    after_0,
    after_1,
    near_0,
    near_1,
    far_1,
    image_sent,
    image_own,
    text_own,
    loss_own,
):
    block = Blocks(firsts, reals)
    weights, losses = block(text_0[...], image_0[...], near_0[...], 0)
    image_own[...] = over_first(weights, text_0[...])
    text_own[...] = by_image(weights, image_0[...])
    loss_own[...] = losses()
    for k, text in ((1, text_1), (2, prior_0), (3, prior_1)):
        weights, losses = block(text[...], image_0[...], near_0[...], k)
        image_own[...] += over_first(weights, text[...])
        loss_own[...] += losses()
    after, far = read_after(after_0)
    for image, positive in ((image_1[...], near_1[...]), (after, far), (after_1[...], far_1[...])):
        weights, _ = block(text_0[...], image, positive, 0)
        text_own[...] += by_image(weights, image)


def call(kernel, name, in_specs, outs, blocks):
    return pl.pallas_call(
        kernel,
        name=name,
        out_shape=outs,
        in_specs=in_specs,
        out_specs=[VMEM] * len(outs),
        compiler_params=pltpu.CompilerParams(vmem_limit_bytes=LIMIT),
        cost_estimate=pl.CostEstimate(
            flops=2 * blocks * 256 * 256 * 1152, bytes_accessed=1 << 20, transcendentals=0
        ),
    )


def per_device(images, texts, positive, logit_scale, logit_bias):
    rows, width = texts.shape
    count = lax.axis_size("outer")
    group = lax.axis_index("outer")
    me = lax.axis_index("inner")
    whole = lax.axis_size("inner") * rows
    before = (group - 1 + count) % count
    firsts = jnp.stack(
        [
            group * whole + me * rows,
            group * whole + (3 - me) * rows,
            before * whole + me * rows,
            before * whole + (3 - me) * rows,
        ]
    ).astype(jnp.int32)
    reals = jnp.concatenate([logit_scale, logit_bias])
    shard = jax.ShapeDtypeStruct((rows, width), jnp.bfloat16)
    long_shard = jax.ShapeDtypeStruct((rows + TAIL, width), jnp.bfloat16)
    real_shard = jax.ShapeDtypeStruct((rows, width), jnp.float32)
    line = jax.ShapeDtypeStruct((1, rows), jnp.float32)

    text_1 = lax.ppermute(texts, "inner", TEXT_PAIRS)
    image_1 = lax.ppermute(images, "inner", IMAGE_PAIRS)
    near_0 = positive[None, :]
    images_later, texts_later = call(
        hold_kernel, "hold", [VMEM] * 3, [long_shard, shard], 1
    )(images, texts, near_0)
    near_1 = lax.ppermute(near_0, "inner", IMAGE_PAIRS)
    prior_0 = from_behind(texts_later, 1)
    after_0 = from_behind(images_later, -1)
    image_1 = gate(image_1, near_1)
    after_1 = from_behind(image_1, -1)
    prior_1 = from_behind(text_1, 1)
    far_1 = from_behind(near_1, -1)

    image_part, text_part, loss_part = call(
        first_kernel, "first", [SMEM] * 2 + [VMEM] * 8, [real_shard, real_shard, line], 11
    )(firsts, reals, images, image_1, texts, text_1, prior_0, after_0, near_0, near_1)
    (text_send,) = call(text_kernel, "text", [SMEM] * 2 + [VMEM] * 4, [shard], 2)(
        firsts, reals, text_1, after_1, far_1, text_part
    )
    image_send, loss_send = call(image_kernel, "image", [SMEM] * 2 + [VMEM] * 5 + [pl.BlockSpec(memory_space=pl.ANY)], [shard, line], 2)(
        firsts, reals, image_1, prior_1, near_1, image_part, loss_part, text_send
    )
    image_own, text_own, loss_own = call(
        late_kernel,
        "late",
        [SMEM] * 2 + [VMEM] * 11 + [pl.BlockSpec(memory_space=pl.ANY)],
        [real_shard, real_shard, line],
        15,
    )(
        firsts,
        reals,
        images,
        image_1,
        texts,
        text_1,
        prior_0,
        prior_1,
        after_0,
        after_1,
        near_0,
        near_1,
        far_1,
        image_send,
    )
    image_back = lax.ppermute(image_send, "inner", IMAGE_PAIRS)
    text_back = lax.ppermute(text_send, "inner", TEXT_PAIRS)
    loss_back = lax.ppermute(loss_send, "inner", IMAGE_PAIRS)
    scale = logit_scale[0]
    loss_rows = (loss_own + loss_back)[0]
    image_grad = (scale * (image_own + image_back.astype(jnp.float32))).astype(jnp.bfloat16)
    text_grad = (scale * (text_own + text_back.astype(jnp.float32))).astype(jnp.bfloat16)
    return (loss_rows, image_grad, text_grad)


def solution(mesh):
    return jax.shard_map(
        per_device,
        mesh=mesh,
        in_specs=(
            P(("outer", "inner"), None),
            P(("outer", "inner"), None),
            P(("outer", "inner")),
            P(),
            P(),
        ),
        out_specs=(P(("outer", "inner")), P(("outer", "inner"), None), P(("outer", "inner"), None)),
        check_vma=False,
    )
```

time: 143 us -> 130 us (0.909)
  the two profiles are of different devices: /device:TPU:129 before, /device:TPU:1 now
where the time goes in v4:
time: 130 us; the launch traced here: 128 us
  starting transfers between devices  67.2 us (52%)
  waiting for transfers between devices  37.2 us (29%)
  Pallas kernels  14.4 us (11%)
  local copies, waits for them, and re-layouts  4.04 us (3%)
  other arithmetic  2.68 us (2%)
  between operations  2.16 us (2%)
    ppermute x5, starting transfers between devices, from_behind(): lax.ppermute(block, 'outer', [((i - distance) % count, i) for i in range(...  35 us
    ppermute x1, waiting for transfers between devices, per_device(): loss_back = lax.ppermute(loss_send, 'inner', IMAGE_PAIRS)  25.5 us
    ppermute x1, waiting for transfers between devices, per_device(): near_1 = lax.ppermute(near_0, 'inner', IMAGE_PAIRS)  11.6 us
    ppermute x1, starting transfers between devices, per_device(): text_1 = lax.ppermute(texts, 'inner', TEXT_PAIRS)  9.43 us
    ppermute x1, starting transfers between devices, per_device(): image_1 = lax.ppermute(images, 'inner', IMAGE_PAIRS)  8.45 us
    pallas_call x1, Pallas kernels, per_device(): call(late_kernel, 'late', [SMEM] * 2 + [VMEM] * 11 + [pl.BlockSpec(memory...  5.59 us
    ppermute x1, starting transfers between devices, per_device(): text_back = lax.ppermute(text_send, 'inner', TEXT_PAIRS)  5.51 us
    ppermute x1, starting transfers between devices, per_device(): near_1 = lax.ppermute(near_0, 'inner', IMAGE_PAIRS)  4.92 us
  transfers between devices with their start and end apart: 11, of which 2 were waited for; matrix products, arithmetic and copies ran while one was open for 1% of the time, Pallas kernels for 10%

profile of v4, /device:TPU:1, one launch (start us, length us, event | category | flops | bytes accessed | tf_op | source)
XLA Modules:
  0.0 127.7 jit_solution(17747985033868932136)
XLA Ops:
  0.6 8.4 %collective-permute-start = (bf16[256,1152]{1,0:T(8,128)(2,1)}, bf16[256,1152]{1,0:T(8,128)(2,1)S(1)}, u32[]{:S(2)}, u32[]{:S(2)}) collective-permute-start(bf16[256,1152]{1,0:T(8,128)(2,1)} %image_0.3), channel_id=1, source_target_pairs={{0,1},{1,0},{2,3},{3,2},{4,5},{5,4},{6,7},{7,6},{8,9},{9,8},{10,11... | collective-permute-start | bytes 1769480 | tf_op jit(solution)/shard_map/ppermute | solution.py:210
  9.1 9.4 %collective-permute-start.2 = (bf16[256,1152]{1,0:T(8,128)(2,1)}, bf16[256,1152]{1,0:T(8,128)(2,1)S(1)}, u32[]{:S(2)}, u32[]{:S(2)}) collective-permute-start(bf16[256,1152]{1,0:T(8,128)(2,1)} %text_0.3), channel_id=1, source_target_pairs={{1,2},{2,1},{3,0},{0,3},{5,6},{6,5},{7,4},{4,7},{9,10},{10,9},{11,... | collective-permute-start | bytes 1769480 | tf_op jit(solution)/shard_map/ppermute | solution.py:209
  18.5 0.0 copy-start
  18.5 1.1 copy-done
  19.6 0.0 copy-start.2
  19.6 1.1 copy-done.2
  20.7 0.0 copy-start.6
  20.7 0.7 copy-done.6
  21.3 0.0 copy-start.1
  21.3 0.0 copy-start.3
  21.3 0.0 copy-start.7
  21.3 1.1 hold.1
  22.4 3.1 %collective-permute-start.5 = (bf16[272,1152]{1,0:T(8,128)(2,1)}, bf16[272,1152]{1,0:T(8,128)(2,1)}, u32[]{:S(2)}, u32[]{:S(2)}) collective-permute-start(bf16[272,1152]{1,0:T(8,128)(2,1)} %get-tuple-element.14), channel_id=1, source_target_pairs={{4,0},{8,4},{12,8},{16,12},{20,16},{24,20},{28,24},{32,28},{36,32}... | collective-permute-start | bytes 1880072 | tf_op jit(solution)/shard_map/ppermute | solution.py:21
  25.6 3.1 %collective-permute-start.3 = (bf16[256,1152]{1,0:T(8,128)(2,1)}, bf16[256,1152]{1,0:T(8,128)(2,1)}, u32[]{:S(2)}, u32[]{:S(2)}) collective-permute-start(bf16[256,1152]{1,0:T(8,128)(2,1)} %get-tuple-element.13), channel_id=1, source_target_pairs={{764,0},{0,4},{4,8},{8,12},{12,16},{16,20},{20,24},{24,28},{28,32}... | collective-permute-start | bytes 1769480 | tf_op jit(solution)/shard_map/ppermute | solution.py:21
  28.7 4.9 %collective-permute-start.1 = (s32[1,256]{1,0:T(1,128)S(1)}, s32[1,256]{1,0:T(1,128)S(1)}, u32[]{:S(2)}, u32[]{:S(2)}) collective-permute-start(s32[1,256]{1,0:T(1,128)S(1)} %bitcast.10), channel_id=1, source_target_pairs={{0,1},{1,0},{2,3},{3,2},{4,5},{5,4},{6,7},{7,6},{8,9},{9,8},{10,11... | collective-permute-start | bytes 3080 | tf_op jit(solution)/shard_map/ppermute | solution.py:215
  33.6 11.6 %collective-permute-done.1.refs_1_.near_1 = s32[1,256]{1,0:T(1,128)S(1)} collective-permute-done((s32[1,256]{1,0:T(1,128)S(1)}, s32[1,256]{1,0:T(1,128)S(1)}, u32[]{:S(2)}, u32[]{:S(2)}) %collective-permute-start.1) | collective-permute-done | bytes 1056 | tf_op jit(solution)/shard_map/ppermute | solution.py:215
  45.3 0.0 copy-start.4
  45.3 0.0 collective-permute-done.refs_0_
  45.3 0.6 copy-done.4
  45.8 16.8 %collective-permute-start.6 = (bf16[256,1152]{1,0:T(8,128)(2,1)S(1)}, bf16[256,1152]{1,0:T(8,128)(2,1)S(1)}, u32[]{:S(2)}, u32[]{:S(2)}) collective-permute-start(bf16[256,1152]{1,0:T(8,128)(2,1)S(1)} %gate.1.image_1), channel_id=1, source_target_pairs={{4,0},{8,4},{12,8},{16,12},{20,16},{24,20},{28,24},{32,28},{36,32}... | collective-permute-start | bytes 1769480 | tf_op jit(solution)/shard_map/ppermute | solution.py:21
  62.6 0.0 collective-permute-done.2.text_1
  62.6 1.9 %collective-permute-start.4 = (bf16[256,1152]{1,0:T(8,128)(2,1)S(1)}, bf16[256,1152]{1,0:T(8,128)(2,1)S(1)}, u32[]{:S(2)}, u32[]{:S(2)}) collective-permute-start(bf16[256,1152]{1,0:T(8,128)(2,1)S(1)} %collective-permute-done.2.text_1), channel_id=1, source_target_pairs={{764,0},{0,4},{4,8},{8,12},{12,16},{16,20},{20,24},{24,28},{28,32}... | collective-permute-start | bytes 1769480 | tf_op jit(solution)/shard_map/ppermute | solution.py:21
  65.9 0.1 pad_maximum_fusion.reals
  66.0 0.1 pad_add_fusion.firsts
  66.0 10.0 %collective-permute-start.7 = (s32[1,256]{1,0:T(1,128)}, s32[1,256]{1,0:T(1,128)S(1)}, u32[]{:S(2)}, u32[]{:S(2)}) collective-permute-start(s32[1,256]{1,0:T(1,128)} %copy-done.4), channel_id=1, source_target_pairs={{4,0},{8,4},{12,8},{16,12},{20,16},{24,20},{28,24},{32,28},{36,32}... | collective-permute-start | bytes 3080 | tf_op jit(solution)/shard_map/ppermute | solution.py:21
  76.1 0.0 collective-permute-done.3.prior_0
  76.1 0.0 collective-permute-done.5.after_0
  76.1 0.0 copy-done.1
  76.1 0.0 copy-done.3
  76.1 0.0 copy-done.7
  76.1 0.0 copy-start.5
  76.2 0.7 copy-done.5
  76.8 4.5 %first.1 = (f32[256,1152]{1,0:T(8,128)S(1)}, f32[256,1152]{1,0:T(8,128)S(1)}, f32[1,256]{1,0:T(1,128)S(1)}) custom-call(s32[4]{0:T(128)S(1)} %pad_add_fusion.firsts, f32[2]{0:T(128)S(1)} %pad_maximum_fusion.reals, bf16[256,1152]{1,0:T(8,128)(2,1)S(1)} %copy-done.1, bf16[256,1152]{1,0:T(8,128)(2,1)S(1)} %gate.1.image_1, bf16[256,1152]{1,0:T(8,128)(2,1)S(1)} %copy-done.3, ...), custom_call_target="tpu_custom_call" | custom-call | flops 1660944384 | bytes 1048576 | tf_op jit(solution)/shard_map/first/pallas_call | solution.py:223
  81.4 0.0 collective-permute-done.7.far_1
  81.4 0.0 collective-permute-done.6.after_1
  81.4 1.5 %text.1.sent = bf16[256,1152]{1,0:T(8,128)(2,1)S(1)} custom-call(s32[4]{0:T(128)S(1)} %pad_add_fusion.firsts, f32[2]{0:T(128)S(1)} %pad_maximum_fusion.reals, bf16[256,1152]{1,0:T(8,128)(2,1)S(1)} %collective-permute-done.2.text_1, bf16[256,1152]{1,0:T(8,128)(2,1)S(1)} %collective-permute-done.6.after_1, s32[1,256]{1,0:T(1,128)S(1)} %collective-permute-done.7.far_1, ...), custom_call_target="tpu_custom_call" | custom-call | flops 301989888 | bytes 1048576 | tf_op jit(solution)/shard_map/text/pallas_call | solution.py:226
  82.9 0.0 collective-permute-done.4.prior_1
  82.9 1.7 %image.1 = (bf16[256,1152]{1,0:T(8,128)(2,1)S(1)}, f32[1,256]{1,0:T(1,128)S(1)}) custom-call(s32[4]{0:T(128)S(1)} %pad_add_fusion.firsts, f32[2]{0:T(128)S(1)} %pad_maximum_fusion.reals, bf16[256,1152]{1,0:T(8,128)(2,1)S(1)} %gate.1.image_1, bf16[256,1152]{1,0:T(8,128)(2,1)S(1)} %collective-permute-done.4.prior_1, s32[1,256]{1,0:T(1,128)S(1)} %copy-done.5, ...), custom_call_target="tpu_custom_call" | custom-call | flops 301989888 | bytes 1048576 | tf_op jit(solution)/shard_map/image/pallas_call | solution.py:229
  84.6 1.9 %collective-permute-start.9 = (bf16[256,1152]{1,0:T(8,128)(2,1)S(1)}, bf16[256,1152]{1,0:T(8,128)(2,1)S(1)}, u32[]{:S(2)}, u32[]{:S(2)}) collective-permute-start(bf16[256,1152]{1,0:T(8,128)(2,1)S(1)} %get-tuple-element.18.image_sent), channel_id=1, source_target_pairs={{0,1},{1,0},{2,3},{3,2},{4,5},{5,4},{6,7},{7,6},{8,9},{9,8},{10,11... | collective-permute-start | bytes 1769480 | tf_op jit(solution)/shard_map/ppermute | solution.py:254
  86.5 5.5 %collective-permute-start.10 = (bf16[256,1152]{1,0:T(8,128)(2,1)S(1)}, bf16[256,1152]{1,0:T(8,128)(2,1)S(1)}, u32[]{:S(2)}, u32[]{:S(2)}) collective-permute-start(bf16[256,1152]{1,0:T(8,128)(2,1)S(1)} %text.1.sent), channel_id=1, source_target_pairs={{1,2},{2,1},{3,0},{0,3},{5,6},{6,5},{7,4},{4,7},{9,10},{10,9},{11,... | collective-permute-start | bytes 1769480 | tf_op jit(solution)/shard_map/ppermute | solution.py:255
  92.1 1.9 %collective-permute-start.8 = (f32[1,256]{1,0:T(1,128)S(1)}, f32[1,256]{1,0:T(1,128)S(1)}, u32[]{:S(2)}, u32[]{:S(2)}) collective-permute-start(f32[1,256]{1,0:T(1,128)S(1)} %get-tuple-element.20), channel_id=1, source_target_pairs={{0,1},{1,0},{2,3},{3,2},{4,5},{5,4},{6,7},{7,6},{8,9},{9,8},{10,11... | collective-permute-start | bytes 3080 | tf_op jit(solution)/shard_map/ppermute | solution.py:256
  94.0 5.6 %late.1 = (f32[256,1152]{1,0:T(8,128)S(1)}, f32[256,1152]{1,0:T(8,128)S(1)}, f32[1,256]{1,0:T(1,128)S(1)}) custom-call(s32[4]{0:T(128)S(1)} %pad_add_fusion.firsts, f32[2]{0:T(128)S(1)} %pad_maximum_fusion.reals, bf16[256,1152]{1,0:T(8,128)(2,1)S(1)} %copy-done.1, bf16[256,1152]{1,0:T(8,128)(2,1)S(1)} %gate.1.image_1, bf16[256,1152]{1,0:T(8,128)(2,1)S(1)} %copy-done.3, ...), custom_call_target="tpu_custom_call" | custom-call | flops 2264924160 | bytes 1048576 | tf_op jit(solution)/shard_map/late/pallas_call | solution.py:232
  99.6 25.5 %collective-permute-done.8 = f32[1,256]{1,0:T(1,128)S(1)} collective-permute-done((f32[1,256]{1,0:T(1,128)S(1)}, f32[1,256]{1,0:T(1,128)S(1)}, u32[]{:S(2)}, u32[]{:S(2)}) %collective-permute-start.8) | collective-permute-done | bytes 1056 | tf_op jit(solution)/shard_map/ppermute | solution.py:256
  125.1 0.6 add.37
  125.7 0.0 collective-permute-done.9
  125.7 1.0 multiply_convert_fusion.1
  126.7 0.0 collective-permute-done.10
  126.7 1.0 multiply_convert_fusion
  (1 shorter events, 0.0 us)
Async XLA Ops:
  0.6 44.6 %collective-permute-start = (bf16[256,1152]{1,0:T(8,128)(2,1)}, bf16[256,1152]{1,0:T(8,128)(2,1)S(1)}, u32[]{:S(2)}, u32[]{:S(2)}) collective-permute-start(bf16[256,1152]{1,0:T(8,128)(2,1)} %image_0.3), channel_id=1, source_target_pairs={{0,1},{1,0},{2,3},{3,2},{4,5},{5,4},{6,7},{7,6},{8,9},{9,8},{10,11... | collective-permute-start | bytes 1769480 | tf_op jit(solution)/shard_map/ppermute | solution.py:210
  9.1 53.5 %collective-permute-start.2 = (bf16[256,1152]{1,0:T(8,128)(2,1)}, bf16[256,1152]{1,0:T(8,128)(2,1)S(1)}, u32[]{:S(2)}, u32[]{:S(2)}) collective-permute-start(bf16[256,1152]{1,0:T(8,128)(2,1)} %text_0.3), channel_id=1, source_target_pairs={{1,2},{2,1},{3,0},{0,3},{5,6},{6,5},{7,4},{4,7},{9,10},{10,9},{11,... | collective-permute-start | bytes 1769480 | tf_op jit(solution)/shard_map/ppermute | solution.py:209
  18.5 1.1 copy-start
  19.6 1.1 copy-start.2
  20.7 0.7 copy-start.6
  21.3 54.8 %copy-start.1 = (bf16[256,1152]{1,0:T(8,128)(2,1)S(1)}, bf16[256,1152]{1,0:T(8,128)(2,1)}, u32[]{:S(2)}) copy-start(bf16[256,1152]{1,0:T(8,128)(2,1)} %image_0.3) | copy-start | bytes 1769476
  21.3 54.8 %copy-start.3 = (bf16[256,1152]{1,0:T(8,128)(2,1)S(1)}, bf16[256,1152]{1,0:T(8,128)(2,1)}, u32[]{:S(2)}) copy-start(bf16[256,1152]{1,0:T(8,128)(2,1)} %text_0.3) | copy-start | bytes 1769476
  21.3 54.8 %copy-start.7 = (s32[256]{0:T(256)S(1)}, s32[256]{0:T(256)}, u32[]{:S(2)}) copy-start(s32[256]{0:T(256)} %param.7) | copy-start | bytes 3076
  22.4 53.7 %collective-permute-start.5 = (bf16[272,1152]{1,0:T(8,128)(2,1)}, bf16[272,1152]{1,0:T(8,128)(2,1)}, u32[]{:S(2)}, u32[]{:S(2)}) collective-permute-start(bf16[272,1152]{1,0:T(8,128)(2,1)} %get-tuple-element.14), channel_id=1, source_target_pairs={{4,0},{8,4},{12,8},{16,12},{20,16},{24,20},{28,24},{32,28},{36,32}... | collective-permute-start | bytes 1880072 | tf_op jit(solution)/shard_map/ppermute | solution.py:21
  25.6 50.5 %collective-permute-start.3 = (bf16[256,1152]{1,0:T(8,128)(2,1)}, bf16[256,1152]{1,0:T(8,128)(2,1)}, u32[]{:S(2)}, u32[]{:S(2)}) collective-permute-start(bf16[256,1152]{1,0:T(8,128)(2,1)} %get-tuple-element.13), channel_id=1, source_target_pairs={{764,0},{0,4},{4,8},{8,12},{12,16},{16,20},{20,24},{24,28},{28,32}... | collective-permute-start | bytes 1769480 | tf_op jit(solution)/shard_map/ppermute | solution.py:21
  28.7 16.6 %collective-permute-start.1 = (s32[1,256]{1,0:T(1,128)S(1)}, s32[1,256]{1,0:T(1,128)S(1)}, u32[]{:S(2)}, u32[]{:S(2)}) collective-permute-start(s32[1,256]{1,0:T(1,128)S(1)} %bitcast.10), channel_id=1, source_target_pairs={{0,1},{1,0},{2,3},{3,2},{4,5},{5,4},{6,7},{7,6},{8,9},{9,8},{10,11... | collective-permute-start | bytes 3080 | tf_op jit(solution)/shard_map/ppermute | solution.py:215
  45.3 0.6 copy-start.4
  45.8 35.6 %collective-permute-start.6 = (bf16[256,1152]{1,0:T(8,128)(2,1)S(1)}, bf16[256,1152]{1,0:T(8,128)(2,1)S(1)}, u32[]{:S(2)}, u32[]{:S(2)}) collective-permute-start(bf16[256,1152]{1,0:T(8,128)(2,1)S(1)} %gate.1.image_1), channel_id=1, source_target_pairs={{4,0},{8,4},{12,8},{16,12},{20,16},{24,20},{28,24},{32,28},{36,32}... | collective-permute-start | bytes 1769480 | tf_op jit(solution)/shard_map/ppermute | solution.py:21
  62.6 20.3 %collective-permute-start.4 = (bf16[256,1152]{1,0:T(8,128)(2,1)S(1)}, bf16[256,1152]{1,0:T(8,128)(2,1)S(1)}, u32[]{:S(2)}, u32[]{:S(2)}) collective-permute-start(bf16[256,1152]{1,0:T(8,128)(2,1)S(1)} %collective-permute-done.2.text_1), channel_id=1, source_target_pairs={{764,0},{0,4},{4,8},{8,12},{12,16},{16,20},{20,24},{24,28},{28,32}... | collective-permute-start | bytes 1769480 | tf_op jit(solution)/shard_map/ppermute | solution.py:21
  66.0 15.3 %collective-permute-start.7 = (s32[1,256]{1,0:T(1,128)}, s32[1,256]{1,0:T(1,128)S(1)}, u32[]{:S(2)}, u32[]{:S(2)}) collective-permute-start(s32[1,256]{1,0:T(1,128)} %copy-done.4), channel_id=1, source_target_pairs={{4,0},{8,4},{12,8},{16,12},{20,16},{24,20},{28,24},{32,28},{36,32}... | collective-permute-start | bytes 3080 | tf_op jit(solution)/shard_map/ppermute | solution.py:21
  76.1 0.7 copy-start.5
  84.6 41.1 %collective-permute-start.9 = (bf16[256,1152]{1,0:T(8,128)(2,1)S(1)}, bf16[256,1152]{1,0:T(8,128)(2,1)S(1)}, u32[]{:S(2)}, u32[]{:S(2)}) collective-permute-start(bf16[256,1152]{1,0:T(8,128)(2,1)S(1)} %get-tuple-element.18.image_sent), channel_id=1, source_target_pairs={{0,1},{1,0},{2,3},{3,2},{4,5},{5,4},{6,7},{7,6},{8,9},{9,8},{10,11... | collective-permute-start | bytes 1769480 | tf_op jit(solution)/shard_map/ppermute | solution.py:254
  86.5 40.1 %collective-permute-start.10 = (bf16[256,1152]{1,0:T(8,128)(2,1)S(1)}, bf16[256,1152]{1,0:T(8,128)(2,1)S(1)}, u32[]{:S(2)}, u32[]{:S(2)}) collective-permute-start(bf16[256,1152]{1,0:T(8,128)(2,1)S(1)} %text.1.sent), channel_id=1, source_target_pairs={{1,2},{2,1},{3,0},{0,3},{5,6},{6,5},{7,4},{4,7},{9,10},{10,9},{11,... | collective-permute-start | bytes 1769480 | tf_op jit(solution)/shard_map/ppermute | solution.py:255
  92.1 33.1 %collective-permute-start.8 = (f32[1,256]{1,0:T(1,128)S(1)}, f32[1,256]{1,0:T(1,128)S(1)}, u32[]{:S(2)}, u32[]{:S(2)}) collective-permute-start(f32[1,256]{1,0:T(1,128)S(1)} %get-tuple-element.20), channel_id=1, source_target_pairs={{0,1},{1,0},{2,3},{3,2},{4,5},{5,4},{6,7},{7,6},{8,9},{9,8},{10,11... | collective-permute-start | bytes 3080 | tf_op jit(solution)/shard_map/ppermute | solution.py:256

commit v5 on v4

--- a/solution.py
+++ b/solution.py
@@ -14,6 +14,7 @@
 VMEM = pl.BlockSpec(memory_space=pltpu.VMEM)
 SMEM = pl.BlockSpec(memory_space=pltpu.SMEM)
 LIMIT = 40 * 1024 * 1024
+GATE_BLOCKS = 120
 
 
 def from_behind(block, distance):
@@ -29,19 +30,19 @@
     return lax.dot_general(x, y, (((0,), (0,)), ((), ())), preferred_element_type=jnp.float32)
 
 
-def hold_kernel(images, texts, positive, images_out, texts_out):
+def hold_kernel(places, scale, bias, images, texts, near_0, near_1, images_out, texts_out):
     rows = images.shape[0]
     images_out[pl.ds(0, rows), :] = images[...]
     images_out[pl.ds(rows, TAIL), :] = jnp.zeros((TAIL, images.shape[1]), jnp.bfloat16)
-    digits = [(positive[...] >> shift) & 255 for shift in SHIFTS]
-    digits = jnp.concatenate(digits + [jnp.zeros((TAIL - len(SHIFTS), rows), jnp.int32)])
+    digits = [(near[...] >> shift) & 255 for near in (near_0, near_1) for shift in SHIFTS]
+    digits = jnp.concatenate(digits + [jnp.zeros((TAIL - len(digits), rows), jnp.int32)])
     images_out[pl.ds(rows, TAIL), pl.ds(0, rows)] = digits.astype(jnp.float32).astype(jnp.bfloat16)
     texts_out[...] = texts[...]
 
 
 class Blocks:
-    def __init__(self, firsts, reals):
-        self.firsts, self.scale, self.bias = firsts, reals[0], reals[1]
+    def __init__(self, places, scale, bias):
+        self.firsts, self.scale, self.bias = places, scale[0], bias[0]
 
     def logits(self, text, image, positive, first):
         logits = self.scale * over_last(text, image) + self.bias
@@ -62,11 +63,11 @@
         return weights, loss
 
 
-def read_after(after):
+def read_far(after, shard):
     rows = after.shape[0] - TAIL
     digits = after[pl.ds(rows, TAIL), pl.ds(0, rows)].astype(jnp.float32).astype(jnp.int32)
-    far = sum(digits[k : k + 1, :] << shift for k, shift in enumerate(SHIFTS))
-    return after[pl.ds(0, rows), :], far
+    first = shard * len(SHIFTS)
+    return sum(digits[first + k : first + k + 1, :] << shift for k, shift in enumerate(SHIFTS))
 
 
 def by_image(weights, image):
@@ -86,12 +87,14 @@
         in_specs=[anywhere] * (1 + len(tokens)),
         out_specs=anywhere,
         input_output_aliases={0: 0},
+        cost_estimate=cost(GATE_BLOCKS),
     )(pltpu.with_memory_space_constraint(array, pltpu.VMEM), *tokens)
 
 
 def first_kernel(
-    firsts,
-    reals,
+    places,
+    scale,
+    bias,
     image_0,
     image_1,
     text_0,
@@ -104,7 +107,7 @@
     text_part,
     loss_part,
 ):
-    block = Blocks(firsts, reals)
+    block = Blocks(places, scale, bias)
     weights, losses = block(text_1[...], image_1[...], near_1[...], 1)
     image_part[...] = over_first(weights, text_1[...])
     text_part[...] = by_image(weights, image_1[...])
@@ -117,29 +120,39 @@
     loss_part[...] += losses()
     weights, _ = block(text_1[...], image_0[...], near_0[...], 1)
     text_part[...] += by_image(weights, image_0[...])
-    image, far = read_after(after_0)
-    weights, _ = block(text_1[...], image, far, 1)
-    text_part[...] += by_image(weights, image)
-
-
-def text_kernel(firsts, reals, text_1, after_1, far_1, text_part, text_send):
-    weights, _ = Blocks(firsts, reals)(text_1[...], after_1[...], far_1[...], 1)
+    after = after_0[pl.ds(0, image_0.shape[0]), :]
+    weights, _ = block(text_1[...], after, read_far(after_0, 0), 1)
+    text_part[...] += by_image(weights, after)
+
+
+def text_kernel(places, scale, bias, text_1, after_0, after_1, text_part, sent, text_send):
+    weights, _ = Blocks(places, scale, bias)(text_1[...], after_1[...], read_far(after_0, 1), 1)
     total = text_part[...] + by_image(weights, after_1[...])
     text_send[...] = total.astype(text_send.dtype)
 
 
 def image_kernel(
-    firsts, reals, image_1, prior_1, near_1, image_part, loss_part, sent, image_send, loss_send
+    places,
+    scale,
+    bias,
+    image_1,
+    prior_1,
+    near_1,
+    image_part,
+    loss_part,
+    image_send,
+    loss_send,
 ):
-    weights, losses = Blocks(firsts, reals)(prior_1[...], image_1[...], near_1[...], 3)
+    weights, losses = Blocks(places, scale, bias)(prior_1[...], image_1[...], near_1[...], 3)
     total = image_part[...] + over_first(weights, prior_1[...])
     image_send[...] = total.astype(image_send.dtype)
     loss_send[...] = loss_part[...] + losses()
 
 
 def late_kernel(
-    firsts,
-    reals,
+    places,
+    scale,
+    bias,
     image_0,
     image_1,
     text_0,
@@ -150,13 +163,12 @@
     after_1,
     near_0,
     near_1,
-    far_1,
-    image_sent,
+    sent,
     image_own,
     text_own,
     loss_own,
 ):
-    block = Blocks(firsts, reals)
+    block = Blocks(places, scale, bias)
     weights, losses = block(text_0[...], image_0[...], near_0[...], 0)
     image_own[...] = over_first(weights, text_0[...])
     text_own[...] = by_image(weights, image_0[...])
@@ -165,10 +177,20 @@
         weights, losses = block(text[...], image_0[...], near_0[...], k)
         image_own[...] += over_first(weights, text[...])
         loss_own[...] += losses()
-    after, far = read_after(after_0)
-    for image, positive in ((image_1[...], near_1[...]), (after, far), (after_1[...], far_1[...])):
+    after = after_0[pl.ds(0, image_0.shape[0]), :]
+    for image, positive in (
+        (image_1[...], near_1[...]),
+        (after, read_far(after_0, 0)),
+        (after_1[...], read_far(after_0, 1)),
+    ):
         weights, _ = block(text_0[...], image, positive, 0)
         text_own[...] += by_image(weights, image)
+
+
+def cost(blocks):
+    return pl.CostEstimate(
+        flops=2 * blocks * 256 * 256 * 1152, bytes_accessed=1 << 20, transcendentals=0
+    )
 
 
 def call(kernel, name, in_specs, outs, blocks):
@@ -179,9 +201,7 @@
         in_specs=in_specs,
         out_specs=[VMEM] * len(outs),
         compiler_params=pltpu.CompilerParams(vmem_limit_bytes=LIMIT),
-        cost_estimate=pl.CostEstimate(
-            flops=2 * blocks * 256 * 256 * 1152, bytes_accessed=1 << 20, transcendentals=0
-        ),
+        cost_estimate=cost(blocks),
     )
 
 
@@ -192,7 +212,7 @@
     me = lax.axis_index("inner")
     whole = lax.axis_size("inner") * rows
     before = (group - 1 + count) % count
-    firsts = jnp.stack(
+    places = jnp.stack(
         [
             group * whole + me * rows,
             group * whole + (3 - me) * rows,
@@ -200,44 +220,42 @@
             before * whole + (3 - me) * rows,
         ]
     ).astype(jnp.int32)
-    reals = jnp.concatenate([logit_scale, logit_bias])
+    scalars = (places, logit_scale, logit_bias)
     shard = jax.ShapeDtypeStruct((rows, width), jnp.bfloat16)
     long_shard = jax.ShapeDtypeStruct((rows + TAIL, width), jnp.bfloat16)
     real_shard = jax.ShapeDtypeStruct((rows, width), jnp.float32)
     line = jax.ShapeDtypeStruct((1, rows), jnp.float32)
-
-    text_1 = lax.ppermute(texts, "inner", TEXT_PAIRS)
-    image_1 = lax.ppermute(images, "inner", IMAGE_PAIRS)
+    anywhere = [pl.BlockSpec(memory_space=pl.ANY)]
+
     near_0 = positive[None, :]
+    near_1 = lax.ppermute(near_0, "inner", IMAGE_PAIRS)
+    text_1 = gate(lax.ppermute(texts, "inner", TEXT_PAIRS))
+    image_1 = gate(lax.ppermute(images, "inner", IMAGE_PAIRS))
     images_later, texts_later = call(
-        hold_kernel, "hold", [VMEM] * 3, [long_shard, shard], 1
-    )(images, texts, near_0)
-    near_1 = lax.ppermute(near_0, "inner", IMAGE_PAIRS)
+        hold_kernel, "hold", [SMEM] * 3 + [VMEM] * 4, [long_shard, shard], 1
+    )(*scalars, images, texts, near_0, near_1)
     prior_0 = from_behind(texts_later, 1)
     after_0 = from_behind(images_later, -1)
-    image_1 = gate(image_1, near_1)
     after_1 = from_behind(image_1, -1)
     prior_1 = from_behind(text_1, 1)
-    far_1 = from_behind(near_1, -1)
 
     image_part, text_part, loss_part = call(
-        first_kernel, "first", [SMEM] * 2 + [VMEM] * 8, [real_shard, real_shard, line], 11
-    )(firsts, reals, images, image_1, texts, text_1, prior_0, after_0, near_0, near_1)
-    (text_send,) = call(text_kernel, "text", [SMEM] * 2 + [VMEM] * 4, [shard], 2)(
-        firsts, reals, text_1, after_1, far_1, text_part
-    )
-    image_send, loss_send = call(image_kernel, "image", [SMEM] * 2 + [VMEM] * 5 + [pl.BlockSpec(memory_space=pl.ANY)], [shard, line], 2)(
-        firsts, reals, image_1, prior_1, near_1, image_part, loss_part, text_send
+        first_kernel, "first", [SMEM] * 3 + [VMEM] * 8, [real_shard, real_shard, line], 11
+    )(*scalars, images, image_1, texts, text_1, prior_0, after_0, near_0, near_1)
+    image_send, loss_send = call(
+        image_kernel, "image", [SMEM] * 3 + [VMEM] * 5, [shard, line], 2
+    )(*scalars, image_1, prior_1, near_1, image_part, loss_part)
+    (text_send,) = call(text_kernel, "text", [SMEM] * 3 + [VMEM] * 4 + anywhere, [shard], 2)(
+        *scalars, text_1, after_0, after_1, text_part, image_send
     )
     image_own, text_own, loss_own = call(
         late_kernel,
         "late",
-        [SMEM] * 2 + [VMEM] * 11 + [pl.BlockSpec(memory_space=pl.ANY)],
+        [SMEM] * 3 + [VMEM] * 10 + anywhere,
         [real_shard, real_shard, line],
         15,
     )(
-        firsts,
-        reals,
+        *scalars,
         images,
         image_1,
         texts,
@@ -248,9 +266,9 @@
         after_1,
         near_0,
         near_1,
-        far_1,
-        image_send,
-    )
+        text_send,
+    )
+
     image_back = lax.ppermute(image_send, "inner", IMAGE_PAIRS)
     text_back = lax.ppermute(text_send, "inner", TEXT_PAIRS)
     loss_back = lax.ppermute(loss_send, "inner", IMAGE_PAIRS)

time: 130 us -> 139 us (1.069)
  the two profiles are of different devices: /device:TPU:1 before, /device:TPU:127 now
where the time goes in v5:
time: 139 us
  starting transfers between devices  87 us (63%)
  waiting for transfers between devices  28.7 us (21%)
  Pallas kernels  15.4 us (11%)
  local copies, waits for them, and re-layouts  2.81 us (2%)
  other arithmetic  2.55 us (2%)
  between operations  2.15 us (2%)
    ppermute x1, starting transfers between devices, per_device(): text_back = lax.ppermute(text_send, 'inner', TEXT_PAIRS)  33.5 us
    ppermute x1, waiting for transfers between devices, per_device(): text_1 = gate(lax.ppermute(texts, 'inner', TEXT_PAIRS))  24 us
    ppermute x4, starting transfers between devices, from_behind(): lax.ppermute(block, 'outer', [((i - distance) % count, i) for i in range(...  23.6 us
    ppermute x1, starting transfers between devices, per_device(): text_1 = gate(lax.ppermute(texts, 'inner', TEXT_PAIRS))  13.4 us
    ppermute x1, starting transfers between devices, per_device(): image_back = lax.ppermute(image_send, 'inner', IMAGE_PAIRS)  5.65 us
    pallas_call x1, Pallas kernels, per_device(): call(late_kernel, 'late', [SMEM] * 3 + [VMEM] * 10 + anywhere, [real_shar...  5.6 us
    ppermute x1, starting transfers between devices, per_device(): image_1 = gate(lax.ppermute(images, 'inner', IMAGE_PAIRS))  5.53 us
    ppermute x1, waiting for transfers between devices, per_device(): loss_back = lax.ppermute(loss_send, 'inner', IMAGE_PAIRS)  4.66 us
  transfers between devices with their start and end apart: 10, of which 2 were waited for; matrix products, arithmetic and copies ran while one was open for 1% of the time, Pallas kernels for 10%

profile of v5, /device:TPU:127, one launch (start us, length us, event | category | flops | bytes accessed | tf_op | source)
XLA Modules:
  0.0 138.6 jit_solution(5327244254640094065)
XLA Ops:
  0.6 13.4 %collective-permute-start.1 = (bf16[256,1152]{1,0:T(8,128)(2,1)}, bf16[256,1152]{1,0:T(8,128)(2,1)S(1)}, u32[]{:S(2)}, u32[]{:S(2)}) collective-permute-start(bf16[256,1152]{1,0:T(8,128)(2,1)} %text_0.3), channel_id=1, source_target_pairs={{1,2},{2,1},{3,0},{0,3},{5,6},{6,5},{7,4},{4,7},{9,10},{10,9},{11,... | collective-permute-start | bytes 1769480 | tf_op jit(solution)/shard_map/ppermute | solution.py:232
  14.0 2.8 %collective-permute-start.2 = (s32[1,256]{1,0:T(1,128)}, s32[1,256]{1,0:T(1,128)S(1)}, u32[]{:S(2)}, u32[]{:S(2)}) collective-permute-start(s32[1,256]{1,0:T(1,128)} %bitcast.9), channel_id=1, source_target_pairs={{0,1},{1,0},{2,3},{3,2},{4,5},{5,4},{6,7},{7,6},{8,9},{9,8},{10,11... | collective-permute-start | bytes 3080 | tf_op jit(solution)/shard_map/ppermute | solution.py:231
  16.8 5.5 %collective-permute-start = (bf16[256,1152]{1,0:T(8,128)(2,1)}, bf16[256,1152]{1,0:T(8,128)(2,1)S(1)}, u32[]{:S(2)}, u32[]{:S(2)}) collective-permute-start(bf16[256,1152]{1,0:T(8,128)(2,1)} %image_0.3), channel_id=1, source_target_pairs={{0,1},{1,0},{2,3},{3,2},{4,5},{5,4},{6,7},{7,6},{8,9},{9,8},{10,11... | collective-permute-start | bytes 1769480 | tf_op jit(solution)/shard_map/ppermute | solution.py:233
  22.4 0.1 pad_add_fusion.places
  23.7 0.0 collective-permute-done.2.near_1
  23.8 0.0 copy-start
  23.8 1.1 copy-done
  24.8 0.0 copy-start.2
  24.8 1.1 copy-done.2
  25.9 0.0 copy-start.4
  25.9 0.7 copy-done.4
  26.6 1.6 %hold.1 = (bf16[272,1152]{1,0:T(8,128)(2,1)}, bf16[256,1152]{1,0:T(8,128)(2,1)}) custom-call(s32[4]{0:T(128)S(1)} %pad_add_fusion.places, f32[1]{0:T(128)} %copy.12.scale, f32[1]{0:T(128)S(6)} %copy.13.bias, bf16[256,1152]{1,0:T(8,128)(2,1)S(1)} %copy-done, bf16[256,1152]{1,0:T(8,128)(2,1)S(1)} %copy-done.2, s32[1,256]{1,0:T(1,128)S(1)} %bitcast.10, ...), custom_call_target="tpu_custom_call" | custom-call | flops 150994944 | bytes 1048576 | tf_op jit(solution)/shard_map/hold/pallas_call | solution.py:234
  28.2 3.6 %collective-permute-start.3 = (bf16[256,1152]{1,0:T(8,128)(2,1)}, bf16[256,1152]{1,0:T(8,128)(2,1)}, u32[]{:S(2)}, u32[]{:S(2)}) collective-permute-start(bf16[256,1152]{1,0:T(8,128)(2,1)} %get-tuple-element.13), channel_id=1, source_target_pairs={{764,0},{0,4},{4,8},{8,12},{12,16},{16,20},{20,24},{24,28},{28,32}... | collective-permute-start | bytes 1769480 | tf_op jit(solution)/shard_map/ppermute | solution.py:22
  31.8 1.9 %collective-permute-start.5 = (bf16[272,1152]{1,0:T(8,128)(2,1)}, bf16[272,1152]{1,0:T(8,128)(2,1)S(1)}, u32[]{:S(2)}, u32[]{:S(2)}) collective-permute-start(bf16[272,1152]{1,0:T(8,128)(2,1)} %get-tuple-element.14), channel_id=1, source_target_pairs={{4,0},{8,4},{12,8},{16,12},{20,16},{24,20},{28,24},{32,28},{36,32}... | collective-permute-start | bytes 1880072 | tf_op jit(solution)/shard_map/ppermute | solution.py:22
  33.8 24.0 %collective-permute-done.1.refs_0_ = bf16[256,1152]{1,0:T(8,128)(2,1)S(1)} collective-permute-done((bf16[256,1152]{1,0:T(8,128)(2,1)}, bf16[256,1152]{1,0:T(8,128)(2,1)S(1)}, u32[]{:S(2)}, u32[]{:S(2)}) %collective-permute-start.1) | collective-permute-done | bytes 589856 | tf_op jit(solution)/shard_map/ppermute | solution.py:232
  57.8 0.0 copy-start.1
  57.8 0.0 copy-start.3
  57.8 0.0 copy-start.5
  57.8 2.0 %collective-permute-start.4 = (bf16[256,1152]{1,0:T(8,128)(2,1)S(1)}, bf16[256,1152]{1,0:T(8,128)(2,1)}, u32[]{:S(2)}, u32[]{:S(2)}) collective-permute-start(bf16[256,1152]{1,0:T(8,128)(2,1)S(1)} %gate.3.text_1), channel_id=1, source_target_pairs={{764,0},{0,4},{4,8},{8,12},{12,16},{16,20},{20,24},{24,28},{28,32}... | collective-permute-start | bytes 1769480 | tf_op jit(solution)/shard_map/ppermute | solution.py:22
  59.8 0.0 collective-permute-done.refs_0_
  59.9 16.0 %collective-permute-start.6 = (bf16[256,1152]{1,0:T(8,128)(2,1)S(1)}, bf16[256,1152]{1,0:T(8,128)(2,1)S(1)}, u32[]{:S(2)}, u32[]{:S(2)}) collective-permute-start(bf16[256,1152]{1,0:T(8,128)(2,1)S(1)} %gate.2.image_1), channel_id=1, source_target_pairs={{4,0},{8,4},{12,8},{16,12},{20,16},{24,20},{28,24},{32,28},{36,32}... | collective-permute-start | bytes 1769480 | tf_op jit(solution)/shard_map/ppermute | solution.py:22
  75.9 0.0 collective-permute-done.3.prior_0
  75.9 0.0 collective-permute-done.5.after_0
  75.9 0.0 copy-done.1
  75.9 0.0 copy-done.3
  75.9 0.0 copy-done.5
  76.0 4.4 %first.1 = (f32[256,1152]{1,0:T(8,128)S(1)}, f32[256,1152]{1,0:T(8,128)S(1)}, f32[1,256]{1,0:T(1,128)S(1)}) custom-call(s32[4]{0:T(128)S(1)} %pad_add_fusion.places, f32[1]{0:T(128)} %copy.12.scale, f32[1]{0:T(128)S(6)} %copy.13.bias, bf16[256,1152]{1,0:T(8,128)(2,1)S(1)} %copy-done.1, bf16[256,1152]{1,0:T(8,128)(2,1)S(1)} %gate.2.image_1, ...), custom_call_target="tpu_custom_call" | custom-call | flops 1660944384 | bytes 1048576 | tf_op jit(solution)/shard_map/first/pallas_call | solution.py:242
  80.3 0.0 collective-permute-done.4.prior_1
  80.3 2.2 %image.1 = (bf16[256,1152]{1,0:T(8,128)(2,1)S(1)}, f32[1,256]{1,0:T(1,128)S(1)}) custom-call(s32[4]{0:T(128)S(1)} %pad_add_fusion.places, f32[1]{0:T(128)} %copy.12.scale, f32[1]{0:T(128)S(6)} %copy.13.bias, bf16[256,1152]{1,0:T(8,128)(2,1)S(1)} %gate.2.image_1, bf16[256,1152]{1,0:T(8,128)(2,1)} %collective-permute-done.4.prior_1, ...), custom_call_target="tpu_custom_call" | custom-call | flops 301989888 | bytes 1048576 | tf_op jit(solution)/shard_map/image/pallas_call | solution.py:245
  82.6 0.0 collective-permute-done.6.after_1
  82.6 1.5 %text.1.sent = bf16[256,1152]{1,0:T(8,128)(2,1)S(1)} custom-call(s32[4]{0:T(128)S(1)} %pad_add_fusion.places, f32[1]{0:T(128)} %copy.12.scale, f32[1]{0:T(128)S(6)} %copy.13.bias, bf16[256,1152]{1,0:T(8,128)(2,1)S(1)} %gate.3.text_1, bf16[272,1152]{1,0:T(8,128)(2,1)S(1)} %collective-permute-done.5.after_0, ...), custom_call_target="tpu_custom_call" | custom-call | flops 301989888 | bytes 1048576 | tf_op jit(solution)/shard_map/text/pallas_call | solution.py:248
  84.1 33.5 %collective-permute-start.9 = (bf16[256,1152]{1,0:T(8,128)(2,1)S(1)}, bf16[256,1152]{1,0:T(8,128)(2,1)S(1)}, u32[]{:S(2)}, u32[]{:S(2)}) collective-permute-start(bf16[256,1152]{1,0:T(8,128)(2,1)S(1)} %text.1.sent), channel_id=1, source_target_pairs={{1,2},{2,1},{3,0},{0,3},{5,6},{6,5},{7,4},{4,7},{9,10},{10,9},{11,... | collective-permute-start | bytes 1769480 | tf_op jit(solution)/shard_map/ppermute | solution.py:273
  117.6 5.6 %collective-permute-start.8 = (bf16[256,1152]{1,0:T(8,128)(2,1)S(1)}, bf16[256,1152]{1,0:T(8,128)(2,1)S(1)}, u32[]{:S(2)}, u32[]{:S(2)}) collective-permute-start(bf16[256,1152]{1,0:T(8,128)(2,1)S(1)} %get-tuple-element.18.sent), channel_id=1, source_target_pairs={{0,1},{1,0},{2,3},{3,2},{4,5},{5,4},{6,7},{7,6},{8,9},{9,8},{10,11... | collective-permute-start | bytes 1769480 | tf_op jit(solution)/shard_map/ppermute | solution.py:272
  123.2 2.6 %collective-permute-start.7 = (f32[1,256]{1,0:T(1,128)S(1)}, f32[1,256]{1,0:T(1,128)S(1)}, u32[]{:S(2)}, u32[]{:S(2)}) collective-permute-start(f32[1,256]{1,0:T(1,128)S(1)} %get-tuple-element.20), channel_id=1, source_target_pairs={{0,1},{1,0},{2,3},{3,2},{4,5},{5,4},{6,7},{7,6},{8,9},{9,8},{10,11... | collective-permute-start | bytes 3080 | tf_op jit(solution)/shard_map/ppermute | solution.py:274
  125.9 5.6 %late.1 = (f32[256,1152]{1,0:T(8,128)S(1)}, f32[256,1152]{1,0:T(8,128)S(1)}, f32[1,256]{1,0:T(1,128)S(1)}) custom-call(s32[4]{0:T(128)S(1)} %pad_add_fusion.places, f32[1]{0:T(128)} %copy.12.scale, f32[1]{0:T(128)S(6)} %copy.13.bias, bf16[256,1152]{1,0:T(8,128)(2,1)S(1)} %copy-done.1, bf16[256,1152]{1,0:T(8,128)(2,1)S(1)} %gate.2.image_1, ...), custom_call_target="tpu_custom_call" | custom-call | flops 2264924160 | bytes 1048576 | tf_op jit(solution)/shard_map/late/pallas_call | solution.py:251
  131.5 4.7 %collective-permute-done.7 = f32[1,256]{1,0:T(1,128)S(1)} collective-permute-done((f32[1,256]{1,0:T(1,128)S(1)}, f32[1,256]{1,0:T(1,128)S(1)}, u32[]{:S(2)}, u32[]{:S(2)}) %collective-permute-start.7) | collective-permute-done | bytes 1056 | tf_op jit(solution)/shard_map/ppermute | solution.py:274
  136.1 0.6 add.37
  136.7 0.0 collective-permute-done.9
  136.7 1.0 multiply_convert_fusion
  137.7 0.0 collective-permute-done.8
  137.7 1.0 multiply_convert_fusion.1
  (2 shorter events, 0.0 us)
Async XLA Ops:
  0.6 57.2 %collective-permute-start.1 = (bf16[256,1152]{1,0:T(8,128)(2,1)}, bf16[256,1152]{1,0:T(8,128)(2,1)S(1)}, u32[]{:S(2)}, u32[]{:S(2)}) collective-permute-start(bf16[256,1152]{1,0:T(8,128)(2,1)} %text_0.3), channel_id=1, source_target_pairs={{1,2},{2,1},{3,0},{0,3},{5,6},{6,5},{7,4},{4,7},{9,10},{10,9},{11,... | collective-permute-start | bytes 1769480 | tf_op jit(solution)/shard_map/ppermute | solution.py:232
  14.0 9.7 %collective-permute-start.2 = (s32[1,256]{1,0:T(1,128)}, s32[1,256]{1,0:T(1,128)S(1)}, u32[]{:S(2)}, u32[]{:S(2)}) collective-permute-start(s32[1,256]{1,0:T(1,128)} %bitcast.9), channel_id=1, source_target_pairs={{0,1},{1,0},{2,3},{3,2},{4,5},{5,4},{6,7},{7,6},{8,9},{9,8},{10,11... | collective-permute-start | bytes 3080 | tf_op jit(solution)/shard_map/ppermute | solution.py:231
  16.8 43.0 %collective-permute-start = (bf16[256,1152]{1,0:T(8,128)(2,1)}, bf16[256,1152]{1,0:T(8,128)(2,1)S(1)}, u32[]{:S(2)}, u32[]{:S(2)}) collective-permute-start(bf16[256,1152]{1,0:T(8,128)(2,1)} %image_0.3), channel_id=1, source_target_pairs={{0,1},{1,0},{2,3},{3,2},{4,5},{5,4},{6,7},{7,6},{8,9},{9,8},{10,11... | collective-permute-start | bytes 1769480 | tf_op jit(solution)/shard_map/ppermute | solution.py:233
  23.8 1.1 copy-start
  24.8 1.1 copy-start.2
  25.9 0.7 copy-start.4
  28.2 47.7 %collective-permute-start.3 = (bf16[256,1152]{1,0:T(8,128)(2,1)}, bf16[256,1152]{1,0:T(8,128)(2,1)}, u32[]{:S(2)}, u32[]{:S(2)}) collective-permute-start(bf16[256,1152]{1,0:T(8,128)(2,1)} %get-tuple-element.13), channel_id=1, source_target_pairs={{764,0},{0,4},{4,8},{8,12},{12,16},{16,20},{20,24},{24,28},{28,32}... | collective-permute-start | bytes 1769480 | tf_op jit(solution)/shard_map/ppermute | solution.py:22
  31.8 44.1 %collective-permute-start.5 = (bf16[272,1152]{1,0:T(8,128)(2,1)}, bf16[272,1152]{1,0:T(8,128)(2,1)S(1)}, u32[]{:S(2)}, u32[]{:S(2)}) collective-permute-start(bf16[272,1152]{1,0:T(8,128)(2,1)} %get-tuple-element.14), channel_id=1, source_target_pairs={{4,0},{8,4},{12,8},{16,12},{20,16},{24,20},{28,24},{32,28},{36,32}... | collective-permute-start | bytes 1880072 | tf_op jit(solution)/shard_map/ppermute | solution.py:22
  57.8 18.1 %copy-start.1 = (bf16[256,1152]{1,0:T(8,128)(2,1)S(1)}, bf16[256,1152]{1,0:T(8,128)(2,1)}, u32[]{:S(2)}) copy-start(bf16[256,1152]{1,0:T(8,128)(2,1)} %image_0.3) | copy-start | bytes 1769476
  57.8 18.2 %copy-start.3 = (bf16[256,1152]{1,0:T(8,128)(2,1)S(1)}, bf16[256,1152]{1,0:T(8,128)(2,1)}, u32[]{:S(2)}) copy-start(bf16[256,1152]{1,0:T(8,128)(2,1)} %text_0.3) | copy-start | bytes 1769476
  57.8 18.2 %copy-start.5 = (s32[256]{0:T(256)S(1)}, s32[256]{0:T(256)}, u32[]{:S(2)}) copy-start(s32[256]{0:T(256)} %param.7) | copy-start | bytes 3076
  57.8 22.5 %collective-permute-start.4 = (bf16[256,1152]{1,0:T(8,128)(2,1)S(1)}, bf16[256,1152]{1,0:T(8,128)(2,1)}, u32[]{:S(2)}, u32[]{:S(2)}) collective-permute-start(bf16[256,1152]{1,0:T(8,128)(2,1)S(1)} %gate.3.text_1), channel_id=1, source_target_pairs={{764,0},{0,4},{4,8},{8,12},{12,16},{16,20},{20,24},{24,28},{28,32}... | collective-permute-start | bytes 1769480 | tf_op jit(solution)/shard_map/ppermute | solution.py:22
  59.9 22.7 %collective-permute-start.6 = (bf16[256,1152]{1,0:T(8,128)(2,1)S(1)}, bf16[256,1152]{1,0:T(8,128)(2,1)S(1)}, u32[]{:S(2)}, u32[]{:S(2)}) collective-permute-start(bf16[256,1152]{1,0:T(8,128)(2,1)S(1)} %gate.2.image_1), channel_id=1, source_target_pairs={{4,0},{8,4},{12,8},{16,12},{20,16},{24,20},{28,24},{32,28},{36,32}... | collective-permute-start | bytes 1769480 | tf_op jit(solution)/shard_map/ppermute | solution.py:22
  84.1 52.6 %collective-permute-start.9 = (bf16[256,1152]{1,0:T(8,128)(2,1)S(1)}, bf16[256,1152]{1,0:T(8,128)(2,1)S(1)}, u32[]{:S(2)}, u32[]{:S(2)}) collective-permute-start(bf16[256,1152]{1,0:T(8,128)(2,1)S(1)} %text.1.sent), channel_id=1, source_target_pairs={{1,2},{2,1},{3,0},{0,3},{5,6},{6,5},{7,4},{4,7},{9,10},{10,9},{11,... | collective-permute-start | bytes 1769480 | tf_op jit(solution)/shard_map/ppermute | solution.py:273
  117.6 20.1 %collective-permute-start.8 = (bf16[256,1152]{1,0:T(8,128)(2,1)S(1)}, bf16[256,1152]{1,0:T(8,128)(2,1)S(1)}, u32[]{:S(2)}, u32[]{:S(2)}) collective-permute-start(bf16[256,1152]{1,0:T(8,128)(2,1)S(1)} %get-tuple-element.18.sent), channel_id=1, source_target_pairs={{0,1},{1,0},{2,3},{3,2},{4,5},{5,4},{6,7},{7,6},{8,9},{9,8},{10,11... | collective-permute-start | bytes 1769480 | tf_op jit(solution)/shard_map/ppermute | solution.py:272
  123.2 12.9 %collective-permute-start.7 = (f32[1,256]{1,0:T(1,128)S(1)}, f32[1,256]{1,0:T(1,128)S(1)}, u32[]{:S(2)}, u32[]{:S(2)}) collective-permute-start(f32[1,256]{1,0:T(1,128)S(1)} %get-tuple-element.20), channel_id=1, source_target_pairs={{0,1},{1,0},{2,3},{3,2},{4,5},{5,4},{6,7},{7,6},{8,9},{9,8},{10,11... | collective-permute-start | bytes 3080 | tf_op jit(solution)/shard_map/ppermute | solution.py:274

commit v6 on v5

--- a/solution.py
+++ b/solution.py
@@ -14,12 +14,26 @@
 VMEM = pl.BlockSpec(memory_space=pltpu.VMEM)
 SMEM = pl.BlockSpec(memory_space=pltpu.SMEM)
 LIMIT = 40 * 1024 * 1024
-GATE_BLOCKS = 120
-
-
-def from_behind(block, distance):
+ROOM = 5
+IS_FIRST, IS_LAST = 4, 5
+
+
+PLANES = 3
+
+
+def from_behind(block, distance, within=False):
     count = lax.axis_size("outer")
-    return lax.ppermute(block, "outer", [((i - distance) % count, i) for i in range(count)])
+    plane = count // PLANES
+    pairs = [((i - distance) % count, i) for i in range(count)]
+    if within:
+        pairs = [(i, j) for i, j in pairs if i // plane == j // plane]
+    return lax.ppermute(block, "outer", pairs)
+
+
+def over_edge(block):
+    plane = lax.axis_size("outer") // PLANES
+    pairs = [(k * plane + plane - 1, (k + 1) % PLANES * plane) for k in range(PLANES)]
+    return lax.ppermute(block, "outer", pairs + [(j, i) for i, j in pairs])
 
 
 def over_last(x, y):
@@ -30,14 +44,24 @@
     return lax.dot_general(x, y, (((0,), (0,)), ((), ())), preferred_element_type=jnp.float32)
 
 
-def hold_kernel(places, scale, bias, images, texts, near_0, near_1, images_out, texts_out):
+def hold_kernel(
+    places, scale, bias, images, texts, positive, images_out, texts_out, edge_out
+):
     rows = images.shape[0]
     images_out[pl.ds(0, rows), :] = images[...]
     images_out[pl.ds(rows, TAIL), :] = jnp.zeros((TAIL, images.shape[1]), jnp.bfloat16)
-    digits = [(near[...] >> shift) & 255 for near in (near_0, near_1) for shift in SHIFTS]
-    digits = jnp.concatenate(digits + [jnp.zeros((TAIL - len(digits), rows), jnp.int32)])
+    digits = [(positive[...] >> shift) & 255 for shift in SHIFTS]
+    digits = jnp.concatenate(digits + [jnp.zeros((TAIL - len(SHIFTS), rows), jnp.int32)])
     images_out[pl.ds(rows, TAIL), pl.ds(0, rows)] = digits.astype(jnp.float32).astype(jnp.bfloat16)
     texts_out[...] = texts[...]
+
+    @pl.when(places[IS_LAST] == 1)
+    def _():
+        edge_out[pl.ds(0, rows), :] = texts[...]
+
+    @pl.when(places[IS_LAST] == 0)
+    def _():
+        edge_out[...] = images_out[...]
 
 
 class Blocks:
@@ -63,11 +87,11 @@
         return weights, loss
 
 
-def read_far(after, shard):
+def read_after(after):
     rows = after.shape[0] - TAIL
     digits = after[pl.ds(rows, TAIL), pl.ds(0, rows)].astype(jnp.float32).astype(jnp.int32)
-    first = shard * len(SHIFTS)
-    return sum(digits[first + k : first + k + 1, :] << shift for k, shift in enumerate(SHIFTS))
+    far = sum(digits[k : k + 1, :] << shift for k, shift in enumerate(SHIFTS))
+    return after[pl.ds(0, rows), :], far
 
 
 def by_image(weights, image):
@@ -78,7 +102,7 @@
     pass
 
 
-def gate(array, *tokens):
+def gate(array, *tokens, blocks=0):
     anywhere = pl.BlockSpec(memory_space=pl.ANY)
     return pl.pallas_call(
         gate_kernel,
@@ -87,7 +111,7 @@
         in_specs=[anywhere] * (1 + len(tokens)),
         out_specs=anywhere,
         input_output_aliases={0: 0},
-        cost_estimate=cost(GATE_BLOCKS),
+        cost_estimate=cost(blocks),
     )(pltpu.with_memory_space_constraint(array, pltpu.VMEM), *tokens)
 
 
@@ -106,7 +130,9 @@
     image_part,
     text_part,
     loss_part,
-):
+    near_out,
+):
+    near_out[...] = near_1[...]
     block = Blocks(places, scale, bias)
     weights, losses = block(text_1[...], image_1[...], near_1[...], 1)
     image_part[...] = over_first(weights, text_1[...])
@@ -115,20 +141,20 @@
     weights, losses = block(text_0[...], image_1[...], near_1[...], 0)
     image_part[...] += over_first(weights, text_0[...])
     loss_part[...] += losses()
-    weights, losses = block(prior_0[...], image_1[...], near_1[...], 2)
-    image_part[...] += over_first(weights, prior_0[...])
-    loss_part[...] += losses()
     weights, _ = block(text_1[...], image_0[...], near_0[...], 1)
     text_part[...] += by_image(weights, image_0[...])
-    after = after_0[pl.ds(0, image_0.shape[0]), :]
-    weights, _ = block(text_1[...], after, read_far(after_0, 0), 1)
-    text_part[...] += by_image(weights, after)
-
-
-def text_kernel(places, scale, bias, text_1, after_0, after_1, text_part, sent, text_send):
-    weights, _ = Blocks(places, scale, bias)(text_1[...], after_1[...], read_far(after_0, 1), 1)
-    total = text_part[...] + by_image(weights, after_1[...])
-    text_send[...] = total.astype(text_send.dtype)
+
+    @pl.when(places[IS_FIRST] == 0)
+    def _():
+        weights, losses = block(prior_0[...], image_1[...], near_1[...], 2)
+        image_part[...] += over_first(weights, prior_0[...])
+        loss_part[...] += losses()
+
+    @pl.when(places[IS_LAST] == 0)
+    def _():
+        image, far = read_after(after_0)
+        weights, _ = block(text_1[...], image, far, 1)
+        text_part[...] += by_image(weights, image)
 
 
 def image_kernel(
@@ -140,13 +166,50 @@
     near_1,
     image_part,
     loss_part,
+    edge,
     image_send,
     loss_send,
 ):
-    weights, losses = Blocks(places, scale, bias)(prior_1[...], image_1[...], near_1[...], 3)
+    block = Blocks(places, scale, bias)
+    weights, losses = block(prior_1[...], image_1[...], near_1[...], 3)
     total = image_part[...] + over_first(weights, prior_1[...])
+    loss_send[...] = loss_part[...] + losses()
     image_send[...] = total.astype(image_send.dtype)
-    loss_send[...] = loss_part[...] + losses()
+
+    @pl.when(places[IS_FIRST] == 1)
+    def _():
+        prior_0 = edge[pl.ds(0, image_1.shape[0]), :]
+        weights, _ = block(prior_1[...], image_1[...], near_1[...], 3)
+        more, losses = block(prior_0, image_1[...], near_1[...], 2)
+        total = image_part[...] + over_first(weights, prior_1[...]) + over_first(more, prior_0)
+        loss_send[...] += losses()
+        image_send[...] = total.astype(image_send.dtype)
+
+
+def text_kernel(
+    places,
+    scale,
+    bias,
+    text_1,
+    after_1,
+    far_1,
+    text_part,
+    edge,
+    sent,
+    text_send,
+):
+    block = Blocks(places, scale, bias)
+    weights, _ = block(text_1[...], after_1[...], far_1[...], 1)
+    total = text_part[...] + by_image(weights, after_1[...])
+    text_send[...] = total.astype(text_send.dtype)
+
+    @pl.when(places[IS_LAST] == 1)
+    def _():
+        after_0, far_0 = read_after(edge)
+        weights, _ = block(text_1[...], after_1[...], far_1[...], 1)
+        more, _ = block(text_1[...], after_0, far_0, 1)
+        total = text_part[...] + by_image(weights, after_1[...]) + by_image(more, after_0)
+        text_send[...] = total.astype(text_send.dtype)
 
 
 def late_kernel(
@@ -163,28 +226,49 @@
     after_1,
     near_0,
     near_1,
+    far_1,
+    edge,
     sent,
     image_own,
     text_own,
     loss_own,
 ):
     block = Blocks(places, scale, bias)
+    rows = image_0.shape[0]
     weights, losses = block(text_0[...], image_0[...], near_0[...], 0)
     image_own[...] = over_first(weights, text_0[...])
     text_own[...] = by_image(weights, image_0[...])
     loss_own[...] = losses()
-    for k, text in ((1, text_1), (2, prior_0), (3, prior_1)):
-        weights, losses = block(text[...], image_0[...], near_0[...], k)
-        image_own[...] += over_first(weights, text[...])
+
+    def add_image(text, k):
+        weights, losses = block(text, image_0[...], near_0[...], k)
+        image_own[...] += over_first(weights, text)
         loss_own[...] += losses()
-    after = after_0[pl.ds(0, image_0.shape[0]), :]
-    for image, positive in (
-        (image_1[...], near_1[...]),
-        (after, read_far(after_0, 0)),
-        (after_1[...], read_far(after_0, 1)),
-    ):
+
+    def add_text(image, positive):
         weights, _ = block(text_0[...], image, positive, 0)
         text_own[...] += by_image(weights, image)
+
+    add_image(text_1[...], 1)
+    add_image(prior_1[...], 3)
+    add_text(image_1[...], near_1[...])
+    add_text(after_1[...], far_1[...])
+
+    @pl.when(places[IS_FIRST] == 0)
+    def _():
+        add_image(prior_0[...], 2)
+
+    @pl.when(places[IS_FIRST] == 1)
+    def _():
+        add_image(edge[pl.ds(0, rows), :], 2)
+
+    @pl.when(places[IS_LAST] == 0)
+    def _():
+        add_text(*read_after(after_0))
+
+    @pl.when(places[IS_LAST] == 1)
+    def _():
+        add_text(*read_after(edge))
 
 
 def cost(blocks):
@@ -212,12 +296,15 @@
     me = lax.axis_index("inner")
     whole = lax.axis_size("inner") * rows
     before = (group - 1 + count) % count
+    plane = count // PLANES
     places = jnp.stack(
         [
             group * whole + me * rows,
             group * whole + (3 - me) * rows,
             before * whole + me * rows,
             before * whole + (3 - me) * rows,
+            (group % plane == 0).astype(jnp.int32),
+            (group % plane == plane - 1).astype(jnp.int32),
         ]
     ).astype(jnp.int32)
     scalars = (places, logit_scale, logit_bias)
@@ -225,33 +312,41 @@
     long_shard = jax.ShapeDtypeStruct((rows + TAIL, width), jnp.bfloat16)
     real_shard = jax.ShapeDtypeStruct((rows, width), jnp.float32)
     line = jax.ShapeDtypeStruct((1, rows), jnp.float32)
+    int_line = jax.ShapeDtypeStruct((1, rows), jnp.int32)
     anywhere = [pl.BlockSpec(memory_space=pl.ANY)]
 
+    text_1 = lax.ppermute(texts, "inner", TEXT_PAIRS)
+    image_1 = lax.ppermute(images, "inner", IMAGE_PAIRS)
     near_0 = positive[None, :]
+    images_later, texts_later, edge = call(
+        hold_kernel,
+        "hold",
+        [SMEM] * 3 + [VMEM] * 3,
+        [long_shard, shard, long_shard],
+        1,
+    )(*scalars, images, texts, near_0)
     near_1 = lax.ppermute(near_0, "inner", IMAGE_PAIRS)
-    text_1 = gate(lax.ppermute(texts, "inner", TEXT_PAIRS))
-    image_1 = gate(lax.ppermute(images, "inner", IMAGE_PAIRS))
-    images_later, texts_later = call(
-        hold_kernel, "hold", [SMEM] * 3 + [VMEM] * 4, [long_shard, shard], 1
-    )(*scalars, images, texts, near_0, near_1)
-    prior_0 = from_behind(texts_later, 1)
-    after_0 = from_behind(images_later, -1)
-    after_1 = from_behind(image_1, -1)
-    prior_1 = from_behind(text_1, 1)
-
-    image_part, text_part, loss_part = call(
-        first_kernel, "first", [SMEM] * 3 + [VMEM] * 8, [real_shard, real_shard, line], 11
+    prior_0 = from_behind(texts_later, 1, within=True)
+    after_0 = from_behind(images_later, -1, within=True)
+    image_1 = gate(image_1, near_1)
+    after_1 = gate(from_behind(image_1, -1), blocks=ROOM)
+    prior_1 = gate(from_behind(text_1, 1), blocks=ROOM)
+    edge = over_edge(gate(edge, image_1, text_1))
+
+    image_part, text_part, loss_part, near_late = call(
+        first_kernel, "first", [SMEM] * 3 + [VMEM] * 8, [real_shard, real_shard, line, int_line], 11
     )(*scalars, images, image_1, texts, text_1, prior_0, after_0, near_0, near_1)
+    far_1 = from_behind(near_late, -1)
     image_send, loss_send = call(
-        image_kernel, "image", [SMEM] * 3 + [VMEM] * 5, [shard, line], 2
-    )(*scalars, image_1, prior_1, near_1, image_part, loss_part)
-    (text_send,) = call(text_kernel, "text", [SMEM] * 3 + [VMEM] * 4 + anywhere, [shard], 2)(
-        *scalars, text_1, after_0, after_1, text_part, image_send
-    )
+        image_kernel, "image", [SMEM] * 3 + [VMEM] * 6, [shard, line], 2
+    )(*scalars, image_1, prior_1, near_1, image_part, loss_part, edge)
+    (text_send,) = call(
+        text_kernel, "text", [SMEM] * 3 + [VMEM] * 5 + anywhere, [shard], 2
+    )(*scalars, text_1, after_1, far_1, text_part, edge, image_send)
     image_own, text_own, loss_own = call(
         late_kernel,
         "late",
-        [SMEM] * 3 + [VMEM] * 10 + anywhere,
+        [SMEM] * 3 + [VMEM] * 12 + anywhere,
         [real_shard, real_shard, line],
         15,
     )(
@@ -266,6 +361,8 @@
         after_1,
         near_0,
         near_1,
+        far_1,
+        edge,
         text_send,
     )
 

time: 139 us -> 144 us (1.036)
  the two profiles are of different devices: /device:TPU:127 before, /device:TPU:64 now
where the time goes in v6:
time: 144 us; the launch traced here: 143 us
  starting transfers between devices  70.5 us (49%)
  waiting for transfers between devices  37.4 us (26%)
  Pallas kernels  18.5 us (13%)
  local copies, waits for them, and re-layouts  12.1 us (8%)
  other arithmetic  2.52 us (2%)
  between operations  2.29 us (2%)
    ppermute x1, waiting for transfers between devices, per_device(): loss_back = lax.ppermute(loss_send, 'inner', IMAGE_PAIRS)  28 us
    ppermute x5, starting transfers between devices, from_behind(): return lax.ppermute(block, 'outer', pairs)  19.2 us
    unnamed x44, local copies, waits for them, and re-layouts  12 us
    ppermute x1, starting transfers between devices, per_device(): text_back = lax.ppermute(text_send, 'inner', TEXT_PAIRS)  11.4 us
    ppermute x1, waiting for transfers between devices, per_device(): near_1 = lax.ppermute(near_0, 'inner', IMAGE_PAIRS)  9.36 us
    ppermute x1, starting transfers between devices, over_edge(): return lax.ppermute(block, 'outer', pairs + [(j, i) for i, j in pairs])  9.13 us
    ppermute x1, starting transfers between devices, per_device(): image_1 = lax.ppermute(images, 'inner', IMAGE_PAIRS)  9.11 us
    ppermute x1, starting transfers between devices, per_device(): text_1 = lax.ppermute(texts, 'inner', TEXT_PAIRS)  8.21 us
  transfers between devices with their start and end apart: 12, of which 2 were waited for; matrix products, arithmetic and copies ran while one was open for 1% of the time, Pallas kernels for 12%

profile of v6, /device:TPU:64, one launch (start us, length us, event | category | flops | bytes accessed | tf_op | source)
XLA Modules:
  0.0 143.2 jit_solution(4984645205991712584)
XLA Ops:
  0.6 9.1 %collective-permute-start = (bf16[256,1152]{1,0:T(8,128)(2,1)}, bf16[256,1152]{1,0:T(8,128)(2,1)S(1)}, u32[]{:S(2)}, u32[]{:S(2)}) collective-permute-start(bf16[256,1152]{1,0:T(8,128)(2,1)} %image_0.3), channel_id=1, source_target_pairs={{0,1},{1,0},{2,3},{3,2},{4,5},{5,4},{6,7},{7,6},{8,9},{9,8},{10,11... | collective-permute-start | bytes 1769480 | tf_op jit(solution)/shard_map/ppermute | solution.py:319
  9.7 8.2 %collective-permute-start.2 = (bf16[256,1152]{1,0:T(8,128)(2,1)}, bf16[256,1152]{1,0:T(8,128)(2,1)S(1)}, u32[]{:S(2)}, u32[]{:S(2)}) collective-permute-start(bf16[256,1152]{1,0:T(8,128)(2,1)} %text_0.3), channel_id=1, source_target_pairs={{1,2},{2,1},{3,0},{0,3},{5,6},{6,5},{7,4},{4,7},{9,10},{10,9},{11,... | collective-permute-start | bytes 1769480 | tf_op jit(solution)/shard_map/ppermute | solution.py:318
  19.3 0.1 stack.35.places
  19.4 0.0 copy-start.12
  19.4 1.1 copy-done.12
  20.5 1.1 copy-done.15
  21.5 0.7 copy-done.20
  22.2 1.9 %hold.1 = (bf16[272,1152]{1,0:T(8,128)(2,1)}, bf16[256,1152]{1,0:T(8,128)(2,1)}, bf16[272,1152]{1,0:T(8,128)(2,1)}) custom-call(s32[6]{0:T(128)S(1)} %stack.35.places, f32[1]{0:T(128)} %copy.16.scale, f32[1]{0:T(128)S(6)} %copy.17.bias, bf16[256,1152]{1,0:T(8,128)(2,1)S(1)} %copy-done.12, bf16[256,1152]{1,0:T(8,128)(2,1)S(1)} %copy-done.15, ...), custom_call_target="tpu_custom_call" | custom-call | flops 150994944 | bytes 1048576 | tf_op jit(solution)/shard_map/hold/pallas_call | solution.py:321
  24.1 1.3 collective-permute-start.5
  25.4 3.9 %collective-permute-start.3 = (bf16[256,1152]{1,0:T(8,128)(2,1)}, bf16[256,1152]{1,0:T(8,128)(2,1)}, u32[]{:S(2)}, u32[]{:S(2)}) collective-permute-start(bf16[256,1152]{1,0:T(8,128)(2,1)} %get-tuple-element.15), channel_id=1, source_target_pairs={{0,4},{4,8},{8,12},{12,16},{16,20},{20,24},{24,28},{28,32},{32,36}... | collective-permute-start | bytes 1769480 | tf_op jit(solution)/shard_map/ppermute | solution.py:30
  29.3 4.6 %collective-permute-start.1 = (s32[1,256]{1,0:T(1,128)S(1)}, s32[1,256]{1,0:T(1,128)S(1)}, u32[]{:S(2)}, u32[]{:S(2)}) collective-permute-start(s32[1,256]{1,0:T(1,128)S(1)} %bitcast.12), channel_id=1, source_target_pairs={{0,1},{1,0},{2,3},{3,2},{4,5},{5,4},{6,7},{7,6},{8,9},{9,8},{10,11... | collective-permute-start | bytes 3080 | tf_op jit(solution)/shard_map/ppermute | solution.py:328
  33.9 9.4 %collective-permute-done.1.refs_1_.near_1 = s32[1,256]{1,0:T(1,128)S(1)} collective-permute-done((s32[1,256]{1,0:T(1,128)S(1)}, s32[1,256]{1,0:T(1,128)S(1)}, u32[]{:S(2)}, u32[]{:S(2)}) %collective-permute-start.1) | collective-permute-done | bytes 1056 | tf_op jit(solution)/shard_map/ppermute | solution.py:328
  43.3 0.0 collective-permute-done.refs_0_
  43.3 0.6 copy-done.18
  43.8 10.0 %collective-permute-start.6 = (bf16[256,1152]{1,0:T(8,128)(2,1)S(1)}, bf16[256,1152]{1,0:T(8,128)(2,1)S(1)}, u32[]{:S(2)}, u32[]{:S(2)}) collective-permute-start(bf16[256,1152]{1,0:T(8,128)(2,1)S(1)} %gate.4.image_1.refs_1_), channel_id=1, source_target_pairs={{4,0},{8,4},{12,8},{16,12},{20,16},{24,20},{28,24},{32,28},{36,32}... | collective-permute-start | bytes 1769480 | tf_op jit(solution)/shard_map/ppermute | solution.py:30
  53.9 0.0 collective-permute-done.2.text_1.refs_2_
  53.9 0.0 copy-start.3
  53.9 1.9 %collective-permute-start.4 = (bf16[256,1152]{1,0:T(8,128)(2,1)S(1)}, bf16[256,1152]{1,0:T(8,128)(2,1)}, u32[]{:S(2)}, u32[]{:S(2)}) collective-permute-start(bf16[256,1152]{1,0:T(8,128)(2,1)S(1)} %collective-permute-done.2.text_1.refs_2_), channel_id=1, source_target_pairs={{764,0},{0,4},{4,8},{8,12},{12,16},{16,20},{20,24},{24,28},{28,32}... | collective-permute-start | bytes 1769480 | tf_op jit(solution)/shard_map/ppermute | solution.py:30
  55.8 0.0 copy-done
  55.8 0.0 copy-done.3
  55.8 0.0 copy-start.19
  55.8 0.0 copy-start.21
  55.9 9.1 %collective-permute-start.8 = (bf16[272,1152]{1,0:T(8,128)(2,1)}, bf16[272,1152]{1,0:T(8,128)(2,1)S(1)}, u32[]{:S(2)}, u32[]{:S(2)}) collective-permute-start(bf16[272,1152]{1,0:T(8,128)(2,1)} %gate.7), channel_id=1, source_target_pairs={{252,256},{508,512},{764,0},{256,252},{512,508},{0,764},{253,257},... | collective-permute-start | bytes 1880072 | tf_op jit(solution)/shard_map/ppermute | solution.py:36
  65.0 0.0 collective-permute-done.3.prior_0
  65.0 0.0 collective-permute-done.5.after_0
  65.0 0.0 copy-done.19
  65.0 0.0 copy-done.21
  65.0 0.0 copy-start.1
  65.1 1.1 copy-done.1
  66.1 1.1 copy-done.4
  67.2 1.1 copy-done.13
  68.2 1.1 copy-done.16
  69.3 4.3 %first.1 = (f32[256,1152]{1,0:T(8,128)S(1)}, f32[256,1152]{1,0:T(8,128)S(1)}, f32[1,256]{1,0:T(1,128)S(1)}, s32[1,256]{1,0:T(1,128)S(1)}) custom-call(s32[6]{0:T(128)S(1)} %stack.35.places, f32[1]{0:T(128)} %copy.16.scale, f32[1]{0:T(128)S(6)} %copy.17.bias, bf16[256,1152]{1,0:T(8,128)(2,1)S(1)} %copy-done.13, bf16[256,1152]{1,0:T(8,128)(2,1)S(1)} %copy-done.1, ...), custom_call_target="tpu_custom_call" | custom-call | flops 1660944384 | bytes 1048576 | tf_op jit(solution)/shard_map/first/pallas_call | solution.py:336
  73.6 0.0 copy-start.6
  73.6 1.0 copy-done.6
  74.6 1.0 copy-done.8
  75.7 2.1 %collective-permute-start.7 = (s32[1,256]{1,0:T(1,128)S(1)}, s32[1,256]{1,0:T(1,128)S(1)}, u32[]{:S(2)}, u32[]{:S(2)}) collective-permute-start(s32[1,256]{1,0:T(1,128)S(1)} %get-tuple-element.17), channel_id=1, source_target_pairs={{4,0},{8,4},{12,8},{16,12},{20,16},{24,20},{28,24},{32,28},{36,32}... | collective-permute-start | bytes 3080 | tf_op jit(solution)/shard_map/ppermute | solution.py:30
  77.8 0.0 collective-permute-done.6.refs_0_
  77.8 0.0 copy-start.10
  77.8 0.8 copy-done.10
  78.6 0.0 collective-permute-done.4.refs_0_
  78.6 0.0 collective-permute-done.8.edge
  78.7 1.0 copy-done.2
  79.7 0.4 copy-done.9
  80.1 3.7 %image.1 = (bf16[256,1152]{1,0:T(8,128)(2,1)S(1)}, f32[1,256]{1,0:T(1,128)S(1)}) custom-call(s32[6]{0:T(128)S(1)} %stack.35.places, f32[1]{0:T(128)} %copy.16.scale, f32[1]{0:T(128)S(6)} %copy.17.bias, bf16[256,1152]{1,0:T(8,128)(2,1)S(1)} %copy-done.2, bf16[256,1152]{1,0:T(8,128)(2,1)} %gate.5.prior_1, s32[1,256]{1,0:T(1,128)S(1)} %copy-done.19, ...), custom_call_target="tpu_custom_call" | custom-call | flops 301989888 | bytes 1048576 | tf_op jit(solution)/shard_map/image/pallas_call | solution.py:340
  83.8 0.0 collective-permute-done.7.far_1
  83.8 0.0 copy-done.5
  83.8 0.0 copy-done.7
  83.8 0.0 copy-done.11
  83.8 0.0 copy-start.14
  83.8 0.0 copy-start.17
  83.8 1.5 %text.1.sent = bf16[256,1152]{1,0:T(8,128)(2,1)S(1)} custom-call(s32[6]{0:T(128)S(1)} %stack.35.places, f32[1]{0:T(128)} %copy.16.scale, f32[1]{0:T(128)S(6)} %copy.17.bias, bf16[256,1152]{1,0:T(8,128)(2,1)S(1)} %copy-done.5, bf16[256,1152]{1,0:T(8,128)(2,1)S(1)} %copy-done.11, s32[1,256]{1,0:T(1,128)S(1)} %collective-permute-done.7.far_1, ...), custom_call_target="tpu_custom_call" | custom-call | flops 301989888 | bytes 1048576 | tf_op jit(solution)/shard_map/text/pallas_call | solution.py:343
  85.4 11.4 %collective-permute-start.11 = (bf16[256,1152]{1,0:T(8,128)(2,1)S(1)}, bf16[256,1152]{1,0:T(8,128)(2,1)S(1)}, u32[]{:S(2)}, u32[]{:S(2)}) collective-permute-start(bf16[256,1152]{1,0:T(8,128)(2,1)S(1)} %text.1.sent), channel_id=1, source_target_pairs={{1,2},{2,1},{3,0},{0,3},{5,6},{6,5},{7,4},{4,7},{9,10},{10,9},{11,... | collective-permute-start | bytes 1769480 | tf_op jit(solution)/shard_map/ppermute | solution.py:370
  96.8 1.9 %collective-permute-start.10 = (bf16[256,1152]{1,0:T(8,128)(2,1)S(1)}, bf16[256,1152]{1,0:T(8,128)(2,1)S(1)}, u32[]{:S(2)}, u32[]{:S(2)}) collective-permute-start(bf16[256,1152]{1,0:T(8,128)(2,1)S(1)} %get-tuple-element.22.sent), channel_id=1, source_target_pairs={{0,1},{1,0},{2,3},{3,2},{4,5},{5,4},{6,7},{7,6},{8,9},{9,8},{10,11... | collective-permute-start | bytes 1769480 | tf_op jit(solution)/shard_map/ppermute | solution.py:369
  98.7 6.9 %collective-permute-start.9 = (f32[1,256]{1,0:T(1,128)S(1)}, f32[1,256]{1,0:T(1,128)S(1)}, u32[]{:S(2)}, u32[]{:S(2)}) collective-permute-start(f32[1,256]{1,0:T(1,128)S(1)} %get-tuple-element.24), channel_id=1, source_target_pairs={{0,1},{1,0},{2,3},{3,2},{4,5},{5,4},{6,7},{7,6},{8,9},{9,8},{10,11... | collective-permute-start | bytes 3080 | tf_op jit(solution)/shard_map/ppermute | solution.py:371
  105.7 0.0 copy-done.14
  105.7 0.0 copy-done.17
  105.7 7.1 %late.1 = (f32[256,1152]{1,0:T(8,128)S(1)}, f32[256,1152]{1,0:T(8,128)S(1)}, f32[1,256]{1,0:T(1,128)S(1)}) custom-call(s32[6]{0:T(128)S(1)} %stack.35.places, f32[1]{0:T(128)} %copy.16.scale, f32[1]{0:T(128)S(6)} %copy.17.bias, bf16[256,1152]{1,0:T(8,128)(2,1)S(1)} %copy-done.14, bf16[256,1152]{1,0:T(8,128)(2,1)S(1)} %copy-done.2, ...), custom_call_target="tpu_custom_call" | custom-call | flops 2264924160 | bytes 1048576 | tf_op jit(solution)/shard_map/late/pallas_call | solution.py:346
  112.8 28.0 %collective-permute-done.9 = f32[1,256]{1,0:T(1,128)S(1)} collective-permute-done((f32[1,256]{1,0:T(1,128)S(1)}, f32[1,256]{1,0:T(1,128)S(1)}, u32[]{:S(2)}, u32[]{:S(2)}) %collective-permute-start.9) | collective-permute-done | bytes 1056 | tf_op jit(solution)/shard_map/ppermute | solution.py:371
  140.7 0.6 add.42
  141.3 0.0 collective-permute-done.11
  141.3 1.0 multiply_convert_fusion
  142.3 0.0 collective-permute-done.10
  142.3 1.0 multiply_convert_fusion.1
  (17 shorter events, 0.0 us)
Async XLA Ops:
  0.6 42.6 %collective-permute-start = (bf16[256,1152]{1,0:T(8,128)(2,1)}, bf16[256,1152]{1,0:T(8,128)(2,1)S(1)}, u32[]{:S(2)}, u32[]{:S(2)}) collective-permute-start(bf16[256,1152]{1,0:T(8,128)(2,1)} %image_0.3), channel_id=1, source_target_pairs={{0,1},{1,0},{2,3},{3,2},{4,5},{5,4},{6,7},{7,6},{8,9},{9,8},{10,11... | collective-permute-start | bytes 1769480 | tf_op jit(solution)/shard_map/ppermute | solution.py:319
  9.7 44.1 %collective-permute-start.2 = (bf16[256,1152]{1,0:T(8,128)(2,1)}, bf16[256,1152]{1,0:T(8,128)(2,1)S(1)}, u32[]{:S(2)}, u32[]{:S(2)}) collective-permute-start(bf16[256,1152]{1,0:T(8,128)(2,1)} %text_0.3), channel_id=1, source_target_pairs={{1,2},{2,1},{3,0},{0,3},{5,6},{6,5},{7,4},{4,7},{9,10},{10,9},{11,... | collective-permute-start | bytes 1769480 | tf_op jit(solution)/shard_map/ppermute | solution.py:318
  19.4 1.1 copy-start.12
  20.4 1.1 copy-start.15
  21.5 0.7 copy-start.20
  24.1 40.9 %collective-permute-start.5 = (bf16[272,1152]{1,0:T(8,128)(2,1)}, bf16[272,1152]{1,0:T(8,128)(2,1)}, u32[]{:S(2)}, u32[]{:S(2)}) collective-permute-start(bf16[272,1152]{1,0:T(8,128)(2,1)} %get-tuple-element.16), channel_id=1, source_target_pairs={{4,0},{8,4},{12,8},{16,12},{20,16},{24,20},{28,24},{32,28},{36,32}... | collective-permute-start | bytes 1880072 | tf_op jit(solution)/shard_map/ppermute | solution.py:30
  25.4 39.6 %collective-permute-start.3 = (bf16[256,1152]{1,0:T(8,128)(2,1)}, bf16[256,1152]{1,0:T(8,128)(2,1)}, u32[]{:S(2)}, u32[]{:S(2)}) collective-permute-start(bf16[256,1152]{1,0:T(8,128)(2,1)} %get-tuple-element.15), channel_id=1, source_target_pairs={{0,4},{4,8},{8,12},{12,16},{16,20},{20,24},{24,28},{28,32},{32,36}... | collective-permute-start | bytes 1769480 | tf_op jit(solution)/shard_map/ppermute | solution.py:30
  29.3 14.0 %collective-permute-start.1 = (s32[1,256]{1,0:T(1,128)S(1)}, s32[1,256]{1,0:T(1,128)S(1)}, u32[]{:S(2)}, u32[]{:S(2)}) collective-permute-start(s32[1,256]{1,0:T(1,128)S(1)} %bitcast.12), channel_id=1, source_target_pairs={{0,1},{1,0},{2,3},{3,2},{4,5},{5,4},{6,7},{7,6},{8,9},{9,8},{10,11... | collective-permute-start | bytes 3080 | tf_op jit(solution)/shard_map/ppermute | solution.py:328
  43.3 0.6 copy-start.18
  43.8 12.0 %copy-start = (bf16[256,1152]{1,0:T(8,128)(2,1)}, bf16[256,1152]{1,0:T(8,128)(2,1)S(1)}, u32[]{:S(2)}) copy-start(bf16[256,1152]{1,0:T(8,128)(2,1)S(1)} %gate.4.image_1.refs_1_) | copy-start | bytes 1769476
  43.8 33.9 %collective-permute-start.6 = (bf16[256,1152]{1,0:T(8,128)(2,1)S(1)}, bf16[256,1152]{1,0:T(8,128)(2,1)S(1)}, u32[]{:S(2)}, u32[]{:S(2)}) collective-permute-start(bf16[256,1152]{1,0:T(8,128)(2,1)S(1)} %gate.4.image_1.refs_1_), channel_id=1, source_target_pairs={{4,0},{8,4},{12,8},{16,12},{20,16},{24,20},{28,24},{32,28},{36,32}... | collective-permute-start | bytes 1769480 | tf_op jit(solution)/shard_map/ppermute | solution.py:30
  53.9 2.0 %copy-start.3 = (bf16[256,1152]{1,0:T(8,128)(2,1)}, bf16[256,1152]{1,0:T(8,128)(2,1)S(1)}, u32[]{:S(2)}) copy-start(bf16[256,1152]{1,0:T(8,128)(2,1)S(1)} %collective-permute-done.2.text_1.refs_2_) | copy-start | bytes 1769476
  53.9 24.8 %collective-permute-start.4 = (bf16[256,1152]{1,0:T(8,128)(2,1)S(1)}, bf16[256,1152]{1,0:T(8,128)(2,1)}, u32[]{:S(2)}, u32[]{:S(2)}) collective-permute-start(bf16[256,1152]{1,0:T(8,128)(2,1)S(1)} %collective-permute-done.2.text_1.refs_2_), channel_id=1, source_target_pairs={{764,0},{0,4},{4,8},{8,12},{12,16},{16,20},{20,24},{24,28},{28,32}... | collective-permute-start | bytes 1769480 | tf_op jit(solution)/shard_map/ppermute | solution.py:30
  55.8 9.2 %copy-start.19 = (s32[1,256]{1,0:T(1,128)S(1)}, s32[1,256]{1,0:T(1,128)}, u32[]{:S(2)}) copy-start(s32[1,256]{1,0:T(1,128)} %copy-done.18) | copy-start | bytes 3076
  55.8 9.2 %copy-start.21 = (s32[256]{0:T(256)S(1)}, s32[256]{0:T(256)}, u32[]{:S(2)}) copy-start(s32[256]{0:T(256)} %param.7) | copy-start | bytes 3076
  55.9 22.8 %collective-permute-start.8 = (bf16[272,1152]{1,0:T(8,128)(2,1)}, bf16[272,1152]{1,0:T(8,128)(2,1)S(1)}, u32[]{:S(2)}, u32[]{:S(2)}) collective-permute-start(bf16[272,1152]{1,0:T(8,128)(2,1)} %gate.7), channel_id=1, source_target_pairs={{252,256},{508,512},{764,0},{256,252},{512,508},{0,764},{253,257},... | collective-permute-start | bytes 1880072 | tf_op jit(solution)/shard_map/ppermute | solution.py:36
  65.0 1.1 copy-start.1
  66.1 1.1 copy-start.4
  67.2 1.1 copy-start.13
  68.2 1.1 copy-start.16
  73.6 1.0 copy-start.6
  74.6 1.0 copy-start.8
  75.7 8.1 %collective-permute-start.7 = (s32[1,256]{1,0:T(1,128)S(1)}, s32[1,256]{1,0:T(1,128)S(1)}, u32[]{:S(2)}, u32[]{:S(2)}) collective-permute-start(s32[1,256]{1,0:T(1,128)S(1)} %get-tuple-element.17), channel_id=1, source_target_pairs={{4,0},{8,4},{12,8},{16,12},{20,16},{24,20},{28,24},{32,28},{36,32}... | collective-permute-start | bytes 3080 | tf_op jit(solution)/shard_map/ppermute | solution.py:30
  77.8 0.8 copy-start.10
  78.6 1.1 copy-start.2
  78.6 1.5 %copy-start.9 = (f32[256,1152]{1,0:T(8,128)S(1)}, f32[256,1152]{1,0:T(8,128)}, u32[]{:S(2)}) copy-start(f32[256,1152]{1,0:T(8,128)} %copy-done.8) | copy-start | bytes 3538948
  80.1 3.7 %copy-start.5 = (bf16[256,1152]{1,0:T(8,128)(2,1)S(1)}, bf16[256,1152]{1,0:T(8,128)(2,1)}, u32[]{:S(2)}) copy-start(bf16[256,1152]{1,0:T(8,128)(2,1)} %copy-done.3) | copy-start | bytes 1769476
  80.1 3.7 %copy-start.7 = (f32[256,1152]{1,0:T(8,128)S(1)}, f32[256,1152]{1,0:T(8,128)}, u32[]{:S(2)}) copy-start(f32[256,1152]{1,0:T(8,128)} %copy-done.6) | copy-start | bytes 3538948
  80.1 3.7 %copy-start.11 = (bf16[256,1152]{1,0:T(8,128)(2,1)S(1)}, bf16[256,1152]{1,0:T(8,128)(2,1)}, u32[]{:S(2)}) copy-start(bf16[256,1152]{1,0:T(8,128)(2,1)} %copy-done.10) | copy-start | bytes 1769476
  83.8 21.9 %copy-start.14 = (bf16[256,1152]{1,0:T(8,128)(2,1)S(1)}, bf16[256,1152]{1,0:T(8,128)(2,1)}, u32[]{:S(2)}) copy-start(bf16[256,1152]{1,0:T(8,128)(2,1)} %image_0.3) | copy-start | bytes 1769476
  83.8 21.9 %copy-start.17 = (bf16[256,1152]{1,0:T(8,128)(2,1)S(1)}, bf16[256,1152]{1,0:T(8,128)(2,1)}, u32[]{:S(2)}) copy-start(bf16[256,1152]{1,0:T(8,128)(2,1)} %text_0.3) | copy-start | bytes 1769476
  85.4 55.9 %collective-permute-start.11 = (bf16[256,1152]{1,0:T(8,128)(2,1)S(1)}, bf16[256,1152]{1,0:T(8,128)(2,1)S(1)}, u32[]{:S(2)}, u32[]{:S(2)}) collective-permute-start(bf16[256,1152]{1,0:T(8,128)(2,1)S(1)} %text.1.sent), channel_id=1, source_target_pairs={{1,2},{2,1},{3,0},{0,3},{5,6},{6,5},{7,4},{4,7},{9,10},{10,9},{11,... | collective-permute-start | bytes 1769480 | tf_op jit(solution)/shard_map/ppermute | solution.py:370
  96.8 45.5 %collective-permute-start.10 = (bf16[256,1152]{1,0:T(8,128)(2,1)S(1)}, bf16[256,1152]{1,0:T(8,128)(2,1)S(1)}, u32[]{:S(2)}, u32[]{:S(2)}) collective-permute-start(bf16[256,1152]{1,0:T(8,128)(2,1)S(1)} %get-tuple-element.22.sent), channel_id=1, source_target_pairs={{0,1},{1,0},{2,3},{3,2},{4,5},{5,4},{6,7},{7,6},{8,9},{9,8},{10,11... | collective-permute-start | bytes 1769480 | tf_op jit(solution)/shard_map/ppermute | solution.py:369
  98.7 42.0 %collective-permute-start.9 = (f32[1,256]{1,0:T(1,128)S(1)}, f32[1,256]{1,0:T(1,128)S(1)}, u32[]{:S(2)}, u32[]{:S(2)}) collective-permute-start(f32[1,256]{1,0:T(1,128)S(1)} %get-tuple-element.24), channel_id=1, source_target_pairs={{0,1},{1,0},{2,3},{3,2},{4,5},{5,4},{6,7},{7,6},{8,9},{9,8},{10,11... | collective-permute-start | bytes 3080 | tf_op jit(solution)/shard_map/ppermute | solution.py:371

commit v7 on v5

--- a/solution.py
+++ b/solution.py
@@ -13,8 +13,8 @@
 
 VMEM = pl.BlockSpec(memory_space=pltpu.VMEM)
 SMEM = pl.BlockSpec(memory_space=pltpu.SMEM)
-LIMIT = 40 * 1024 * 1024
-GATE_BLOCKS = 120
+LIMIT = 20 * 1024 * 1024
+LATE_BLOCKS = 19
 
 
 def from_behind(block, distance):
@@ -30,12 +30,12 @@
     return lax.dot_general(x, y, (((0,), (0,)), ((), ())), preferred_element_type=jnp.float32)
 
 
-def hold_kernel(places, scale, bias, images, texts, near_0, near_1, images_out, texts_out):
+def hold_kernel(places, scale, bias, images, texts, positive, images_out, texts_out):
     rows = images.shape[0]
     images_out[pl.ds(0, rows), :] = images[...]
     images_out[pl.ds(rows, TAIL), :] = jnp.zeros((TAIL, images.shape[1]), jnp.bfloat16)
-    digits = [(near[...] >> shift) & 255 for near in (near_0, near_1) for shift in SHIFTS]
-    digits = jnp.concatenate(digits + [jnp.zeros((TAIL - len(digits), rows), jnp.int32)])
+    digits = [(positive[...] >> shift) & 255 for shift in SHIFTS]
+    digits = jnp.concatenate(digits + [jnp.zeros((TAIL - len(SHIFTS), rows), jnp.int32)])
     images_out[pl.ds(rows, TAIL), pl.ds(0, rows)] = digits.astype(jnp.float32).astype(jnp.bfloat16)
     texts_out[...] = texts[...]
 
@@ -63,11 +63,11 @@
         return weights, loss
 
 
-def read_far(after, shard):
+def read_after(after):
     rows = after.shape[0] - TAIL
     digits = after[pl.ds(rows, TAIL), pl.ds(0, rows)].astype(jnp.float32).astype(jnp.int32)
-    first = shard * len(SHIFTS)
-    return sum(digits[first + k : first + k + 1, :] << shift for k, shift in enumerate(SHIFTS))
+    far = sum(digits[k : k + 1, :] << shift for k, shift in enumerate(SHIFTS))
+    return after[pl.ds(0, rows), :], far
 
 
 def by_image(weights, image):
@@ -87,7 +87,6 @@
         in_specs=[anywhere] * (1 + len(tokens)),
         out_specs=anywhere,
         input_output_aliases={0: 0},
-        cost_estimate=cost(GATE_BLOCKS),
     )(pltpu.with_memory_space_constraint(array, pltpu.VMEM), *tokens)
 
 
@@ -105,48 +104,45 @@
     near_1,
     image_part,
     text_part,
-    loss_part,
+    near_out,
 ):
+    near_out[...] = near_1[...]
     block = Blocks(places, scale, bias)
-    weights, losses = block(text_1[...], image_1[...], near_1[...], 1)
+    weights, _ = block(text_1[...], image_1[...], near_1[...], 1)
     image_part[...] = over_first(weights, text_1[...])
     text_part[...] = by_image(weights, image_1[...])
-    loss_part[...] = losses()
-    weights, losses = block(text_0[...], image_1[...], near_1[...], 0)
+    weights, _ = block(text_0[...], image_1[...], near_1[...], 0)
     image_part[...] += over_first(weights, text_0[...])
-    loss_part[...] += losses()
-    weights, losses = block(prior_0[...], image_1[...], near_1[...], 2)
-    image_part[...] += over_first(weights, prior_0[...])
-    loss_part[...] += losses()
     weights, _ = block(text_1[...], image_0[...], near_0[...], 1)
     text_part[...] += by_image(weights, image_0[...])
-    after = after_0[pl.ds(0, image_0.shape[0]), :]
-    weights, _ = block(text_1[...], after, read_far(after_0, 0), 1)
-    text_part[...] += by_image(weights, after)
-
-
-def text_kernel(places, scale, bias, text_1, after_0, after_1, text_part, sent, text_send):
-    weights, _ = Blocks(places, scale, bias)(text_1[...], after_1[...], read_far(after_0, 1), 1)
-    total = text_part[...] + by_image(weights, after_1[...])
-    text_send[...] = total.astype(text_send.dtype)
-
-
-def image_kernel(
+    weights, _ = block(prior_0[...], image_1[...], near_1[...], 2)
+    image_part[...] += over_first(weights, prior_0[...])
+    image, far = read_after(after_0)
+    weights, _ = block(text_1[...], image, far, 1)
+    text_part[...] += by_image(weights, image)
+
+
+def image_kernel(places, scale, bias, image_1, prior_1, near_1, image_part, image_send):
+    weights, _ = Blocks(places, scale, bias)(prior_1[...], image_1[...], near_1[...], 3)
+    total = image_part[...] + over_first(weights, prior_1[...])
+    image_send[...] = total.astype(image_send.dtype)
+
+
+def text_kernel(
     places,
     scale,
     bias,
-    image_1,
-    prior_1,
-    near_1,
-    image_part,
-    loss_part,
-    image_send,
-    loss_send,
+    text_1,
+    after_1,
+    far_1,
+    text_part,
+    sent,
+    text_send,
 ):
-    weights, losses = Blocks(places, scale, bias)(prior_1[...], image_1[...], near_1[...], 3)
-    total = image_part[...] + over_first(weights, prior_1[...])
-    image_send[...] = total.astype(image_send.dtype)
-    loss_send[...] = loss_part[...] + losses()
+    block = Blocks(places, scale, bias)
+    weights, _ = block(text_1[...], after_1[...], far_1[...], 1)
+    total = text_part[...] + by_image(weights, after_1[...])
+    text_send[...] = total.astype(text_send.dtype)
 
 
 def late_kernel(
@@ -163,28 +159,39 @@
     after_1,
     near_0,
     near_1,
+    far_1,
     sent,
     image_own,
     text_own,
     loss_own,
+    loss_send,
 ):
     block = Blocks(places, scale, bias)
+    rows = image_0.shape[0]
     weights, losses = block(text_0[...], image_0[...], near_0[...], 0)
     image_own[...] = over_first(weights, text_0[...])
     text_own[...] = by_image(weights, image_0[...])
     loss_own[...] = losses()
-    for k, text in ((1, text_1), (2, prior_0), (3, prior_1)):
-        weights, losses = block(text[...], image_0[...], near_0[...], k)
-        image_own[...] += over_first(weights, text[...])
+
+    def add_image(text, k):
+        weights, losses = block(text, image_0[...], near_0[...], k)
+        image_own[...] += over_first(weights, text)
         loss_own[...] += losses()
-    after = after_0[pl.ds(0, image_0.shape[0]), :]
-    for image, positive in (
-        (image_1[...], near_1[...]),
-        (after, read_far(after_0, 0)),
-        (after_1[...], read_far(after_0, 1)),
-    ):
+
+    def add_text(image, positive):
         weights, _ = block(text_0[...], image, positive, 0)
         text_own[...] += by_image(weights, image)
+
+    add_image(text_1[...], 1)
+    add_image(prior_1[...], 3)
+    add_text(image_1[...], near_1[...])
+    add_text(after_1[...], far_1[...])
+    add_image(prior_0[...], 2)
+    add_text(*read_after(after_0))
+    loss_send[...] = jnp.zeros_like(loss_send)
+    for k, text in enumerate((text_0, text_1, prior_0, prior_1)):
+        _, losses = block(text[...], image_1[...], near_1[...], k)
+        loss_send[...] += losses()
 
 
 def cost(blocks):
@@ -225,35 +232,43 @@
     long_shard = jax.ShapeDtypeStruct((rows + TAIL, width), jnp.bfloat16)
     real_shard = jax.ShapeDtypeStruct((rows, width), jnp.float32)
     line = jax.ShapeDtypeStruct((1, rows), jnp.float32)
+    int_line = jax.ShapeDtypeStruct((1, rows), jnp.int32)
     anywhere = [pl.BlockSpec(memory_space=pl.ANY)]
 
+    text_1 = lax.ppermute(texts, "inner", TEXT_PAIRS)
+    image_1 = lax.ppermute(images, "inner", IMAGE_PAIRS)
     near_0 = positive[None, :]
+    images_later, texts_later = call(
+        hold_kernel,
+        "hold",
+        [SMEM] * 3 + [VMEM] * 3,
+        [long_shard, shard],
+        1,
+    )(*scalars, images, texts, near_0)
     near_1 = lax.ppermute(near_0, "inner", IMAGE_PAIRS)
-    text_1 = gate(lax.ppermute(texts, "inner", TEXT_PAIRS))
-    image_1 = gate(lax.ppermute(images, "inner", IMAGE_PAIRS))
-    images_later, texts_later = call(
-        hold_kernel, "hold", [SMEM] * 3 + [VMEM] * 4, [long_shard, shard], 1
-    )(*scalars, images, texts, near_0, near_1)
     prior_0 = from_behind(texts_later, 1)
     after_0 = from_behind(images_later, -1)
+    image_1 = gate(image_1, near_1)
     after_1 = from_behind(image_1, -1)
+    text_1 = gate(text_1, near_1)
     prior_1 = from_behind(text_1, 1)
 
-    image_part, text_part, loss_part = call(
-        first_kernel, "first", [SMEM] * 3 + [VMEM] * 8, [real_shard, real_shard, line], 11
+    image_part, text_part, near_late = call(
+        first_kernel, "first", [SMEM] * 3 + [VMEM] * 8, [real_shard, real_shard, int_line], 11
     )(*scalars, images, image_1, texts, text_1, prior_0, after_0, near_0, near_1)
-    image_send, loss_send = call(
-        image_kernel, "image", [SMEM] * 3 + [VMEM] * 5, [shard, line], 2
-    )(*scalars, image_1, prior_1, near_1, image_part, loss_part)
-    (text_send,) = call(text_kernel, "text", [SMEM] * 3 + [VMEM] * 4 + anywhere, [shard], 2)(
-        *scalars, text_1, after_0, after_1, text_part, image_send
-    )
-    image_own, text_own, loss_own = call(
+    far_1 = from_behind(near_late, -1)
+    (image_send,) = call(
+        image_kernel, "image", [SMEM] * 3 + [VMEM] * 4, [shard], 2
+    )(*scalars, image_1, prior_1, near_1, image_part)
+    (text_send,) = call(
+        text_kernel, "text", [SMEM] * 3 + [VMEM] * 4 + anywhere, [shard], 2
+    )(*scalars, text_1, after_1, far_1, text_part, image_send)
+    image_own, text_own, loss_own, loss_send = call(
         late_kernel,
         "late",
-        [SMEM] * 3 + [VMEM] * 10 + anywhere,
-        [real_shard, real_shard, line],
-        15,
+        [SMEM] * 3 + [VMEM] * 11 + anywhere,
+        [real_shard, real_shard, line, line],
+        LATE_BLOCKS,
     )(
         *scalars,
         images,
@@ -266,7 +281,8 @@
         after_1,
         near_0,
         near_1,
-        text_send,
+        far_1,
+            text_send,
     )
 
     image_back = lax.ppermute(image_send, "inner", IMAGE_PAIRS)

time: 139 us -> 137 us (0.986)
  the two profiles are of different devices: /device:TPU:127 before, /device:TPU:1 now
where the time goes in v7:
time: 137 us; the launch traced here: 135 us
  starting transfers between devices  63 us (46%)
  waiting for transfers between devices  48.6 us (35%)
  Pallas kernels  15.5 us (11%)
  local copies, waits for them, and re-layouts  3.39 us (2%)
  other arithmetic  2.6 us (2%)
  between operations  2.17 us (2%)
    ppermute x1, waiting for transfers between devices, per_device(): loss_back = lax.ppermute(loss_send, 'inner', IMAGE_PAIRS)  28.5 us
    ppermute x5, starting transfers between devices, from_behind(): lax.ppermute(block, 'outer', [((i - distance) % count, i) for i in range(...  28 us
    ppermute x1, waiting for transfers between devices, per_device(): near_1 = lax.ppermute(near_0, 'inner', IMAGE_PAIRS)  20 us
    ppermute x1, starting transfers between devices, per_device(): text_1 = lax.ppermute(texts, 'inner', TEXT_PAIRS)  15.1 us
    pallas_call x1, Pallas kernels, per_device(): call(late_kernel, 'late', [SMEM] * 3 + [VMEM] * 11 + anywhere, [real_shar...  6.46 us
    ppermute x1, starting transfers between devices, per_device(): text_back = lax.ppermute(text_send, 'inner', TEXT_PAIRS)  5.76 us
    ppermute x1, starting transfers between devices, per_device(): near_1 = lax.ppermute(near_0, 'inner', IMAGE_PAIRS)  4.92 us
    pallas_call x1, Pallas kernels, per_device(): call(first_kernel, 'first', [SMEM] * 3 + [VMEM] * 8, [real_shard, real_sh...  4.28 us
  transfers between devices with their start and end apart: 11, of which 2 were waited for; matrix products, arithmetic and copies ran while one was open for 1% of the time, Pallas kernels for 10%

profile of v7, /device:TPU:1, one launch (start us, length us, event | category | flops | bytes accessed | tf_op | source)
XLA Modules:
  0.0 135.3 jit_solution(16182955282026838396)
XLA Ops:
  0.6 15.1 %collective-permute-start.2 = (bf16[256,1152]{1,0:T(8,128)(2,1)}, bf16[256,1152]{1,0:T(8,128)(2,1)S(1)}, u32[]{:S(2)}, u32[]{:S(2)}) collective-permute-start(bf16[256,1152]{1,0:T(8,128)(2,1)} %text_0.3), channel_id=1, source_target_pairs={{1,2},{2,1},{3,0},{0,3},{5,6},{6,5},{7,4},{4,7},{9,10},{10,9},{11,... | collective-permute-start | bytes 1769480 | tf_op jit(solution)/shard_map/ppermute | solution.py:238
  15.8 2.2 %collective-permute-start = (bf16[256,1152]{1,0:T(8,128)(2,1)}, bf16[256,1152]{1,0:T(8,128)(2,1)S(1)}, u32[]{:S(2)}, u32[]{:S(2)}) collective-permute-start(bf16[256,1152]{1,0:T(8,128)(2,1)} %image_0.3), channel_id=1, source_target_pairs={{0,1},{1,0},{2,3},{3,2},{4,5},{5,4},{6,7},{7,6},{8,9},{9,8},{10,11... | collective-permute-start | bytes 1769480 | tf_op jit(solution)/shard_map/ppermute | solution.py:239
  19.2 0.1 pad_add_fusion.places
  19.3 0.0 copy-start
  19.3 1.1 copy-done
  20.4 0.0 copy-start.2
  20.4 1.1 copy-done.2
  21.5 0.0 copy-start.6
  21.5 0.7 copy-done.6
  22.1 1.6 %hold.1 = (bf16[272,1152]{1,0:T(8,128)(2,1)}, bf16[256,1152]{1,0:T(8,128)(2,1)}) custom-call(s32[4]{0:T(128)S(1)} %pad_add_fusion.places, f32[1]{0:T(128)} %copy.12.scale, f32[1]{0:T(128)S(6)} %copy.13.bias, bf16[256,1152]{1,0:T(8,128)(2,1)S(1)} %copy-done, bf16[256,1152]{1,0:T(8,128)(2,1)S(1)} %copy-done.2, s32[1,256]{1,0:T(1,128)S(1)} %bitcast.9), custom_call_target="tpu_custom_call" | custom-call | flops 150994944 | bytes 1048576 | tf_op jit(solution)/shard_map/hold/pallas_call | solution.py:241
  23.8 3.1 %collective-permute-start.5 = (bf16[272,1152]{1,0:T(8,128)(2,1)}, bf16[272,1152]{1,0:T(8,128)(2,1)}, u32[]{:S(2)}, u32[]{:S(2)}) collective-permute-start(bf16[272,1152]{1,0:T(8,128)(2,1)} %get-tuple-element.13), channel_id=1, source_target_pairs={{4,0},{8,4},{12,8},{16,12},{20,16},{24,20},{28,24},{32,28},{36,32}... | collective-permute-start | bytes 1880072 | tf_op jit(solution)/shard_map/ppermute | solution.py:22
  26.9 0.0 copy-start.1
  26.9 0.0 copy-start.3
  26.9 0.0 copy-start.7
  27.0 3.2 %collective-permute-start.3 = (bf16[256,1152]{1,0:T(8,128)(2,1)}, bf16[256,1152]{1,0:T(8,128)(2,1)S(1)}, u32[]{:S(2)}, u32[]{:S(2)}) collective-permute-start(bf16[256,1152]{1,0:T(8,128)(2,1)} %get-tuple-element.12), channel_id=1, source_target_pairs={{764,0},{0,4},{4,8},{8,12},{12,16},{16,20},{20,24},{24,28},{28,32}... | collective-permute-start | bytes 1769480 | tf_op jit(solution)/shard_map/ppermute | solution.py:22
  30.2 4.9 %collective-permute-start.1 = (s32[1,256]{1,0:T(1,128)S(1)}, s32[1,256]{1,0:T(1,128)S(1)}, u32[]{:S(2)}, u32[]{:S(2)}) collective-permute-start(s32[1,256]{1,0:T(1,128)S(1)} %bitcast.10), channel_id=1, source_target_pairs={{0,1},{1,0},{2,3},{3,2},{4,5},{5,4},{6,7},{7,6},{8,9},{9,8},{10,11... | collective-permute-start | bytes 3080 | tf_op jit(solution)/shard_map/ppermute | solution.py:248
  35.1 20.0 %collective-permute-done.1.refs_1_.near_1 = s32[1,256]{1,0:T(1,128)S(1)} collective-permute-done((s32[1,256]{1,0:T(1,128)S(1)}, s32[1,256]{1,0:T(1,128)S(1)}, u32[]{:S(2)}, u32[]{:S(2)}) %collective-permute-start.1) | collective-permute-done | bytes 1056 | tf_op jit(solution)/shard_map/ppermute | solution.py:248
  55.1 0.0 copy-start.4
  55.1 0.0 collective-permute-done.2.refs_0_
  55.2 0.6 copy-done.4
  55.7 0.0 copy-start.5
  55.7 8.9 %collective-permute-start.4 = (bf16[256,1152]{1,0:T(8,128)(2,1)S(1)}, bf16[256,1152]{1,0:T(8,128)(2,1)S(1)}, u32[]{:S(2)}, u32[]{:S(2)}) collective-permute-start(bf16[256,1152]{1,0:T(8,128)(2,1)S(1)} %gate.3.text_1), channel_id=1, source_target_pairs={{764,0},{0,4},{4,8},{8,12},{12,16},{16,20},{20,24},{24,28},{28,32}... | collective-permute-start | bytes 1769480 | tf_op jit(solution)/shard_map/ppermute | solution.py:22
  64.7 0.0 collective-permute-done.refs_0_
  64.7 3.7 %collective-permute-start.6 = (bf16[256,1152]{1,0:T(8,128)(2,1)S(1)}, bf16[256,1152]{1,0:T(8,128)(2,1)S(1)}, u32[]{:S(2)}, u32[]{:S(2)}) collective-permute-start(bf16[256,1152]{1,0:T(8,128)(2,1)S(1)} %gate.2.image_1), channel_id=1, source_target_pairs={{4,0},{8,4},{12,8},{16,12},{20,16},{24,20},{28,24},{32,28},{36,32}... | collective-permute-start | bytes 1769480 | tf_op jit(solution)/shard_map/ppermute | solution.py:22
  68.4 0.0 collective-permute-done.3.prior_0
  68.4 0.0 collective-permute-done.5.after_0
  68.4 0.0 copy-done.1
  68.5 0.0 copy-done.3
  68.5 0.0 copy-done.7
  68.5 0.0 copy-done.5
  68.5 4.3 %first.1 = (f32[256,1152]{1,0:T(8,128)S(1)}, f32[256,1152]{1,0:T(8,128)S(1)}, s32[1,256]{1,0:T(1,128)S(1)}) custom-call(s32[4]{0:T(128)S(1)} %pad_add_fusion.places, f32[1]{0:T(128)} %copy.12.scale, f32[1]{0:T(128)S(6)} %copy.13.bias, bf16[256,1152]{1,0:T(8,128)(2,1)S(1)} %copy-done.1, bf16[256,1152]{1,0:T(8,128)(2,1)S(1)} %gate.2.image_1, ...), custom_call_target="tpu_custom_call" | custom-call | flops 1660944384 | bytes 1048576 | tf_op jit(solution)/shard_map/first/pallas_call | solution.py:256
  72.8 9.0 %collective-permute-start.7 = (s32[1,256]{1,0:T(1,128)S(1)}, s32[1,256]{1,0:T(1,128)S(1)}, u32[]{:S(2)}, u32[]{:S(2)}) collective-permute-start(s32[1,256]{1,0:T(1,128)S(1)} %get-tuple-element.14), channel_id=1, source_target_pairs={{4,0},{8,4},{12,8},{16,12},{20,16},{24,20},{28,24},{32,28},{36,32}... | collective-permute-start | bytes 3080 | tf_op jit(solution)/shard_map/ppermute | solution.py:22
  81.7 0.0 collective-permute-done.4.prior_1
  81.8 1.6 %image.1.sent = bf16[256,1152]{1,0:T(8,128)(2,1)S(1)} custom-call(s32[4]{0:T(128)S(1)} %pad_add_fusion.places, f32[1]{0:T(128)} %copy.12.scale, f32[1]{0:T(128)S(6)} %copy.13.bias, bf16[256,1152]{1,0:T(8,128)(2,1)S(1)} %gate.2.image_1, bf16[256,1152]{1,0:T(8,128)(2,1)S(1)} %collective-permute-done.4.prior_1, s32[1,256]{1,0:T(1,128)S(1)} %copy-done.5, ...), custom_call_target="tpu_custom_call" | custom-call | flops 301989888 | bytes 1048576 | tf_op jit(solution)/shard_map/image/pallas_call | solution.py:260
  83.4 0.0 collective-permute-done.7.far_1
  83.4 0.0 collective-permute-done.6.after_1
  83.4 1.5 %text.1.sent = bf16[256,1152]{1,0:T(8,128)(2,1)S(1)} custom-call(s32[4]{0:T(128)S(1)} %pad_add_fusion.places, f32[1]{0:T(128)} %copy.12.scale, f32[1]{0:T(128)S(6)} %copy.13.bias, bf16[256,1152]{1,0:T(8,128)(2,1)S(1)} %gate.3.text_1, bf16[256,1152]{1,0:T(8,128)(2,1)S(1)} %collective-permute-done.6.after_1, s32[1,256]{1,0:T(1,128)S(1)} %collective-permute-done.7.far_1, ...), custom_call_target="tpu_custom_call" | custom-call | flops 301989888 | bytes 1048576 | tf_op jit(solution)/shard_map/text/pallas_call | solution.py:263
  84.9 5.8 %collective-permute-start.10 = (bf16[256,1152]{1,0:T(8,128)(2,1)S(1)}, bf16[256,1152]{1,0:T(8,128)(2,1)S(1)}, u32[]{:S(2)}, u32[]{:S(2)}) collective-permute-start(bf16[256,1152]{1,0:T(8,128)(2,1)S(1)} %text.1.sent), channel_id=1, source_target_pairs={{1,2},{2,1},{3,0},{0,3},{5,6},{6,5},{7,4},{4,7},{9,10},{10,9},{11,... | collective-permute-start | bytes 1769480 | tf_op jit(solution)/shard_map/ppermute | solution.py:289
  90.7 3.0 %collective-permute-start.9 = (bf16[256,1152]{1,0:T(8,128)(2,1)S(1)}, bf16[256,1152]{1,0:T(8,128)(2,1)S(1)}, u32[]{:S(2)}, u32[]{:S(2)}) collective-permute-start(bf16[256,1152]{1,0:T(8,128)(2,1)S(1)} %image.1.sent), channel_id=1, source_target_pairs={{0,1},{1,0},{2,3},{3,2},{4,5},{5,4},{6,7},{7,6},{8,9},{9,8},{10,11... | collective-permute-start | bytes 1769480 | tf_op jit(solution)/shard_map/ppermute | solution.py:288
  93.7 6.5 %late.1 = (f32[256,1152]{1,0:T(8,128)S(1)}, f32[256,1152]{1,0:T(8,128)S(1)}, f32[1,256]{1,0:T(1,128)S(1)}, f32[1,256]{1,0:T(1,128)S(1)}) custom-call(s32[4]{0:T(128)S(1)} %pad_add_fusion.places, f32[1]{0:T(128)} %copy.12.scale, f32[1]{0:T(128)S(6)} %copy.13.bias, bf16[256,1152]{1,0:T(8,128)(2,1)S(1)} %copy-done.1, bf16[256,1152]{1,0:T(8,128)(2,1)S(1)} %gate.2.image_1, ...), custom_call_target="tpu_custom_call" | custom-call | flops 2868903936 | bytes 1048576 | tf_op jit(solution)/shard_map/late/pallas_call | solution.py:266
  100.1 4.1 %collective-permute-start.8 = (f32[1,256]{1,0:T(1,128)S(1)}, f32[1,256]{1,0:T(1,128)S(1)}, u32[]{:S(2)}, u32[]{:S(2)}) collective-permute-start(f32[1,256]{1,0:T(1,128)S(1)} %get-tuple-element.18), channel_id=1, source_target_pairs={{0,1},{1,0},{2,3},{3,2},{4,5},{5,4},{6,7},{7,6},{8,9},{9,8},{10,11... | collective-permute-start | bytes 3080 | tf_op jit(solution)/shard_map/ppermute | solution.py:290
  104.2 28.5 %collective-permute-done.8 = f32[1,256]{1,0:T(1,128)S(1)} collective-permute-done((f32[1,256]{1,0:T(1,128)S(1)}, f32[1,256]{1,0:T(1,128)S(1)}, u32[]{:S(2)}, u32[]{:S(2)}) %collective-permute-start.8) | collective-permute-done | bytes 1056 | tf_op jit(solution)/shard_map/ppermute | solution.py:290
  132.8 0.6 add.37
  133.3 0.0 collective-permute-done.10
  133.3 1.0 multiply_convert_fusion
  134.3 0.0 collective-permute-done.9
  134.3 1.0 multiply_convert_fusion.1
  (2 shorter events, 0.0 us)
Async XLA Ops:
  0.6 54.5 %collective-permute-start.2 = (bf16[256,1152]{1,0:T(8,128)(2,1)}, bf16[256,1152]{1,0:T(8,128)(2,1)S(1)}, u32[]{:S(2)}, u32[]{:S(2)}) collective-permute-start(bf16[256,1152]{1,0:T(8,128)(2,1)} %text_0.3), channel_id=1, source_target_pairs={{1,2},{2,1},{3,0},{0,3},{5,6},{6,5},{7,4},{4,7},{9,10},{10,9},{11,... | collective-permute-start | bytes 1769480 | tf_op jit(solution)/shard_map/ppermute | solution.py:238
  15.8 48.9 %collective-permute-start = (bf16[256,1152]{1,0:T(8,128)(2,1)}, bf16[256,1152]{1,0:T(8,128)(2,1)S(1)}, u32[]{:S(2)}, u32[]{:S(2)}) collective-permute-start(bf16[256,1152]{1,0:T(8,128)(2,1)} %image_0.3), channel_id=1, source_target_pairs={{0,1},{1,0},{2,3},{3,2},{4,5},{5,4},{6,7},{7,6},{8,9},{9,8},{10,11... | collective-permute-start | bytes 1769480 | tf_op jit(solution)/shard_map/ppermute | solution.py:239
  19.3 1.1 copy-start
  20.4 1.1 copy-start.2
  21.5 0.7 copy-start.6
  23.8 44.7 %collective-permute-start.5 = (bf16[272,1152]{1,0:T(8,128)(2,1)}, bf16[272,1152]{1,0:T(8,128)(2,1)}, u32[]{:S(2)}, u32[]{:S(2)}) collective-permute-start(bf16[272,1152]{1,0:T(8,128)(2,1)} %get-tuple-element.13), channel_id=1, source_target_pairs={{4,0},{8,4},{12,8},{16,12},{20,16},{24,20},{28,24},{32,28},{36,32}... | collective-permute-start | bytes 1880072 | tf_op jit(solution)/shard_map/ppermute | solution.py:22
  26.9 41.5 %copy-start.1 = (bf16[256,1152]{1,0:T(8,128)(2,1)S(1)}, bf16[256,1152]{1,0:T(8,128)(2,1)}, u32[]{:S(2)}) copy-start(bf16[256,1152]{1,0:T(8,128)(2,1)} %image_0.3) | copy-start | bytes 1769476
  26.9 41.5 %copy-start.3 = (bf16[256,1152]{1,0:T(8,128)(2,1)S(1)}, bf16[256,1152]{1,0:T(8,128)(2,1)}, u32[]{:S(2)}) copy-start(bf16[256,1152]{1,0:T(8,128)(2,1)} %text_0.3) | copy-start | bytes 1769476
  26.9 41.5 %copy-start.7 = (s32[256]{0:T(256)S(1)}, s32[256]{0:T(256)}, u32[]{:S(2)}) copy-start(s32[256]{0:T(256)} %param.7) | copy-start | bytes 3076
  27.0 41.5 %collective-permute-start.3 = (bf16[256,1152]{1,0:T(8,128)(2,1)}, bf16[256,1152]{1,0:T(8,128)(2,1)S(1)}, u32[]{:S(2)}, u32[]{:S(2)}) collective-permute-start(bf16[256,1152]{1,0:T(8,128)(2,1)} %get-tuple-element.12), channel_id=1, source_target_pairs={{764,0},{0,4},{4,8},{8,12},{12,16},{16,20},{20,24},{24,28},{28,32}... | collective-permute-start | bytes 1769480 | tf_op jit(solution)/shard_map/ppermute | solution.py:22
  30.2 24.9 %collective-permute-start.1 = (s32[1,256]{1,0:T(1,128)S(1)}, s32[1,256]{1,0:T(1,128)S(1)}, u32[]{:S(2)}, u32[]{:S(2)}) collective-permute-start(s32[1,256]{1,0:T(1,128)S(1)} %bitcast.10), channel_id=1, source_target_pairs={{0,1},{1,0},{2,3},{3,2},{4,5},{5,4},{6,7},{7,6},{8,9},{9,8},{10,11... | collective-permute-start | bytes 3080 | tf_op jit(solution)/shard_map/ppermute | solution.py:248
  55.1 0.6 copy-start.4
  55.7 12.8 %copy-start.5 = (s32[1,256]{1,0:T(1,128)S(1)}, s32[1,256]{1,0:T(1,128)}, u32[]{:S(2)}) copy-start(s32[1,256]{1,0:T(1,128)} %copy-done.4) | copy-start | bytes 3076
  55.7 26.0 %collective-permute-start.4 = (bf16[256,1152]{1,0:T(8,128)(2,1)S(1)}, bf16[256,1152]{1,0:T(8,128)(2,1)S(1)}, u32[]{:S(2)}, u32[]{:S(2)}) collective-permute-start(bf16[256,1152]{1,0:T(8,128)(2,1)S(1)} %gate.3.text_1), channel_id=1, source_target_pairs={{764,0},{0,4},{4,8},{8,12},{12,16},{16,20},{20,24},{24,28},{28,32}... | collective-permute-start | bytes 1769480 | tf_op jit(solution)/shard_map/ppermute | solution.py:22
  64.7 18.7 %collective-permute-start.6 = (bf16[256,1152]{1,0:T(8,128)(2,1)S(1)}, bf16[256,1152]{1,0:T(8,128)(2,1)S(1)}, u32[]{:S(2)}, u32[]{:S(2)}) collective-permute-start(bf16[256,1152]{1,0:T(8,128)(2,1)S(1)} %gate.2.image_1), channel_id=1, source_target_pairs={{4,0},{8,4},{12,8},{16,12},{20,16},{24,20},{28,24},{32,28},{36,32}... | collective-permute-start | bytes 1769480 | tf_op jit(solution)/shard_map/ppermute | solution.py:22
  72.8 10.6 %collective-permute-start.7 = (s32[1,256]{1,0:T(1,128)S(1)}, s32[1,256]{1,0:T(1,128)S(1)}, u32[]{:S(2)}, u32[]{:S(2)}) collective-permute-start(s32[1,256]{1,0:T(1,128)S(1)} %get-tuple-element.14), channel_id=1, source_target_pairs={{4,0},{8,4},{12,8},{16,12},{20,16},{24,20},{28,24},{32,28},{36,32}... | collective-permute-start | bytes 3080 | tf_op jit(solution)/shard_map/ppermute | solution.py:22
  84.9 48.4 %collective-permute-start.10 = (bf16[256,1152]{1,0:T(8,128)(2,1)S(1)}, bf16[256,1152]{1,0:T(8,128)(2,1)S(1)}, u32[]{:S(2)}, u32[]{:S(2)}) collective-permute-start(bf16[256,1152]{1,0:T(8,128)(2,1)S(1)} %text.1.sent), channel_id=1, source_target_pairs={{1,2},{2,1},{3,0},{0,3},{5,6},{6,5},{7,4},{4,7},{9,10},{10,9},{11,... | collective-permute-start | bytes 1769480 | tf_op jit(solution)/shard_map/ppermute | solution.py:289
  90.7 43.6 %collective-permute-start.9 = (bf16[256,1152]{1,0:T(8,128)(2,1)S(1)}, bf16[256,1152]{1,0:T(8,128)(2,1)S(1)}, u32[]{:S(2)}, u32[]{:S(2)}) collective-permute-start(bf16[256,1152]{1,0:T(8,128)(2,1)S(1)} %image.1.sent), channel_id=1, source_target_pairs={{0,1},{1,0},{2,3},{3,2},{4,5},{5,4},{6,7},{7,6},{8,9},{9,8},{10,11... | collective-permute-start | bytes 1769480 | tf_op jit(solution)/shard_map/ppermute | solution.py:288
  100.1 32.6 %collective-permute-start.8 = (f32[1,256]{1,0:T(1,128)S(1)}, f32[1,256]{1,0:T(1,128)S(1)}, u32[]{:S(2)}, u32[]{:S(2)}) collective-permute-start(f32[1,256]{1,0:T(1,128)S(1)} %get-tuple-element.18), channel_id=1, source_target_pairs={{0,1},{1,0},{2,3},{3,2},{4,5},{5,4},{6,7},{7,6},{8,9},{9,8},{10,11... | collective-permute-start | bytes 3080 | tf_op jit(solution)/shard_map/ppermute | solution.py:290

commit v8 on v7

--- a/solution.py
+++ b/solution.py
@@ -87,6 +87,7 @@
         in_specs=[anywhere] * (1 + len(tokens)),
         out_specs=anywhere,
         input_output_aliases={0: 0},
+        cost_estimate=cost(0),
     )(pltpu.with_memory_space_constraint(array, pltpu.VMEM), *tokens)
 
 
@@ -122,24 +123,25 @@
     text_part[...] += by_image(weights, image)
 
 
-def image_kernel(places, scale, bias, image_1, prior_1, near_1, image_part, image_send):
-    weights, _ = Blocks(places, scale, bias)(prior_1[...], image_1[...], near_1[...], 3)
-    total = image_part[...] + over_first(weights, prior_1[...])
-    image_send[...] = total.astype(image_send.dtype)
-
-
-def text_kernel(
+def second_kernel(
     places,
     scale,
     bias,
+    image_1,
     text_1,
+    prior_1,
     after_1,
+    near_1,
     far_1,
+    image_part,
     text_part,
-    sent,
+    image_send,
     text_send,
 ):
     block = Blocks(places, scale, bias)
+    weights, _ = block(prior_1[...], image_1[...], near_1[...], 3)
+    total = image_part[...] + over_first(weights, prior_1[...])
+    image_send[...] = total.astype(image_send.dtype)
     weights, _ = block(text_1[...], after_1[...], far_1[...], 1)
     total = text_part[...] + by_image(weights, after_1[...])
     text_send[...] = total.astype(text_send.dtype)
@@ -257,12 +259,9 @@
         first_kernel, "first", [SMEM] * 3 + [VMEM] * 8, [real_shard, real_shard, int_line], 11
     )(*scalars, images, image_1, texts, text_1, prior_0, after_0, near_0, near_1)
     far_1 = from_behind(near_late, -1)
-    (image_send,) = call(
-        image_kernel, "image", [SMEM] * 3 + [VMEM] * 4, [shard], 2
-    )(*scalars, image_1, prior_1, near_1, image_part)
-    (text_send,) = call(
-        text_kernel, "text", [SMEM] * 3 + [VMEM] * 4 + anywhere, [shard], 2
-    )(*scalars, text_1, after_1, far_1, text_part, image_send)
+    image_send, text_send = call(
+        second_kernel, "second", [SMEM] * 3 + [VMEM] * 8, [shard, shard], 4
+    )(*scalars, image_1, text_1, prior_1, after_1, near_1, far_1, image_part, text_part)
     image_own, text_own, loss_own, loss_send = call(
         late_kernel,
         "late",

time: 137 us -> 130 us (0.949)
  waiting for transfers between devices: 48.6 us -> 37 us
  starting transfers between devices: 63 us -> 68.6 us
    ppermute x1, waiting for transfers between devices: 20 us -> 9.54 us  [per_device(): near_1 = lax.ppermute(near_0, 'inner', IMAGE_PAIRS)]
    ppermute x5, starting transfers between devices: 28 us -> 35.7 us  [from_behind(): lax.ppermute(block, 'outer', [((i - distance) % count, i) for i in range(...]
    ppermute x1, starting transfers between devices: 2.16 us -> 8.45 us  [per_device(): image_1 = lax.ppermute(images, 'inner', IMAGE_PAIRS)]
    ppermute x1, starting transfers between devices: 15.1 us -> 9.43 us  [per_device(): text_1 = lax.ppermute(texts, 'inner', TEXT_PAIRS)]
    ppermute x1, waiting for transfers between devices: 28.5 us -> 26.6 us  [per_device(): loss_back = lax.ppermute(loss_send, 'inner', IMAGE_PAIRS)]
    pallas_call x2 -> x1, Pallas kernels: 3.12 us -> 2.39 us  [per_device(): call(second_kernel, 'second', [SMEM] * 3 + [VMEM] * 8, [shard, shard], 4)]
  transfers between devices with their start and end apart: 11 -> 11, of which waited for: 2 -> 3; matrix products, arithmetic and copies ran while one was open for 1% -> 1% of each run, Pallas kernels for 10% -> 10%
where the time goes in v8:
time: 130 us; the launch traced here: 129 us
  starting transfers between devices  68.6 us (53%)
  waiting for transfers between devices  37 us (28%)
  Pallas kernels  14.8 us (11%)
  local copies, waits for them, and re-layouts  3.39 us (3%)
  other arithmetic  2.6 us (2%)
  between operations  2.14 us (2%)
    ppermute x5, starting transfers between devices, from_behind(): lax.ppermute(block, 'outer', [((i - distance) % count, i) for i in range(...  35.7 us
    ppermute x1, waiting for transfers between devices, per_device(): loss_back = lax.ppermute(loss_send, 'inner', IMAGE_PAIRS)  26.6 us
    ppermute x1, waiting for transfers between devices, per_device(): near_1 = lax.ppermute(near_0, 'inner', IMAGE_PAIRS)  9.54 us
    ppermute x1, starting transfers between devices, per_device(): text_1 = lax.ppermute(texts, 'inner', TEXT_PAIRS)  9.43 us
    ppermute x1, starting transfers between devices, per_device(): image_1 = lax.ppermute(images, 'inner', IMAGE_PAIRS)  8.45 us
    pallas_call x1, Pallas kernels, per_device(): call(late_kernel, 'late', [SMEM] * 3 + [VMEM] * 11 + anywhere, [real_shar...  6.46 us
    ppermute x1, starting transfers between devices, per_device(): near_1 = lax.ppermute(near_0, 'inner', IMAGE_PAIRS)  4.92 us
    ppermute x1, starting transfers between devices, per_device(): text_back = lax.ppermute(text_send, 'inner', TEXT_PAIRS)  4.91 us
  transfers between devices with their start and end apart: 11, of which 3 were waited for; matrix products, arithmetic and copies ran while one was open for 1% of the time, Pallas kernels for 10%

profile of v8, /device:TPU:1, one launch (start us, length us, event | category | flops | bytes accessed | tf_op | source)
XLA Modules:
  0.0 128.5 jit_solution(2776497800632573705)
XLA Ops:
  0.6 8.4 %collective-permute-start = (bf16[256,1152]{1,0:T(8,128)(2,1)}, bf16[256,1152]{1,0:T(8,128)(2,1)S(1)}, u32[]{:S(2)}, u32[]{:S(2)}) collective-permute-start(bf16[256,1152]{1,0:T(8,128)(2,1)} %image_0.3), channel_id=1, source_target_pairs={{0,1},{1,0},{2,3},{3,2},{4,5},{5,4},{6,7},{7,6},{8,9},{9,8},{10,11... | collective-permute-start | bytes 1769480 | tf_op jit(solution)/shard_map/ppermute | solution.py:241
  9.1 9.4 %collective-permute-start.2 = (bf16[256,1152]{1,0:T(8,128)(2,1)}, bf16[256,1152]{1,0:T(8,128)(2,1)S(1)}, u32[]{:S(2)}, u32[]{:S(2)}) collective-permute-start(bf16[256,1152]{1,0:T(8,128)(2,1)} %text_0.3), channel_id=1, source_target_pairs={{1,2},{2,1},{3,0},{0,3},{5,6},{6,5},{7,4},{4,7},{9,10},{10,9},{11,... | collective-permute-start | bytes 1769480 | tf_op jit(solution)/shard_map/ppermute | solution.py:240
  19.8 0.1 pad_add_fusion.places
  19.9 0.0 copy-start
  19.9 1.1 copy-done
  21.0 0.0 copy-start.2
  21.0 1.1 copy-done.2
  22.1 0.0 copy-start.6
  22.1 0.7 copy-done.6
  22.7 1.6 %hold.1 = (bf16[272,1152]{1,0:T(8,128)(2,1)}, bf16[256,1152]{1,0:T(8,128)(2,1)}) custom-call(s32[4]{0:T(128)S(1)} %pad_add_fusion.places, f32[1]{0:T(128)} %copy.12.scale, f32[1]{0:T(128)S(6)} %copy.13.bias, bf16[256,1152]{1,0:T(8,128)(2,1)S(1)} %copy-done, bf16[256,1152]{1,0:T(8,128)(2,1)S(1)} %copy-done.2, s32[1,256]{1,0:T(1,128)S(1)} %bitcast.9), custom_call_target="tpu_custom_call" | custom-call | flops 150994944 | bytes 1048576 | tf_op jit(solution)/shard_map/hold/pallas_call | solution.py:243
  24.4 3.1 %collective-permute-start.5 = (bf16[272,1152]{1,0:T(8,128)(2,1)}, bf16[272,1152]{1,0:T(8,128)(2,1)}, u32[]{:S(2)}, u32[]{:S(2)}) collective-permute-start(bf16[272,1152]{1,0:T(8,128)(2,1)} %get-tuple-element.15), channel_id=1, source_target_pairs={{4,0},{8,4},{12,8},{16,12},{20,16},{24,20},{28,24},{32,28},{36,32}... | collective-permute-start | bytes 1880072 | tf_op jit(solution)/shard_map/ppermute | solution.py:22
  27.5 0.0 copy-start.1
  27.5 0.0 copy-start.3
  27.5 0.0 copy-start.7
  27.6 3.2 %collective-permute-start.3 = (bf16[256,1152]{1,0:T(8,128)(2,1)}, bf16[256,1152]{1,0:T(8,128)(2,1)S(1)}, u32[]{:S(2)}, u32[]{:S(2)}) collective-permute-start(bf16[256,1152]{1,0:T(8,128)(2,1)} %get-tuple-element.14), channel_id=1, source_target_pairs={{764,0},{0,4},{4,8},{8,12},{12,16},{16,20},{20,24},{24,28},{28,32}... | collective-permute-start | bytes 1769480 | tf_op jit(solution)/shard_map/ppermute | solution.py:22
  30.8 4.9 %collective-permute-start.1 = (s32[1,256]{1,0:T(1,128)S(1)}, s32[1,256]{1,0:T(1,128)S(1)}, u32[]{:S(2)}, u32[]{:S(2)}) collective-permute-start(s32[1,256]{1,0:T(1,128)S(1)} %bitcast.10), channel_id=1, source_target_pairs={{0,1},{1,0},{2,3},{3,2},{4,5},{5,4},{6,7},{7,6},{8,9},{9,8},{10,11... | collective-permute-start | bytes 3080 | tf_op jit(solution)/shard_map/ppermute | solution.py:250
  35.7 9.5 %collective-permute-done.1.refs_1_.near_1 = s32[1,256]{1,0:T(1,128)S(1)} collective-permute-done((s32[1,256]{1,0:T(1,128)S(1)}, s32[1,256]{1,0:T(1,128)S(1)}, u32[]{:S(2)}, u32[]{:S(2)}) %collective-permute-start.1) | collective-permute-done | bytes 1056 | tf_op jit(solution)/shard_map/ppermute | solution.py:250
  45.3 0.0 copy-start.4
  45.3 0.0 collective-permute-done.refs_0_
  45.3 0.6 copy-done.4
  45.8 0.0 copy-start.5
  45.8 16.9 %collective-permute-start.6 = (bf16[256,1152]{1,0:T(8,128)(2,1)S(1)}, bf16[256,1152]{1,0:T(8,128)(2,1)S(1)}, u32[]{:S(2)}, u32[]{:S(2)}) collective-permute-start(bf16[256,1152]{1,0:T(8,128)(2,1)S(1)} %gate.2.image_1), channel_id=1, source_target_pairs={{4,0},{8,4},{12,8},{16,12},{20,16},{24,20},{28,24},{32,28},{36,32}... | collective-permute-start | bytes 1769480 | tf_op jit(solution)/shard_map/ppermute | solution.py:22
  62.8 0.0 collective-permute-done.2.refs_0_
  62.8 1.9 %collective-permute-start.4 = (bf16[256,1152]{1,0:T(8,128)(2,1)S(1)}, bf16[256,1152]{1,0:T(8,128)(2,1)S(1)}, u32[]{:S(2)}, u32[]{:S(2)}) collective-permute-start(bf16[256,1152]{1,0:T(8,128)(2,1)S(1)} %gate.3.text_1), channel_id=1, source_target_pairs={{764,0},{0,4},{4,8},{8,12},{12,16},{16,20},{20,24},{24,28},{28,32}... | collective-permute-start | bytes 1769480 | tf_op jit(solution)/shard_map/ppermute | solution.py:22
  64.7 0.0 collective-permute-done.3.prior_0
  64.7 0.0 collective-permute-done.5.after_0
  64.7 0.0 copy-done.1
  64.7 0.0 copy-done.3
  64.7 0.0 copy-done.7
  64.8 0.0 copy-done.5
  64.8 4.3 %first.1 = (f32[256,1152]{1,0:T(8,128)S(1)}, f32[256,1152]{1,0:T(8,128)S(1)}, s32[1,256]{1,0:T(1,128)S(1)}) custom-call(s32[4]{0:T(128)S(1)} %pad_add_fusion.places, f32[1]{0:T(128)} %copy.12.scale, f32[1]{0:T(128)S(6)} %copy.13.bias, bf16[256,1152]{1,0:T(8,128)(2,1)S(1)} %copy-done.1, bf16[256,1152]{1,0:T(8,128)(2,1)S(1)} %gate.2.image_1, ...), custom_call_target="tpu_custom_call" | custom-call | flops 1660944384 | bytes 1048576 | tf_op jit(solution)/shard_map/first/pallas_call | solution.py:258
  69.1 10.5 %collective-permute-start.7 = (s32[1,256]{1,0:T(1,128)S(1)}, s32[1,256]{1,0:T(1,128)S(1)}, u32[]{:S(2)}, u32[]{:S(2)}) collective-permute-start(s32[1,256]{1,0:T(1,128)S(1)} %get-tuple-element.16), channel_id=1, source_target_pairs={{4,0},{8,4},{12,8},{16,12},{20,16},{24,20},{28,24},{32,28},{36,32}... | collective-permute-start | bytes 3080 | tf_op jit(solution)/shard_map/ppermute | solution.py:22
  79.5 0.8 collective-permute-done.7.far_1
  80.3 0.0 collective-permute-done.6.after_1
  80.3 0.0 collective-permute-done.4.prior_1
  80.3 2.4 %second.1 = (bf16[256,1152]{1,0:T(8,128)(2,1)S(1)}, bf16[256,1152]{1,0:T(8,128)(2,1)S(1)}) custom-call(s32[4]{0:T(128)S(1)} %pad_add_fusion.places, f32[1]{0:T(128)} %copy.12.scale, f32[1]{0:T(128)S(6)} %copy.13.bias, bf16[256,1152]{1,0:T(8,128)(2,1)S(1)} %gate.2.image_1, bf16[256,1152]{1,0:T(8,128)(2,1)S(1)} %gate.3.text_1, ...), custom_call_target="tpu_custom_call" | custom-call | flops 603979776 | bytes 1048576 | tf_op jit(solution)/shard_map/second/pallas_call | solution.py:262
  82.7 1.9 %collective-permute-start.9 = (bf16[256,1152]{1,0:T(8,128)(2,1)S(1)}, bf16[256,1152]{1,0:T(8,128)(2,1)S(1)}, u32[]{:S(2)}, u32[]{:S(2)}) collective-permute-start(bf16[256,1152]{1,0:T(8,128)(2,1)S(1)} %get-tuple-element.23), channel_id=1, source_target_pairs={{0,1},{1,0},{2,3},{3,2},{4,5},{5,4},{6,7},{7,6},{8,9},{9,8},{10,11... | collective-permute-start | bytes 1769480 | tf_op jit(solution)/shard_map/ppermute | solution.py:287
  84.7 4.9 %collective-permute-start.10 = (bf16[256,1152]{1,0:T(8,128)(2,1)S(1)}, bf16[256,1152]{1,0:T(8,128)(2,1)S(1)}, u32[]{:S(2)}, u32[]{:S(2)}) collective-permute-start(bf16[256,1152]{1,0:T(8,128)(2,1)S(1)} %get-tuple-element.19.sent), channel_id=1, source_target_pairs={{1,2},{2,1},{3,0},{0,3},{5,6},{6,5},{7,4},{4,7},{9,10},{10,9},{11,... | collective-permute-start | bytes 1769480 | tf_op jit(solution)/shard_map/ppermute | solution.py:288
  89.6 6.5 %late.1 = (f32[256,1152]{1,0:T(8,128)S(1)}, f32[256,1152]{1,0:T(8,128)S(1)}, f32[1,256]{1,0:T(1,128)S(1)}, f32[1,256]{1,0:T(1,128)S(1)}) custom-call(s32[4]{0:T(128)S(1)} %pad_add_fusion.places, f32[1]{0:T(128)} %copy.12.scale, f32[1]{0:T(128)S(6)} %copy.13.bias, bf16[256,1152]{1,0:T(8,128)(2,1)S(1)} %copy-done.1, bf16[256,1152]{1,0:T(8,128)(2,1)S(1)} %gate.2.image_1, ...), custom_call_target="tpu_custom_call" | custom-call | flops 2868903936 | bytes 1048576 | tf_op jit(solution)/shard_map/late/pallas_call | solution.py:265
  96.0 3.3 %collective-permute-start.8 = (f32[1,256]{1,0:T(1,128)S(1)}, f32[1,256]{1,0:T(1,128)S(1)}, u32[]{:S(2)}, u32[]{:S(2)}) collective-permute-start(f32[1,256]{1,0:T(1,128)S(1)} %get-tuple-element.21), channel_id=1, source_target_pairs={{0,1},{1,0},{2,3},{3,2},{4,5},{5,4},{6,7},{7,6},{8,9},{9,8},{10,11... | collective-permute-start | bytes 3080 | tf_op jit(solution)/shard_map/ppermute | solution.py:289
  99.4 26.6 %collective-permute-done.8 = f32[1,256]{1,0:T(1,128)S(1)} collective-permute-done((f32[1,256]{1,0:T(1,128)S(1)}, f32[1,256]{1,0:T(1,128)S(1)}, u32[]{:S(2)}, u32[]{:S(2)}) %collective-permute-start.8) | collective-permute-done | bytes 1056 | tf_op jit(solution)/shard_map/ppermute | solution.py:289
  126.0 0.6 add.37
  126.6 0.0 collective-permute-done.9
  126.6 1.0 multiply_convert_fusion.1
  127.6 0.0 collective-permute-done.10
  127.6 1.0 multiply_convert_fusion
  (2 shorter events, 0.0 us)
Async XLA Ops:
  0.6 44.6 %collective-permute-start = (bf16[256,1152]{1,0:T(8,128)(2,1)}, bf16[256,1152]{1,0:T(8,128)(2,1)S(1)}, u32[]{:S(2)}, u32[]{:S(2)}) collective-permute-start(bf16[256,1152]{1,0:T(8,128)(2,1)} %image_0.3), channel_id=1, source_target_pairs={{0,1},{1,0},{2,3},{3,2},{4,5},{5,4},{6,7},{7,6},{8,9},{9,8},{10,11... | collective-permute-start | bytes 1769480 | tf_op jit(solution)/shard_map/ppermute | solution.py:241
  9.1 53.7 %collective-permute-start.2 = (bf16[256,1152]{1,0:T(8,128)(2,1)}, bf16[256,1152]{1,0:T(8,128)(2,1)S(1)}, u32[]{:S(2)}, u32[]{:S(2)}) collective-permute-start(bf16[256,1152]{1,0:T(8,128)(2,1)} %text_0.3), channel_id=1, source_target_pairs={{1,2},{2,1},{3,0},{0,3},{5,6},{6,5},{7,4},{4,7},{9,10},{10,9},{11,... | collective-permute-start | bytes 1769480 | tf_op jit(solution)/shard_map/ppermute | solution.py:240
  19.9 1.1 copy-start
  21.0 1.1 copy-start.2
  22.1 0.7 copy-start.6
  24.4 40.3 %collective-permute-start.5 = (bf16[272,1152]{1,0:T(8,128)(2,1)}, bf16[272,1152]{1,0:T(8,128)(2,1)}, u32[]{:S(2)}, u32[]{:S(2)}) collective-permute-start(bf16[272,1152]{1,0:T(8,128)(2,1)} %get-tuple-element.15), channel_id=1, source_target_pairs={{4,0},{8,4},{12,8},{16,12},{20,16},{24,20},{28,24},{32,28},{36,32}... | collective-permute-start | bytes 1880072 | tf_op jit(solution)/shard_map/ppermute | solution.py:22
  27.5 37.2 %copy-start.1 = (bf16[256,1152]{1,0:T(8,128)(2,1)S(1)}, bf16[256,1152]{1,0:T(8,128)(2,1)}, u32[]{:S(2)}) copy-start(bf16[256,1152]{1,0:T(8,128)(2,1)} %image_0.3) | copy-start | bytes 1769476
  27.5 37.2 %copy-start.3 = (bf16[256,1152]{1,0:T(8,128)(2,1)S(1)}, bf16[256,1152]{1,0:T(8,128)(2,1)}, u32[]{:S(2)}) copy-start(bf16[256,1152]{1,0:T(8,128)(2,1)} %text_0.3) | copy-start | bytes 1769476
  27.5 37.2 %copy-start.7 = (s32[256]{0:T(256)S(1)}, s32[256]{0:T(256)}, u32[]{:S(2)}) copy-start(s32[256]{0:T(256)} %param.7) | copy-start | bytes 3076
  27.6 37.1 %collective-permute-start.3 = (bf16[256,1152]{1,0:T(8,128)(2,1)}, bf16[256,1152]{1,0:T(8,128)(2,1)S(1)}, u32[]{:S(2)}, u32[]{:S(2)}) collective-permute-start(bf16[256,1152]{1,0:T(8,128)(2,1)} %get-tuple-element.14), channel_id=1, source_target_pairs={{764,0},{0,4},{4,8},{8,12},{12,16},{16,20},{20,24},{24,28},{28,32}... | collective-permute-start | bytes 1769480 | tf_op jit(solution)/shard_map/ppermute | solution.py:22
  30.8 14.5 %collective-permute-start.1 = (s32[1,256]{1,0:T(1,128)S(1)}, s32[1,256]{1,0:T(1,128)S(1)}, u32[]{:S(2)}, u32[]{:S(2)}) collective-permute-start(s32[1,256]{1,0:T(1,128)S(1)} %bitcast.10), channel_id=1, source_target_pairs={{0,1},{1,0},{2,3},{3,2},{4,5},{5,4},{6,7},{7,6},{8,9},{9,8},{10,11... | collective-permute-start | bytes 3080 | tf_op jit(solution)/shard_map/ppermute | solution.py:250
  45.3 0.6 copy-start.4
  45.8 18.9 %copy-start.5 = (s32[1,256]{1,0:T(1,128)S(1)}, s32[1,256]{1,0:T(1,128)}, u32[]{:S(2)}) copy-start(s32[1,256]{1,0:T(1,128)} %copy-done.4) | copy-start | bytes 3076
  45.8 34.5 %collective-permute-start.6 = (bf16[256,1152]{1,0:T(8,128)(2,1)S(1)}, bf16[256,1152]{1,0:T(8,128)(2,1)S(1)}, u32[]{:S(2)}, u32[]{:S(2)}) collective-permute-start(bf16[256,1152]{1,0:T(8,128)(2,1)S(1)} %gate.2.image_1), channel_id=1, source_target_pairs={{4,0},{8,4},{12,8},{16,12},{20,16},{24,20},{28,24},{32,28},{36,32}... | collective-permute-start | bytes 1769480 | tf_op jit(solution)/shard_map/ppermute | solution.py:22
  62.8 17.6 %collective-permute-start.4 = (bf16[256,1152]{1,0:T(8,128)(2,1)S(1)}, bf16[256,1152]{1,0:T(8,128)(2,1)S(1)}, u32[]{:S(2)}, u32[]{:S(2)}) collective-permute-start(bf16[256,1152]{1,0:T(8,128)(2,1)S(1)} %gate.3.text_1), channel_id=1, source_target_pairs={{764,0},{0,4},{4,8},{8,12},{12,16},{16,20},{20,24},{24,28},{28,32}... | collective-permute-start | bytes 1769480 | tf_op jit(solution)/shard_map/ppermute | solution.py:22
  69.1 11.3 %collective-permute-start.7 = (s32[1,256]{1,0:T(1,128)S(1)}, s32[1,256]{1,0:T(1,128)S(1)}, u32[]{:S(2)}, u32[]{:S(2)}) collective-permute-start(s32[1,256]{1,0:T(1,128)S(1)} %get-tuple-element.16), channel_id=1, source_target_pairs={{4,0},{8,4},{12,8},{16,12},{20,16},{24,20},{28,24},{32,28},{36,32}... | collective-permute-start | bytes 3080 | tf_op jit(solution)/shard_map/ppermute | solution.py:22
  82.7 43.8 %collective-permute-start.9 = (bf16[256,1152]{1,0:T(8,128)(2,1)S(1)}, bf16[256,1152]{1,0:T(8,128)(2,1)S(1)}, u32[]{:S(2)}, u32[]{:S(2)}) collective-permute-start(bf16[256,1152]{1,0:T(8,128)(2,1)S(1)} %get-tuple-element.23), channel_id=1, source_target_pairs={{0,1},{1,0},{2,3},{3,2},{4,5},{5,4},{6,7},{7,6},{8,9},{9,8},{10,11... | collective-permute-start | bytes 1769480 | tf_op jit(solution)/shard_map/ppermute | solution.py:287
  84.7 42.9 %collective-permute-start.10 = (bf16[256,1152]{1,0:T(8,128)(2,1)S(1)}, bf16[256,1152]{1,0:T(8,128)(2,1)S(1)}, u32[]{:S(2)}, u32[]{:S(2)}) collective-permute-start(bf16[256,1152]{1,0:T(8,128)(2,1)S(1)} %get-tuple-element.19.sent), channel_id=1, source_target_pairs={{1,2},{2,1},{3,0},{0,3},{5,6},{6,5},{7,4},{4,7},{9,10},{10,9},{11,... | collective-permute-start | bytes 1769480 | tf_op jit(solution)/shard_map/ppermute | solution.py:288
  96.0 30.0 %collective-permute-start.8 = (f32[1,256]{1,0:T(1,128)S(1)}, f32[1,256]{1,0:T(1,128)S(1)}, u32[]{:S(2)}, u32[]{:S(2)}) collective-permute-start(f32[1,256]{1,0:T(1,128)S(1)} %get-tuple-element.21), channel_id=1, source_target_pairs={{0,1},{1,0},{2,3},{3,2},{4,5},{5,4},{6,7},{7,6},{8,9},{9,8},{10,11... | collective-permute-start | bytes 3080 | tf_op jit(solution)/shard_map/ppermute | solution.py:289

commit v9 on v8

--- a/solution.py
+++ b/solution.py
@@ -30,14 +30,44 @@
     return lax.dot_general(x, y, (((0,), (0,)), ((), ())), preferred_element_type=jnp.float32)
 
 
+def as_digits(positive):
+    digits = [(positive >> shift) & 255 for shift in SHIFTS]
+    digits.append(jnp.zeros((TAIL - len(SHIFTS), positive.shape[1]), jnp.int32))
+    return jnp.concatenate(digits).astype(jnp.float32).astype(jnp.bfloat16)
+
+
 def hold_kernel(places, scale, bias, images, texts, positive, images_out, texts_out):
     rows = images.shape[0]
     images_out[pl.ds(0, rows), :] = images[...]
     images_out[pl.ds(rows, TAIL), :] = jnp.zeros((TAIL, images.shape[1]), jnp.bfloat16)
-    digits = [(positive[...] >> shift) & 255 for shift in SHIFTS]
-    digits = jnp.concatenate(digits + [jnp.zeros((TAIL - len(SHIFTS), rows), jnp.int32)])
-    images_out[pl.ds(rows, TAIL), pl.ds(0, rows)] = digits.astype(jnp.float32).astype(jnp.bfloat16)
+    images_out[pl.ds(rows, TAIL), pl.ds(0, rows)] = as_digits(positive[...])
     texts_out[...] = texts[...]
+
+
+def pack_kernel(image, positive, packed, tail, sems):
+    rows = image.shape[0]
+    body = pltpu.make_async_copy(image, packed.at[pl.ds(0, rows), :], sems.at[0])
+    body.start()
+    tail[...] = jnp.zeros_like(tail)
+    tail[:, pl.ds(0, rows)] = as_digits(positive[...])
+    end = pltpu.make_async_copy(tail, packed.at[pl.ds(rows, TAIL), :], sems.at[1])
+    end.start()
+    body.wait()
+    end.wait()
+
+
+def pack(image, positive):
+    rows, width = image.shape
+    anywhere = pl.BlockSpec(memory_space=pl.ANY)
+    return pl.pallas_call(
+        pack_kernel,
+        name="pack",
+        out_shape=pltpu.VMEM((rows + TAIL, width), image.dtype),
+        in_specs=[anywhere, VMEM],
+        out_specs=anywhere,
+        scratch_shapes=[pltpu.VMEM((TAIL, width), image.dtype), pltpu.SemaphoreType.DMA((2,))],
+        cost_estimate=cost(0),
+    )(pltpu.with_memory_space_constraint(image, pltpu.VMEM), positive)
 
 
 class Blocks:
@@ -105,9 +135,7 @@
     near_1,
     image_part,
     text_part,
-    near_out,
 ):
-    near_out[...] = near_1[...]
     block = Blocks(places, scale, bias)
     weights, _ = block(text_1[...], image_1[...], near_1[...], 1)
     image_part[...] = over_first(weights, text_1[...])
@@ -132,7 +160,6 @@
     prior_1,
     after_1,
     near_1,
-    far_1,
     image_part,
     text_part,
     image_send,
@@ -142,8 +169,9 @@
     weights, _ = block(prior_1[...], image_1[...], near_1[...], 3)
     total = image_part[...] + over_first(weights, prior_1[...])
     image_send[...] = total.astype(image_send.dtype)
-    weights, _ = block(text_1[...], after_1[...], far_1[...], 1)
-    total = text_part[...] + by_image(weights, after_1[...])
+    image, far = read_after(after_1)
+    weights, _ = block(text_1[...], image, far, 1)
+    total = text_part[...] + by_image(weights, image)
     text_send[...] = total.astype(text_send.dtype)
 
 
@@ -161,7 +189,6 @@
     after_1,
     near_0,
     near_1,
-    far_1,
     sent,
     image_own,
     text_own,
@@ -187,7 +214,7 @@
     add_image(text_1[...], 1)
     add_image(prior_1[...], 3)
     add_text(image_1[...], near_1[...])
-    add_text(after_1[...], far_1[...])
+    add_text(*read_after(after_1))
     add_image(prior_0[...], 2)
     add_text(*read_after(after_0))
     loss_send[...] = jnp.zeros_like(loss_send)
@@ -234,7 +261,6 @@
     long_shard = jax.ShapeDtypeStruct((rows + TAIL, width), jnp.bfloat16)
     real_shard = jax.ShapeDtypeStruct((rows, width), jnp.float32)
     line = jax.ShapeDtypeStruct((1, rows), jnp.float32)
-    int_line = jax.ShapeDtypeStruct((1, rows), jnp.int32)
     anywhere = [pl.BlockSpec(memory_space=pl.ANY)]
 
     text_1 = lax.ppermute(texts, "inner", TEXT_PAIRS)
@@ -250,22 +276,20 @@
     near_1 = lax.ppermute(near_0, "inner", IMAGE_PAIRS)
     prior_0 = from_behind(texts_later, 1)
     after_0 = from_behind(images_later, -1)
-    image_1 = gate(image_1, near_1)
-    after_1 = from_behind(image_1, -1)
+    after_1 = from_behind(pack(image_1, near_1), -1)
     text_1 = gate(text_1, near_1)
     prior_1 = from_behind(text_1, 1)
 
-    image_part, text_part, near_late = call(
-        first_kernel, "first", [SMEM] * 3 + [VMEM] * 8, [real_shard, real_shard, int_line], 11
+    image_part, text_part = call(
+        first_kernel, "first", [SMEM] * 3 + [VMEM] * 8, [real_shard, real_shard], 11
     )(*scalars, images, image_1, texts, text_1, prior_0, after_0, near_0, near_1)
-    far_1 = from_behind(near_late, -1)
     image_send, text_send = call(
-        second_kernel, "second", [SMEM] * 3 + [VMEM] * 8, [shard, shard], 4
-    )(*scalars, image_1, text_1, prior_1, after_1, near_1, far_1, image_part, text_part)
+        second_kernel, "second", [SMEM] * 3 + [VMEM] * 7, [shard, shard], 4
+    )(*scalars, image_1, text_1, prior_1, after_1, near_1, image_part, text_part)
     image_own, text_own, loss_own, loss_send = call(
         late_kernel,
         "late",
-        [SMEM] * 3 + [VMEM] * 11 + anywhere,
+        [SMEM] * 3 + [VMEM] * 10 + anywhere,
         [real_shard, real_shard, line, line],
         LATE_BLOCKS,
     )(
@@ -280,7 +304,6 @@
         after_1,
         near_0,
         near_1,
-        far_1,
             text_send,
     )
 

time: 130 us -> 135 us (1.038)
  the two profiles are of different devices: /device:TPU:1 before, /device:TPU:64 now
where the time goes in v9:
time: 135 us
  starting transfers between devices  82.6 us (61%)
  waiting for transfers between devices  26.8 us (20%)
  Pallas kernels  16.1 us (12%)
  local copies, waits for them, and re-layouts  4.44 us (3%)
  other arithmetic  2.6 us (2%)
  between operations  2.14 us (2%)
    ppermute x1, starting transfers between devices, per_device(): text_back = lax.ppermute(text_send, 'inner', TEXT_PAIRS)  22.6 us
    ppermute x4, starting transfers between devices, from_behind(): lax.ppermute(block, 'outer', [((i - distance) % count, i) for i in range(...  19.5 us
    ppermute x1, waiting for transfers between devices, per_device(): near_1 = lax.ppermute(near_0, 'inner', IMAGE_PAIRS)  16.8 us
    ppermute x1, starting transfers between devices, per_device(): image_back = lax.ppermute(image_send, 'inner', IMAGE_PAIRS)  10.4 us
    ppermute x1, starting transfers between devices, per_device(): image_1 = lax.ppermute(images, 'inner', IMAGE_PAIRS)  9.11 us
    ppermute x1, starting transfers between devices, per_device(): text_1 = lax.ppermute(texts, 'inner', TEXT_PAIRS)  8.21 us
    ppermute x4, waiting for transfers between devices, from_behind(): lax.ppermute(block, 'outer', [((i - distance) % count, i) for i in range(...  7.89 us
    pallas_call x1, Pallas kernels, per_device(): call(late_kernel, 'late', [SMEM] * 3 + [VMEM] * 10 + anywhere, [real_shar...  6.67 us
  transfers between devices with their start and end apart: 10, of which 3 were waited for; matrix products, arithmetic and copies ran while one was open for 1% of the time, Pallas kernels for 10%

profile of v9, /device:TPU:64, one launch (start us, length us, event | category | flops | bytes accessed | tf_op | source)
XLA Modules:
  0.0 134.7 jit_solution(18229691697578698650)
XLA Ops:
  0.6 9.1 %collective-permute-start = (bf16[256,1152]{1,0:T(8,128)(2,1)}, bf16[256,1152]{1,0:T(8,128)(2,1)S(1)}, u32[]{:S(2)}, u32[]{:S(2)}) collective-permute-start(bf16[256,1152]{1,0:T(8,128)(2,1)} %image_0.3), channel_id=1, source_target_pairs={{0,1},{1,0},{2,3},{3,2},{4,5},{5,4},{6,7},{7,6},{8,9},{9,8},{10,11... | collective-permute-start | bytes 1769480 | tf_op jit(solution)/shard_map/ppermute | solution.py:267
  9.7 8.2 %collective-permute-start.1 = (bf16[256,1152]{1,0:T(8,128)(2,1)}, bf16[256,1152]{1,0:T(8,128)(2,1)S(1)}, u32[]{:S(2)}, u32[]{:S(2)}) collective-permute-start(bf16[256,1152]{1,0:T(8,128)(2,1)} %text_0.3), channel_id=1, source_target_pairs={{1,2},{2,1},{3,0},{0,3},{5,6},{6,5},{7,4},{4,7},{9,10},{10,9},{11,... | collective-permute-start | bytes 1769480 | tf_op jit(solution)/shard_map/ppermute | solution.py:266
  19.3 0.1 pad_add_fusion.places
  19.4 0.0 copy-start
  19.4 1.1 copy-done
  20.4 0.0 copy-start.2
  20.4 1.1 copy-done.2
  21.5 0.0 copy-start.6
  21.5 0.7 copy-done.6
  22.2 1.6 %hold.1 = (bf16[272,1152]{1,0:T(8,128)(2,1)}, bf16[256,1152]{1,0:T(8,128)(2,1)}) custom-call(s32[4]{0:T(128)S(1)} %pad_add_fusion.places, f32[1]{0:T(128)} %copy.10.scale, f32[1]{0:T(128)S(6)} %copy.11.bias, bf16[256,1152]{1,0:T(8,128)(2,1)S(1)} %copy-done, bf16[256,1152]{1,0:T(8,128)(2,1)S(1)} %copy-done.2, s32[1,256]{1,0:T(1,128)S(1)} %bitcast.9), custom_call_target="tpu_custom_call" | custom-call | flops 150994944 | bytes 1048576 | tf_op jit(solution)/shard_map/hold/pallas_call | solution.py:269
  23.8 5.8 %collective-permute-start.5 = (bf16[272,1152]{1,0:T(8,128)(2,1)}, bf16[272,1152]{1,0:T(8,128)(2,1)}, u32[]{:S(2)}, u32[]{:S(2)}) collective-permute-start(bf16[272,1152]{1,0:T(8,128)(2,1)} %get-tuple-element.14), channel_id=1, source_target_pairs={{4,0},{8,4},{12,8},{16,12},{20,16},{24,20},{28,24},{32,28},{36,32}... | collective-permute-start | bytes 1880072 | tf_op jit(solution)/shard_map/ppermute | solution.py:22
  29.7 0.0 copy-start.1
  29.7 0.0 copy-start.7
  29.7 2.1 %collective-permute-start.3 = (bf16[256,1152]{1,0:T(8,128)(2,1)}, bf16[256,1152]{1,0:T(8,128)(2,1)}, u32[]{:S(2)}, u32[]{:S(2)}) collective-permute-start(bf16[256,1152]{1,0:T(8,128)(2,1)} %get-tuple-element.13), channel_id=1, source_target_pairs={{764,0},{0,4},{4,8},{8,12},{12,16},{16,20},{20,24},{24,28},{28,32}... | collective-permute-start | bytes 1769480 | tf_op jit(solution)/shard_map/ppermute | solution.py:22
  31.7 6.4 %collective-permute-start.2 = (s32[1,256]{1,0:T(1,128)S(1)}, s32[1,256]{1,0:T(1,128)S(1)}, u32[]{:S(2)}, u32[]{:S(2)}) collective-permute-start(s32[1,256]{1,0:T(1,128)S(1)} %bitcast.10), channel_id=1, source_target_pairs={{0,1},{1,0},{2,3},{3,2},{4,5},{5,4},{6,7},{7,6},{8,9},{9,8},{10,11... | collective-permute-start | bytes 3080 | tf_op jit(solution)/shard_map/ppermute | solution.py:276
  38.2 16.8 %collective-permute-done.2.refs_1_.positive.near_1 = s32[1,256]{1,0:T(1,128)S(1)} collective-permute-done((s32[1,256]{1,0:T(1,128)S(1)}, s32[1,256]{1,0:T(1,128)S(1)}, u32[]{:S(2)}, u32[]{:S(2)}) %collective-permute-start.2) | collective-permute-done | bytes 1056 | tf_op jit(solution)/shard_map/ppermute | solution.py:276
  55.0 0.0 copy-start.4
  55.0 0.0 collective-permute-done.image.image_1
  55.0 0.6 copy-done.4
  55.5 0.9 pack.1
  56.4 0.0 copy-start.5
  56.4 9.7 %collective-permute-start.6 = (bf16[272,1152]{1,0:T(8,128)(2,1)S(1)}, bf16[272,1152]{1,0:T(8,128)(2,1)S(1)}, u32[]{:S(2)}, u32[]{:S(2)}) collective-permute-start(bf16[272,1152]{1,0:T(8,128)(2,1)S(1)} %pack.1), channel_id=1, source_target_pairs={{4,0},{8,4},{12,8},{16,12},{20,16},{24,20},{28,24},{32,28},{36,32}... | collective-permute-start | bytes 1880072 | tf_op jit(solution)/shard_map/ppermute | solution.py:22
  66.1 0.0 collective-permute-done.1.refs_0_
  66.2 1.9 %collective-permute-start.4 = (bf16[256,1152]{1,0:T(8,128)(2,1)S(1)}, bf16[256,1152]{1,0:T(8,128)(2,1)S(1)}, u32[]{:S(2)}, u32[]{:S(2)}) collective-permute-start(bf16[256,1152]{1,0:T(8,128)(2,1)S(1)} %gate.1.text_1), channel_id=1, source_target_pairs={{764,0},{0,4},{4,8},{8,12},{12,16},{16,20},{20,24},{24,28},{28,32}... | collective-permute-start | bytes 1769480 | tf_op jit(solution)/shard_map/ppermute | solution.py:22
  68.1 0.0 collective-permute-done.3.prior_0
  68.1 0.0 collective-permute-done.5.after_0
  68.1 0.0 copy-done.1
  68.1 0.0 copy-done.7
  68.1 0.0 copy-done.5
  68.1 0.0 copy-start.3
  68.1 1.1 copy-done.3
  69.2 4.5 %first.1 = (f32[256,1152]{1,0:T(8,128)S(1)}, f32[256,1152]{1,0:T(8,128)S(1)}) custom-call(s32[4]{0:T(128)S(1)} %pad_add_fusion.places, f32[1]{0:T(128)} %copy.10.scale, f32[1]{0:T(128)S(6)} %copy.11.bias, bf16[256,1152]{1,0:T(8,128)(2,1)S(1)} %copy-done.1, bf16[256,1152]{1,0:T(8,128)(2,1)S(1)} %collective-permute-done.image.image_1, ...), custom_call_target="tpu_custom_call" | custom-call | flops 1660944384 | bytes 1048576 | tf_op jit(solution)/shard_map/first/pallas_call | solution.py:283
  73.7 7.9 %collective-permute-done.4.prior_1 = bf16[256,1152]{1,0:T(8,128)(2,1)S(1)} collective-permute-done((bf16[256,1152]{1,0:T(8,128)(2,1)S(1)}, bf16[256,1152]{1,0:T(8,128)(2,1)S(1)}, u32[]{:S(2)}, u32[]{:S(2)}) %collective-permute-start.4) | collective-permute-done | bytes 589856 | tf_op jit(solution)/shard_map/ppermute | solution.py:22
  81.6 0.0 collective-permute-done.6.after_1
  81.6 2.4 %second.1 = (bf16[256,1152]{1,0:T(8,128)(2,1)S(1)}, bf16[256,1152]{1,0:T(8,128)(2,1)S(1)}) custom-call(s32[4]{0:T(128)S(1)} %pad_add_fusion.places, f32[1]{0:T(128)} %copy.10.scale, f32[1]{0:T(128)S(6)} %copy.11.bias, bf16[256,1152]{1,0:T(8,128)(2,1)S(1)} %collective-permute-done.image.image_1, bf16[256,1152]{1,0:T(8,128)(2,1)S(1)} %gate.1.text_1, ...), custom_call_target="tpu_custom_call" | custom-call | flops 603979776 | bytes 1048576 | tf_op jit(solution)/shard_map/second/pallas_call | solution.py:286
  84.0 10.4 %collective-permute-start.8 = (bf16[256,1152]{1,0:T(8,128)(2,1)S(1)}, bf16[256,1152]{1,0:T(8,128)(2,1)S(1)}, u32[]{:S(2)}, u32[]{:S(2)}) collective-permute-start(bf16[256,1152]{1,0:T(8,128)(2,1)S(1)} %get-tuple-element.21), channel_id=1, source_target_pairs={{0,1},{1,0},{2,3},{3,2},{4,5},{5,4},{6,7},{7,6},{8,9},{9,8},{10,11... | collective-permute-start | bytes 1769480 | tf_op jit(solution)/shard_map/ppermute | solution.py:310
  94.4 22.6 %collective-permute-start.9 = (bf16[256,1152]{1,0:T(8,128)(2,1)S(1)}, bf16[256,1152]{1,0:T(8,128)(2,1)S(1)}, u32[]{:S(2)}, u32[]{:S(2)}) collective-permute-start(bf16[256,1152]{1,0:T(8,128)(2,1)S(1)} %get-tuple-element.17.sent), channel_id=1, source_target_pairs={{1,2},{2,1},{3,0},{0,3},{5,6},{6,5},{7,4},{4,7},{9,10},{10,9},{11,... | collective-permute-start | bytes 1769480 | tf_op jit(solution)/shard_map/ppermute | solution.py:311
  117.0 6.7 %late.1 = (f32[256,1152]{1,0:T(8,128)S(1)}, f32[256,1152]{1,0:T(8,128)S(1)}, f32[1,256]{1,0:T(1,128)S(1)}, f32[1,256]{1,0:T(1,128)S(1)}) custom-call(s32[4]{0:T(128)S(1)} %pad_add_fusion.places, f32[1]{0:T(128)} %copy.10.scale, f32[1]{0:T(128)S(6)} %copy.11.bias, bf16[256,1152]{1,0:T(8,128)(2,1)S(1)} %copy-done.1, ...), custom_call_target="tpu_custom_call" | custom-call | flops 2868903936 | bytes 1048576 | tf_op jit(solution)/shard_map/late/pallas_call | solution.py:289
  123.7 6.3 %collective-permute-start.7 = (f32[1,256]{1,0:T(1,128)S(1)}, f32[1,256]{1,0:T(1,128)S(1)}, u32[]{:S(2)}, u32[]{:S(2)}) collective-permute-start(f32[1,256]{1,0:T(1,128)S(1)} %get-tuple-element.19), channel_id=1, source_target_pairs={{0,1},{1,0},{2,3},{3,2},{4,5},{5,4},{6,7},{7,6},{8,9},{9,8},{10,11... | collective-permute-start | bytes 3080 | tf_op jit(solution)/shard_map/ppermute | solution.py:312
  130.0 2.1 %collective-permute-done.7 = f32[1,256]{1,0:T(1,128)S(1)} collective-permute-done((f32[1,256]{1,0:T(1,128)S(1)}, f32[1,256]{1,0:T(1,128)S(1)}, u32[]{:S(2)}, u32[]{:S(2)}) %collective-permute-start.7) | collective-permute-done | bytes 1056 | tf_op jit(solution)/shard_map/ppermute | solution.py:312
  132.2 0.6 add.37
  132.7 0.0 collective-permute-done.8
  132.7 1.0 multiply_convert_fusion.1
  133.7 0.0 collective-permute-done.9
  133.7 1.0 multiply_convert_fusion
  (1 shorter events, 0.0 us)
Async XLA Ops:
  0.6 54.3 %collective-permute-start = (bf16[256,1152]{1,0:T(8,128)(2,1)}, bf16[256,1152]{1,0:T(8,128)(2,1)S(1)}, u32[]{:S(2)}, u32[]{:S(2)}) collective-permute-start(bf16[256,1152]{1,0:T(8,128)(2,1)} %image_0.3), channel_id=1, source_target_pairs={{0,1},{1,0},{2,3},{3,2},{4,5},{5,4},{6,7},{7,6},{8,9},{9,8},{10,11... | collective-permute-start | bytes 1769480 | tf_op jit(solution)/shard_map/ppermute | solution.py:267
  9.7 56.4 %collective-permute-start.1 = (bf16[256,1152]{1,0:T(8,128)(2,1)}, bf16[256,1152]{1,0:T(8,128)(2,1)S(1)}, u32[]{:S(2)}, u32[]{:S(2)}) collective-permute-start(bf16[256,1152]{1,0:T(8,128)(2,1)} %text_0.3), channel_id=1, source_target_pairs={{1,2},{2,1},{3,0},{0,3},{5,6},{6,5},{7,4},{4,7},{9,10},{10,9},{11,... | collective-permute-start | bytes 1769480 | tf_op jit(solution)/shard_map/ppermute | solution.py:266
  19.4 1.1 copy-start
  20.4 1.1 copy-start.2
  21.5 0.7 copy-start.6
  23.8 44.3 %collective-permute-start.5 = (bf16[272,1152]{1,0:T(8,128)(2,1)}, bf16[272,1152]{1,0:T(8,128)(2,1)}, u32[]{:S(2)}, u32[]{:S(2)}) collective-permute-start(bf16[272,1152]{1,0:T(8,128)(2,1)} %get-tuple-element.14), channel_id=1, source_target_pairs={{4,0},{8,4},{12,8},{16,12},{20,16},{24,20},{28,24},{32,28},{36,32}... | collective-permute-start | bytes 1880072 | tf_op jit(solution)/shard_map/ppermute | solution.py:22
  29.7 38.5 %copy-start.1 = (bf16[256,1152]{1,0:T(8,128)(2,1)S(1)}, bf16[256,1152]{1,0:T(8,128)(2,1)}, u32[]{:S(2)}) copy-start(bf16[256,1152]{1,0:T(8,128)(2,1)} %image_0.3) | copy-start | bytes 1769476
  29.7 38.5 %copy-start.7 = (s32[256]{0:T(256)S(1)}, s32[256]{0:T(256)}, u32[]{:S(2)}) copy-start(s32[256]{0:T(256)} %param.7) | copy-start | bytes 3076
  29.7 38.4 %collective-permute-start.3 = (bf16[256,1152]{1,0:T(8,128)(2,1)}, bf16[256,1152]{1,0:T(8,128)(2,1)}, u32[]{:S(2)}, u32[]{:S(2)}) collective-permute-start(bf16[256,1152]{1,0:T(8,128)(2,1)} %get-tuple-element.13), channel_id=1, source_target_pairs={{764,0},{0,4},{4,8},{8,12},{12,16},{16,20},{20,24},{24,28},{28,32}... | collective-permute-start | bytes 1769480 | tf_op jit(solution)/shard_map/ppermute | solution.py:22
  31.7 23.2 %collective-permute-start.2 = (s32[1,256]{1,0:T(1,128)S(1)}, s32[1,256]{1,0:T(1,128)S(1)}, u32[]{:S(2)}, u32[]{:S(2)}) collective-permute-start(s32[1,256]{1,0:T(1,128)S(1)} %bitcast.10), channel_id=1, source_target_pairs={{0,1},{1,0},{2,3},{3,2},{4,5},{5,4},{6,7},{7,6},{8,9},{9,8},{10,11... | collective-permute-start | bytes 3080 | tf_op jit(solution)/shard_map/ppermute | solution.py:276
  55.0 0.6 copy-start.4
  56.4 11.7 %copy-start.5 = (s32[1,256]{1,0:T(1,128)S(1)}, s32[1,256]{1,0:T(1,128)}, u32[]{:S(2)}) copy-start(s32[1,256]{1,0:T(1,128)} %copy-done.4) | copy-start | bytes 3076
  56.4 25.2 %collective-permute-start.6 = (bf16[272,1152]{1,0:T(8,128)(2,1)S(1)}, bf16[272,1152]{1,0:T(8,128)(2,1)S(1)}, u32[]{:S(2)}, u32[]{:S(2)}) collective-permute-start(bf16[272,1152]{1,0:T(8,128)(2,1)S(1)} %pack.1), channel_id=1, source_target_pairs={{4,0},{8,4},{12,8},{16,12},{20,16},{24,20},{28,24},{32,28},{36,32}... | collective-permute-start | bytes 1880072 | tf_op jit(solution)/shard_map/ppermute | solution.py:22
  66.2 15.4 %collective-permute-start.4 = (bf16[256,1152]{1,0:T(8,128)(2,1)S(1)}, bf16[256,1152]{1,0:T(8,128)(2,1)S(1)}, u32[]{:S(2)}, u32[]{:S(2)}) collective-permute-start(bf16[256,1152]{1,0:T(8,128)(2,1)S(1)} %gate.1.text_1), channel_id=1, source_target_pairs={{764,0},{0,4},{4,8},{8,12},{12,16},{16,20},{20,24},{24,28},{28,32}... | collective-permute-start | bytes 1769480 | tf_op jit(solution)/shard_map/ppermute | solution.py:22
  68.1 1.1 copy-start.3
  84.0 48.7 %collective-permute-start.8 = (bf16[256,1152]{1,0:T(8,128)(2,1)S(1)}, bf16[256,1152]{1,0:T(8,128)(2,1)S(1)}, u32[]{:S(2)}, u32[]{:S(2)}) collective-permute-start(bf16[256,1152]{1,0:T(8,128)(2,1)S(1)} %get-tuple-element.21), channel_id=1, source_target_pairs={{0,1},{1,0},{2,3},{3,2},{4,5},{5,4},{6,7},{7,6},{8,9},{9,8},{10,11... | collective-permute-start | bytes 1769480 | tf_op jit(solution)/shard_map/ppermute | solution.py:310
  94.4 39.3 %collective-permute-start.9 = (bf16[256,1152]{1,0:T(8,128)(2,1)S(1)}, bf16[256,1152]{1,0:T(8,128)(2,1)S(1)}, u32[]{:S(2)}, u32[]{:S(2)}) collective-permute-start(bf16[256,1152]{1,0:T(8,128)(2,1)S(1)} %get-tuple-element.17.sent), channel_id=1, source_target_pairs={{1,2},{2,1},{3,0},{0,3},{5,6},{6,5},{7,4},{4,7},{9,10},{10,9},{11,... | collective-permute-start | bytes 1769480 | tf_op jit(solution)/shard_map/ppermute | solution.py:311
  123.7 8.5 %collective-permute-start.7 = (f32[1,256]{1,0:T(1,128)S(1)}, f32[1,256]{1,0:T(1,128)S(1)}, u32[]{:S(2)}, u32[]{:S(2)}) collective-permute-start(f32[1,256]{1,0:T(1,128)S(1)} %get-tuple-element.19), channel_id=1, source_target_pairs={{0,1},{1,0},{2,3},{3,2},{4,5},{5,4},{6,7},{7,6},{8,9},{9,8},{10,11... | collective-permute-start | bytes 3080 | tf_op jit(solution)/shard_map/ppermute | solution.py:312

commit v10 on v9

--- a/solution.py
+++ b/solution.py
@@ -15,11 +15,20 @@
 SMEM = pl.BlockSpec(memory_space=pltpu.SMEM)
 LIMIT = 20 * 1024 * 1024
 LATE_BLOCKS = 19
+PLANES = 3
 
 
 def from_behind(block, distance):
     count = lax.axis_size("outer")
     return lax.ppermute(block, "outer", [((i - distance) % count, i) for i in range(count)])
+
+
+def credit_from_edge(block):
+    count = lax.axis_size("outer")
+    plane = count // PLANES
+    firsts = range(0, count, plane)
+    pairs = [(k, k + 1) for k in firsts] + [(k + plane - 1, k + plane - 2) for k in firsts]
+    return lax.ppermute(block, "outer", pairs)
 
 
 def over_last(x, y):
@@ -42,6 +51,10 @@
     images_out[pl.ds(rows, TAIL), :] = jnp.zeros((TAIL, images.shape[1]), jnp.bfloat16)
     images_out[pl.ds(rows, TAIL), pl.ds(0, rows)] = as_digits(positive[...])
     texts_out[...] = texts[...]
+
+
+def note_kernel(line, first, second, line_out):
+    line_out[...] = line[...]
 
 
 def pack_kernel(image, positive, packed, tail, sems):
@@ -261,6 +274,7 @@
     long_shard = jax.ShapeDtypeStruct((rows + TAIL, width), jnp.bfloat16)
     real_shard = jax.ShapeDtypeStruct((rows, width), jnp.float32)
     line = jax.ShapeDtypeStruct((1, rows), jnp.float32)
+    int_line = jax.ShapeDtypeStruct((1, rows), jnp.int32)
     anywhere = [pl.BlockSpec(memory_space=pl.ANY)]
 
     text_1 = lax.ppermute(texts, "inner", TEXT_PAIRS)
@@ -286,6 +300,11 @@
     image_send, text_send = call(
         second_kernel, "second", [SMEM] * 3 + [VMEM] * 7, [shard, shard], 4
     )(*scalars, image_1, text_1, prior_1, after_1, near_1, image_part, text_part)
+    (note,) = call(note_kernel, "note", [VMEM] + anywhere * 2, [int_line], 0)(
+        near_1, after_1, prior_1
+    )
+    credit = credit_from_edge(note)
+    image_send, text_send = gate(image_send, credit), gate(text_send, credit)
     image_own, text_own, loss_own, loss_send = call(
         late_kernel,
         "late",

time: 135 us -> 139 us (1.030)
  the two profiles are of different devices: /device:TPU:64 before, /device:TPU:1 now
where the time goes in v10:
time: 139 us; the launch traced here: 138 us
  starting transfers between devices  59 us (42%)
  waiting for transfers between devices  47 us (34%)
  Pallas kernels  16.1 us (12%)
  local copies, waits for them, and re-layouts  10.1 us (7%)
  other arithmetic  3.63 us (3%)
  between operations  2.15 us (2%)
    ppermute x4, starting transfers between devices, from_behind(): lax.ppermute(block, 'outer', [((i - distance) % count, i) for i in range(...  25 us
    ppermute x1, waiting for transfers between devices, per_device(): loss_back = lax.ppermute(loss_send, 'inner', IMAGE_PAIRS)  20.6 us
    ppermute x1, waiting for transfers between devices, credit_from_edge(): return lax.ppermute(block, 'outer', pairs)  10.3 us
    unnamed x26, local copies, waits for them, and re-layouts  10.1 us
    ppermute x1, waiting for transfers between devices, per_device(): near_1 = lax.ppermute(near_0, 'inner', IMAGE_PAIRS)  9.69 us
    ppermute x1, starting transfers between devices, per_device(): text_1 = lax.ppermute(texts, 'inner', TEXT_PAIRS)  9.43 us
    ppermute x1, starting transfers between devices, per_device(): image_1 = lax.ppermute(images, 'inner', IMAGE_PAIRS)  8.45 us
    pallas_call x1, Pallas kernels, per_device(): call(late_kernel, 'late', [SMEM] * 3 + [VMEM] * 10 + anywhere, [real_shar...  6.62 us
  transfers between devices with their start and end apart: 11, of which 5 were waited for; matrix products, arithmetic and copies ran while one was open for 2% of the time, Pallas kernels for 12%

profile of v10, /device:TPU:1, one launch (start us, length us, event | category | flops | bytes accessed | tf_op | source)
XLA Modules:
  0.0 137.9 jit_solution(5373472146209688282)
XLA Ops:
  0.6 8.4 %collective-permute-start = (bf16[256,1152]{1,0:T(8,128)(2,1)}, bf16[256,1152]{1,0:T(8,128)(2,1)S(1)}, u32[]{:S(2)}, u32[]{:S(2)}) collective-permute-start(bf16[256,1152]{1,0:T(8,128)(2,1)} %image_0.3), channel_id=1, source_target_pairs={{0,1},{1,0},{2,3},{3,2},{4,5},{5,4},{6,7},{7,6},{8,9},{9,8},{10,11... | collective-permute-start | bytes 1769480 | tf_op jit(solution)/shard_map/ppermute | solution.py:281
  9.1 9.4 %collective-permute-start.1 = (bf16[256,1152]{1,0:T(8,128)(2,1)}, bf16[256,1152]{1,0:T(8,128)(2,1)S(1)}, u32[]{:S(2)}, u32[]{:S(2)}) collective-permute-start(bf16[256,1152]{1,0:T(8,128)(2,1)} %text_0.3), channel_id=1, source_target_pairs={{1,2},{2,1},{3,0},{0,3},{5,6},{6,5},{7,4},{4,7},{9,10},{10,9},{11,... | collective-permute-start | bytes 1769480 | tf_op jit(solution)/shard_map/ppermute | solution.py:280
  19.8 0.1 pad_add_fusion.places
  19.9 0.0 copy-start
  19.9 1.1 copy-done
  21.0 0.0 copy-start.3
  21.0 1.1 copy-done.3
  22.1 0.0 copy-start.10
  22.1 0.7 copy-done.10
  22.7 1.6 %hold.1 = (bf16[272,1152]{1,0:T(8,128)(2,1)}, bf16[256,1152]{1,0:T(8,128)(2,1)}) custom-call(s32[4]{0:T(128)S(1)} %pad_add_fusion.places, f32[1]{0:T(128)} %copy.14.scale, f32[1]{0:T(128)S(6)} %copy.15.bias, bf16[256,1152]{1,0:T(8,128)(2,1)S(1)} %copy-done, bf16[256,1152]{1,0:T(8,128)(2,1)S(1)} %copy-done.3, s32[1,256]{1,0:T(1,128)S(1)} %bitcast.9), custom_call_target="tpu_custom_call" | custom-call | flops 150994944 | bytes 1048576 | tf_op jit(solution)/shard_map/hold/pallas_call | solution.py:283
  24.4 3.1 %collective-permute-start.5 = (bf16[272,1152]{1,0:T(8,128)(2,1)}, bf16[272,1152]{1,0:T(8,128)(2,1)}, u32[]{:S(2)}, u32[]{:S(2)}) collective-permute-start(bf16[272,1152]{1,0:T(8,128)(2,1)} %get-tuple-element.14), channel_id=1, source_target_pairs={{4,0},{8,4},{12,8},{16,12},{20,16},{24,20},{28,24},{32,28},{36,32}... | collective-permute-start | bytes 1880072 | tf_op jit(solution)/shard_map/ppermute | solution.py:23
  27.5 0.0 copy-start.11
  27.5 3.1 %collective-permute-start.3 = (bf16[256,1152]{1,0:T(8,128)(2,1)}, bf16[256,1152]{1,0:T(8,128)(2,1)}, u32[]{:S(2)}, u32[]{:S(2)}) collective-permute-start(bf16[256,1152]{1,0:T(8,128)(2,1)} %get-tuple-element.13), channel_id=1, source_target_pairs={{764,0},{0,4},{4,8},{8,12},{12,16},{16,20},{20,24},{24,28},{28,32}... | collective-permute-start | bytes 1769480 | tf_op jit(solution)/shard_map/ppermute | solution.py:23
  30.6 4.9 %collective-permute-start.2 = (s32[1,256]{1,0:T(1,128)S(1)}, s32[1,256]{1,0:T(1,128)S(1)}, u32[]{:S(2)}, u32[]{:S(2)}) collective-permute-start(s32[1,256]{1,0:T(1,128)S(1)} %bitcast.10), channel_id=1, source_target_pairs={{0,1},{1,0},{2,3},{3,2},{4,5},{5,4},{6,7},{7,6},{8,9},{9,8},{10,11... | collective-permute-start | bytes 3080 | tf_op jit(solution)/shard_map/ppermute | solution.py:290
  35.6 9.7 %collective-permute-done.2.refs_1_.positive.near_1.line = s32[1,256]{1,0:T(1,128)S(1)} collective-permute-done((s32[1,256]{1,0:T(1,128)S(1)}, s32[1,256]{1,0:T(1,128)S(1)}, u32[]{:S(2)}, u32[]{:S(2)}) %collective-permute-start.2) | collective-permute-done | bytes 1056 | tf_op jit(solution)/shard_map/ppermute | solution.py:290
  45.3 0.0 copy-start.8
  45.3 0.0 collective-permute-done.image.image_1
  45.3 0.6 copy-done.8
  45.8 0.9 pack.1
  46.7 0.0 copy-start.9
  46.7 16.8 %collective-permute-start.6 = (bf16[272,1152]{1,0:T(8,128)(2,1)S(1)}, bf16[272,1152]{1,0:T(8,128)(2,1)S(1)}, u32[]{:S(2)}, u32[]{:S(2)}) collective-permute-start(bf16[272,1152]{1,0:T(8,128)(2,1)S(1)} %pack.1), channel_id=1, source_target_pairs={{4,0},{8,4},{12,8},{16,12},{20,16},{24,20},{28,24},{32,28},{36,32}... | collective-permute-start | bytes 1880072 | tf_op jit(solution)/shard_map/ppermute | solution.py:23
  63.5 0.0 collective-permute-done.1.refs_0_
  63.5 1.9 %collective-permute-start.4 = (bf16[256,1152]{1,0:T(8,128)(2,1)S(1)}, bf16[256,1152]{1,0:T(8,128)(2,1)S(1)}, u32[]{:S(2)}, u32[]{:S(2)}) collective-permute-start(bf16[256,1152]{1,0:T(8,128)(2,1)S(1)} %gate.3.text_1), channel_id=1, source_target_pairs={{764,0},{0,4},{4,8},{8,12},{12,16},{16,20},{20,24},{24,28},{28,32}... | collective-permute-start | bytes 1769480 | tf_op jit(solution)/shard_map/ppermute | solution.py:23
  65.5 0.0 collective-permute-done.3.prior_0
  65.5 0.0 collective-permute-done.5.after_0
  65.5 0.0 copy-done.11
  65.5 0.0 copy-done.9
  65.5 0.0 copy-start.1
  65.5 1.1 copy-done.1
  66.6 0.0 copy-start.4
  66.6 1.1 copy-done.4
  67.6 4.5 %first.1 = (f32[256,1152]{1,0:T(8,128)S(1)}, f32[256,1152]{1,0:T(8,128)S(1)}) custom-call(s32[4]{0:T(128)S(1)} %pad_add_fusion.places, f32[1]{0:T(128)} %copy.14.scale, f32[1]{0:T(128)S(6)} %copy.15.bias, bf16[256,1152]{1,0:T(8,128)(2,1)S(1)} %copy-done.1, bf16[256,1152]{1,0:T(8,128)(2,1)S(1)} %collective-permute-done.image.image_1, ...), custom_call_target="tpu_custom_call" | custom-call | flops 1660944384 | bytes 1048576 | tf_op jit(solution)/shard_map/first/pallas_call | solution.py:297
  72.1 3.4 %collective-permute-done.4.prior_1.second = bf16[256,1152]{1,0:T(8,128)(2,1)S(1)} collective-permute-done((bf16[256,1152]{1,0:T(8,128)(2,1)S(1)}, bf16[256,1152]{1,0:T(8,128)(2,1)S(1)}, u32[]{:S(2)}, u32[]{:S(2)}) %collective-permute-start.4) | collective-permute-done | bytes 589856 | tf_op jit(solution)/shard_map/ppermute | solution.py:23
  75.5 0.0 collective-permute-done.6.after_1.first
  75.5 1.3 collective-permute-start.7
  76.8 2.4 %second.1 = (bf16[256,1152]{1,0:T(8,128)(2,1)}, bf16[256,1152]{1,0:T(8,128)(2,1)S(1)}) custom-call(s32[4]{0:T(128)S(1)} %pad_add_fusion.places, f32[1]{0:T(128)} %copy.14.scale, f32[1]{0:T(128)S(6)} %copy.15.bias, bf16[256,1152]{1,0:T(8,128)(2,1)S(1)} %collective-permute-done.image.image_1, bf16[256,1152]{1,0:T(8,128)(2,1)S(1)} %gate.3.text_1, ...), custom_call_target="tpu_custom_call" | custom-call | flops 603979776 | bytes 1048576 | tf_op jit(solution)/shard_map/second/pallas_call | solution.py:300
  79.2 0.0 copy-start.6
  79.2 0.8 copy-done.6
  80.1 10.3 %collective-permute-done.7.refs_1_ = s32[1,256]{1,0:T(1,128)S(1)} collective-permute-done((s32[1,256]{1,0:T(1,128)S(1)}, s32[1,256]{1,0:T(1,128)S(1)}, u32[]{:S(2)}, u32[]{:S(2)}) %collective-permute-start.7) | collective-permute-done | bytes 1056 | tf_op jit(solution)/shard_map/ppermute | solution.py:31
  90.3 0.0 copy-start.12
  90.3 0.6 copy-done.12
  90.9 2.8 %collective-permute-start.9 = (bf16[256,1152]{1,0:T(8,128)(2,1)}, bf16[256,1152]{1,0:T(8,128)(2,1)}, u32[]{:S(2)}, u32[]{:S(2)}) collective-permute-start(bf16[256,1152]{1,0:T(8,128)(2,1)} %gate.5), channel_id=1, source_target_pairs={{0,1},{1,0},{2,3},{3,2},{4,5},{5,4},{6,7},{7,6},{8,9},{9,8},{10,11... | collective-permute-start | bytes 1769480 | tf_op jit(solution)/shard_map/ppermute | solution.py:329
  93.7 0.0 copy-start.7
  93.7 1.1 copy-done.7
  94.7 5.3 %collective-permute-start.10 = (bf16[256,1152]{1,0:T(8,128)(2,1)S(1)}, bf16[256,1152]{1,0:T(8,128)(2,1)S(1)}, u32[]{:S(2)}, u32[]{:S(2)}) collective-permute-start(bf16[256,1152]{1,0:T(8,128)(2,1)S(1)} %gate.4.sent), channel_id=1, source_target_pairs={{1,2},{2,1},{3,0},{0,3},{5,6},{6,5},{7,4},{4,7},{9,10},{10,9},{11,... | collective-permute-start | bytes 1769480 | tf_op jit(solution)/shard_map/ppermute | solution.py:330
  100.0 0.0 copy-start.2
  100.0 1.1 copy-done.2
  101.1 0.0 copy-start.5
  101.1 1.1 copy-done.5
  102.1 6.6 %late.1 = (f32[256,1152]{1,0:T(8,128)S(1)}, f32[256,1152]{1,0:T(8,128)S(1)}, f32[1,256]{1,0:T(1,128)S(1)}, f32[1,256]{1,0:T(1,128)S(1)}) custom-call(s32[4]{0:T(128)S(1)} %pad_add_fusion.places, f32[1]{0:T(128)} %copy.14.scale, f32[1]{0:T(128)S(6)} %copy.15.bias, bf16[256,1152]{1,0:T(8,128)(2,1)S(1)} %copy-done.2, ...), custom_call_target="tpu_custom_call" | custom-call | flops 2868903936 | bytes 1048576 | tf_op jit(solution)/shard_map/late/pallas_call | solution.py:308
  108.7 1.9 %collective-permute-start.8 = (f32[1,256]{1,0:T(1,128)S(1)}, f32[1,256]{1,0:T(1,128)S(1)}, u32[]{:S(2)}, u32[]{:S(2)}) collective-permute-start(f32[1,256]{1,0:T(1,128)S(1)} %get-tuple-element.19), channel_id=1, source_target_pairs={{0,1},{1,0},{2,3},{3,2},{4,5},{5,4},{6,7},{7,6},{8,9},{9,8},{10,11... | collective-permute-start | bytes 3080 | tf_op jit(solution)/shard_map/ppermute | solution.py:331
  110.7 20.6 %collective-permute-done.8 = f32[1,256]{1,0:T(1,128)S(1)} collective-permute-done((f32[1,256]{1,0:T(1,128)S(1)}, f32[1,256]{1,0:T(1,128)S(1)}, u32[]{:S(2)}, u32[]{:S(2)}) %collective-permute-start.8) | collective-permute-done | bytes 1056 | tf_op jit(solution)/shard_map/ppermute | solution.py:331
  131.3 0.6 add.37
  131.9 0.0 collective-permute-done.9
  131.9 2.0 %multiply_convert_fusion.1 = bf16[256,1152]{1,0:T(8,128)(2,1)} fusion(f32[256,1152]{1,0:T(8,128)S(1)} %get-tuple-element.20, bf16[256,1152]{1,0:T(8,128)(2,1)} %collective-permute-done.9, f32[]{:T(128)} %bitcast.7), kind=kLoop, calls=%fused_computation.1 | loop fusion | flops 1179648 | bytes 2359300 | tf_op jit(solution)/shard_map/convert_element_type | solution.py:334
  133.9 3.0 %collective-permute-done.10 = bf16[256,1152]{1,0:T(8,128)(2,1)S(1)} collective-permute-done((bf16[256,1152]{1,0:T(8,128)(2,1)S(1)}, bf16[256,1152]{1,0:T(8,128)(2,1)S(1)}, u32[]{:S(2)}, u32[]{:S(2)}) %collective-permute-start.10) | collective-permute-done | bytes 589856 | tf_op jit(solution)/shard_map/ppermute | solution.py:330
  136.9 1.0 multiply_convert_fusion
  (4 shorter events, 0.0 us)
Async XLA Ops:
  0.6 44.6 %collective-permute-start = (bf16[256,1152]{1,0:T(8,128)(2,1)}, bf16[256,1152]{1,0:T(8,128)(2,1)S(1)}, u32[]{:S(2)}, u32[]{:S(2)}) collective-permute-start(bf16[256,1152]{1,0:T(8,128)(2,1)} %image_0.3), channel_id=1, source_target_pairs={{0,1},{1,0},{2,3},{3,2},{4,5},{5,4},{6,7},{7,6},{8,9},{9,8},{10,11... | collective-permute-start | bytes 1769480 | tf_op jit(solution)/shard_map/ppermute | solution.py:281
  9.1 54.4 %collective-permute-start.1 = (bf16[256,1152]{1,0:T(8,128)(2,1)}, bf16[256,1152]{1,0:T(8,128)(2,1)S(1)}, u32[]{:S(2)}, u32[]{:S(2)}) collective-permute-start(bf16[256,1152]{1,0:T(8,128)(2,1)} %text_0.3), channel_id=1, source_target_pairs={{1,2},{2,1},{3,0},{0,3},{5,6},{6,5},{7,4},{4,7},{9,10},{10,9},{11,... | collective-permute-start | bytes 1769480 | tf_op jit(solution)/shard_map/ppermute | solution.py:280
  19.9 1.1 copy-start
  21.0 1.1 copy-start.3
  22.1 0.7 copy-start.10
  24.4 41.1 %collective-permute-start.5 = (bf16[272,1152]{1,0:T(8,128)(2,1)}, bf16[272,1152]{1,0:T(8,128)(2,1)}, u32[]{:S(2)}, u32[]{:S(2)}) collective-permute-start(bf16[272,1152]{1,0:T(8,128)(2,1)} %get-tuple-element.14), channel_id=1, source_target_pairs={{4,0},{8,4},{12,8},{16,12},{20,16},{24,20},{28,24},{32,28},{36,32}... | collective-permute-start | bytes 1880072 | tf_op jit(solution)/shard_map/ppermute | solution.py:23
  27.5 38.0 %copy-start.11 = (s32[256]{0:T(256)S(1)}, s32[256]{0:T(256)}, u32[]{:S(2)}) copy-start(s32[256]{0:T(256)} %param.7) | copy-start | bytes 3076
  27.5 37.9 %collective-permute-start.3 = (bf16[256,1152]{1,0:T(8,128)(2,1)}, bf16[256,1152]{1,0:T(8,128)(2,1)}, u32[]{:S(2)}, u32[]{:S(2)}) collective-permute-start(bf16[256,1152]{1,0:T(8,128)(2,1)} %get-tuple-element.13), channel_id=1, source_target_pairs={{764,0},{0,4},{4,8},{8,12},{12,16},{16,20},{20,24},{24,28},{28,32}... | collective-permute-start | bytes 1769480 | tf_op jit(solution)/shard_map/ppermute | solution.py:23
  30.6 14.6 %collective-permute-start.2 = (s32[1,256]{1,0:T(1,128)S(1)}, s32[1,256]{1,0:T(1,128)S(1)}, u32[]{:S(2)}, u32[]{:S(2)}) collective-permute-start(s32[1,256]{1,0:T(1,128)S(1)} %bitcast.10), channel_id=1, source_target_pairs={{0,1},{1,0},{2,3},{3,2},{4,5},{5,4},{6,7},{7,6},{8,9},{9,8},{10,11... | collective-permute-start | bytes 3080 | tf_op jit(solution)/shard_map/ppermute | solution.py:290
  45.3 0.6 copy-start.8
  46.7 18.8 %copy-start.9 = (s32[1,256]{1,0:T(1,128)S(1)}, s32[1,256]{1,0:T(1,128)}, u32[]{:S(2)}) copy-start(s32[1,256]{1,0:T(1,128)} %copy-done.8) | copy-start | bytes 3076
  46.7 28.8 %collective-permute-start.6 = (bf16[272,1152]{1,0:T(8,128)(2,1)S(1)}, bf16[272,1152]{1,0:T(8,128)(2,1)S(1)}, u32[]{:S(2)}, u32[]{:S(2)}) collective-permute-start(bf16[272,1152]{1,0:T(8,128)(2,1)S(1)} %pack.1), channel_id=1, source_target_pairs={{4,0},{8,4},{12,8},{16,12},{20,16},{24,20},{28,24},{32,28},{36,32}... | collective-permute-start | bytes 1880072 | tf_op jit(solution)/shard_map/ppermute | solution.py:23
  63.5 12.0 %collective-permute-start.4 = (bf16[256,1152]{1,0:T(8,128)(2,1)S(1)}, bf16[256,1152]{1,0:T(8,128)(2,1)S(1)}, u32[]{:S(2)}, u32[]{:S(2)}) collective-permute-start(bf16[256,1152]{1,0:T(8,128)(2,1)S(1)} %gate.3.text_1), channel_id=1, source_target_pairs={{764,0},{0,4},{4,8},{8,12},{12,16},{16,20},{20,24},{24,28},{28,32}... | collective-permute-start | bytes 1769480 | tf_op jit(solution)/shard_map/ppermute | solution.py:23
  65.5 1.1 copy-start.1
  66.6 1.1 copy-start.4
  75.5 14.8 %collective-permute-start.7 = (s32[1,256]{1,0:T(1,128)S(1)}, s32[1,256]{1,0:T(1,128)S(1)}, u32[]{:S(2)}, u32[]{:S(2)}) collective-permute-start(s32[1,256]{1,0:T(1,128)S(1)} %note.1), channel_id=1, source_target_pairs={{0,4},{256,260},{512,516},{252,248},{508,504},{764,760},{1,5},{257... | collective-permute-start | bytes 3080 | tf_op jit(solution)/shard_map/ppermute | solution.py:31
  79.2 0.8 copy-start.6
  90.3 0.6 copy-start.12
  90.9 41.0 %collective-permute-start.9 = (bf16[256,1152]{1,0:T(8,128)(2,1)}, bf16[256,1152]{1,0:T(8,128)(2,1)}, u32[]{:S(2)}, u32[]{:S(2)}) collective-permute-start(bf16[256,1152]{1,0:T(8,128)(2,1)} %gate.5), channel_id=1, source_target_pairs={{0,1},{1,0},{2,3},{3,2},{4,5},{5,4},{6,7},{7,6},{8,9},{9,8},{10,11... | collective-permute-start | bytes 1769480 | tf_op jit(solution)/shard_map/ppermute | solution.py:329
  93.7 1.1 copy-start.7
  94.7 42.2 %collective-permute-start.10 = (bf16[256,1152]{1,0:T(8,128)(2,1)S(1)}, bf16[256,1152]{1,0:T(8,128)(2,1)S(1)}, u32[]{:S(2)}, u32[]{:S(2)}) collective-permute-start(bf16[256,1152]{1,0:T(8,128)(2,1)S(1)} %gate.4.sent), channel_id=1, source_target_pairs={{1,2},{2,1},{3,0},{0,3},{5,6},{6,5},{7,4},{4,7},{9,10},{10,9},{11,... | collective-permute-start | bytes 1769480 | tf_op jit(solution)/shard_map/ppermute | solution.py:330
  100.0 1.1 copy-start.2
  101.1 1.1 copy-start.5
  108.7 22.6 %collective-permute-start.8 = (f32[1,256]{1,0:T(1,128)S(1)}, f32[1,256]{1,0:T(1,128)S(1)}, u32[]{:S(2)}, u32[]{:S(2)}) collective-permute-start(f32[1,256]{1,0:T(1,128)S(1)} %get-tuple-element.19), channel_id=1, source_target_pairs={{0,1},{1,0},{2,3},{3,2},{4,5},{5,4},{6,7},{7,6},{8,9},{9,8},{10,11... | collective-permute-start | bytes 3080 | tf_op jit(solution)/shard_map/ppermute | solution.py:331

commit v11 on v4

--- a/solution.py
+++ b/solution.py
@@ -13,7 +13,7 @@
 
 VMEM = pl.BlockSpec(memory_space=pltpu.VMEM)
 SMEM = pl.BlockSpec(memory_space=pltpu.SMEM)
-LIMIT = 40 * 1024 * 1024
+LIMIT = 20 * 1024 * 1024
 
 
 def from_behind(block, distance):
@@ -29,7 +29,7 @@
     return lax.dot_general(x, y, (((0,), (0,)), ((), ())), preferred_element_type=jnp.float32)
 
 
-def hold_kernel(images, texts, positive, images_out, texts_out):
+def hold_kernel(firsts, reals, images, texts, positive, images_out, texts_out):
     rows = images.shape[0]
     images_out[pl.ds(0, rows), :] = images[...]
     images_out[pl.ds(rows, TAIL), :] = jnp.zeros((TAIL, images.shape[1]), jnp.bfloat16)
@@ -210,8 +210,8 @@
     image_1 = lax.ppermute(images, "inner", IMAGE_PAIRS)
     near_0 = positive[None, :]
     images_later, texts_later = call(
-        hold_kernel, "hold", [VMEM] * 3, [long_shard, shard], 1
-    )(images, texts, near_0)
+        hold_kernel, "hold", [SMEM] * 2 + [VMEM] * 3, [long_shard, shard], 1
+    )(firsts, reals, images, texts, near_0)
     near_1 = lax.ppermute(near_0, "inner", IMAGE_PAIRS)
     prior_0 = from_behind(texts_later, 1)
     after_0 = from_behind(images_later, -1)

time: 130 us -> 129 us (level)
    ppermute x1, waiting for transfers between devices: 11.6 us -> 9.62 us  [per_device(): near_1 = lax.ppermute(near_0, 'inner', IMAGE_PAIRS)]
    ppermute x1, waiting for transfers between devices: 25.5 us -> 27.2 us  [per_device(): loss_back = lax.ppermute(loss_send, 'inner', IMAGE_PAIRS)]
where the time goes in v11:
time: 129 us; the launch traced here: 128 us
  starting transfers between devices  67.2 us (52%)
  waiting for transfers between devices  36.8 us (29%)
  Pallas kernels  14.6 us (11%)
  local copies, waits for them, and re-layouts  4.05 us (3%)
  other arithmetic  2.68 us (2%)
  between operations  2.15 us (2%)
    ppermute x5, starting transfers between devices, from_behind(): lax.ppermute(block, 'outer', [((i - distance) % count, i) for i in range(...  35.4 us
    ppermute x1, waiting for transfers between devices, per_device(): loss_back = lax.ppermute(loss_send, 'inner', IMAGE_PAIRS)  27.2 us
    ppermute x1, waiting for transfers between devices, per_device(): near_1 = lax.ppermute(near_0, 'inner', IMAGE_PAIRS)  9.62 us
    ppermute x1, starting transfers between devices, per_device(): text_1 = lax.ppermute(texts, 'inner', TEXT_PAIRS)  9.43 us
    ppermute x1, starting transfers between devices, per_device(): image_1 = lax.ppermute(images, 'inner', IMAGE_PAIRS)  8.45 us
    pallas_call x1, Pallas kernels, per_device(): call(late_kernel, 'late', [SMEM] * 2 + [VMEM] * 11 + [pl.BlockSpec(memory...  5.43 us
    ppermute x1, starting transfers between devices, per_device(): near_1 = lax.ppermute(near_0, 'inner', IMAGE_PAIRS)  4.92 us
    ppermute x1, starting transfers between devices, per_device(): text_back = lax.ppermute(text_send, 'inner', TEXT_PAIRS)  4.9 us
  transfers between devices with their start and end apart: 11, of which 2 were waited for; matrix products, arithmetic and copies ran while one was open for 1% of the time, Pallas kernels for 10%

profile of v11, /device:TPU:1, one launch (start us, length us, event | category | flops | bytes accessed | tf_op | source)
XLA Modules:
  0.0 127.5 jit_solution(4833889245961295375)
XLA Ops:
  0.6 8.4 %collective-permute-start = (bf16[256,1152]{1,0:T(8,128)(2,1)}, bf16[256,1152]{1,0:T(8,128)(2,1)S(1)}, u32[]{:S(2)}, u32[]{:S(2)}) collective-permute-start(bf16[256,1152]{1,0:T(8,128)(2,1)} %image_0.3), channel_id=1, source_target_pairs={{0,1},{1,0},{2,3},{3,2},{4,5},{5,4},{6,7},{7,6},{8,9},{9,8},{10,11... | collective-permute-start | bytes 1769480 | tf_op jit(solution)/shard_map/ppermute | solution.py:210
  9.1 9.4 %collective-permute-start.2 = (bf16[256,1152]{1,0:T(8,128)(2,1)}, bf16[256,1152]{1,0:T(8,128)(2,1)S(1)}, u32[]{:S(2)}, u32[]{:S(2)}) collective-permute-start(bf16[256,1152]{1,0:T(8,128)(2,1)} %text_0.3), channel_id=1, source_target_pairs={{1,2},{2,1},{3,0},{0,3},{5,6},{6,5},{7,4},{4,7},{9,10},{10,9},{11,... | collective-permute-start | bytes 1769480 | tf_op jit(solution)/shard_map/ppermute | solution.py:209
  19.9 0.1 pad_maximum_fusion.reals
  19.9 0.1 pad_add_fusion.firsts
  20.0 0.0 copy-start
  20.0 1.1 copy-done
  21.1 0.0 copy-start.2
  21.1 1.1 copy-done.2
  22.1 0.0 copy-start.6
  22.1 0.7 copy-done.6
  22.8 0.0 copy-start.1
  22.8 0.0 copy-start.3
  22.8 0.0 copy-start.7
  22.8 1.6 %hold.1 = (bf16[272,1152]{1,0:T(8,128)(2,1)}, bf16[256,1152]{1,0:T(8,128)(2,1)}) custom-call(s32[4]{0:T(128)S(1)} %pad_add_fusion.firsts, f32[2]{0:T(128)S(1)} %pad_maximum_fusion.reals, bf16[256,1152]{1,0:T(8,128)(2,1)S(1)} %copy-done, bf16[256,1152]{1,0:T(8,128)(2,1)S(1)} %copy-done.2, s32[1,256]{1,0:T(1,128)S(1)} %bitcast.9), custom_call_target="tpu_custom_call" | custom-call | flops 150994944 | bytes 1048576 | tf_op jit(solution)/shard_map/hold/pallas_call | solution.py:212
  24.5 3.1 %collective-permute-start.5 = (bf16[272,1152]{1,0:T(8,128)(2,1)}, bf16[272,1152]{1,0:T(8,128)(2,1)S(1)}, u32[]{:S(2)}, u32[]{:S(2)}) collective-permute-start(bf16[272,1152]{1,0:T(8,128)(2,1)} %get-tuple-element.14), channel_id=1, source_target_pairs={{4,0},{8,4},{12,8},{16,12},{20,16},{24,20},{28,24},{32,28},{36,32}... | collective-permute-start | bytes 1880072 | tf_op jit(solution)/shard_map/ppermute | solution.py:21
  27.6 3.1 %collective-permute-start.3 = (bf16[256,1152]{1,0:T(8,128)(2,1)}, bf16[256,1152]{1,0:T(8,128)(2,1)}, u32[]{:S(2)}, u32[]{:S(2)}) collective-permute-start(bf16[256,1152]{1,0:T(8,128)(2,1)} %get-tuple-element.13), channel_id=1, source_target_pairs={{764,0},{0,4},{4,8},{8,12},{12,16},{16,20},{20,24},{24,28},{28,32}... | collective-permute-start | bytes 1769480 | tf_op jit(solution)/shard_map/ppermute | solution.py:21
  30.7 4.9 %collective-permute-start.1 = (s32[1,256]{1,0:T(1,128)S(1)}, s32[1,256]{1,0:T(1,128)S(1)}, u32[]{:S(2)}, u32[]{:S(2)}) collective-permute-start(s32[1,256]{1,0:T(1,128)S(1)} %bitcast.10), channel_id=1, source_target_pairs={{0,1},{1,0},{2,3},{3,2},{4,5},{5,4},{6,7},{7,6},{8,9},{9,8},{10,11... | collective-permute-start | bytes 3080 | tf_op jit(solution)/shard_map/ppermute | solution.py:215
  35.6 9.6 %collective-permute-done.1.refs_1_.near_1 = s32[1,256]{1,0:T(1,128)S(1)} collective-permute-done((s32[1,256]{1,0:T(1,128)S(1)}, s32[1,256]{1,0:T(1,128)S(1)}, u32[]{:S(2)}, u32[]{:S(2)}) %collective-permute-start.1) | collective-permute-done | bytes 1056 | tf_op jit(solution)/shard_map/ppermute | solution.py:215
  45.3 0.0 copy-start.4
  45.3 0.0 collective-permute-done.refs_0_
  45.3 0.6 copy-done.4
  45.8 16.8 %collective-permute-start.6 = (bf16[256,1152]{1,0:T(8,128)(2,1)S(1)}, bf16[256,1152]{1,0:T(8,128)(2,1)S(1)}, u32[]{:S(2)}, u32[]{:S(2)}) collective-permute-start(bf16[256,1152]{1,0:T(8,128)(2,1)S(1)} %gate.1.image_1), channel_id=1, source_target_pairs={{4,0},{8,4},{12,8},{16,12},{20,16},{24,20},{28,24},{32,28},{36,32}... | collective-permute-start | bytes 1769480 | tf_op jit(solution)/shard_map/ppermute | solution.py:21
  62.6 0.0 collective-permute-done.2.text_1
  62.6 1.9 %collective-permute-start.4 = (bf16[256,1152]{1,0:T(8,128)(2,1)S(1)}, bf16[256,1152]{1,0:T(8,128)(2,1)S(1)}, u32[]{:S(2)}, u32[]{:S(2)}) collective-permute-start(bf16[256,1152]{1,0:T(8,128)(2,1)S(1)} %collective-permute-done.2.text_1), channel_id=1, source_target_pairs={{764,0},{0,4},{4,8},{8,12},{12,16},{16,20},{20,24},{24,28},{28,32}... | collective-permute-start | bytes 1769480 | tf_op jit(solution)/shard_map/ppermute | solution.py:21
  64.6 10.5 %collective-permute-start.7 = (s32[1,256]{1,0:T(1,128)}, s32[1,256]{1,0:T(1,128)S(1)}, u32[]{:S(2)}, u32[]{:S(2)}) collective-permute-start(s32[1,256]{1,0:T(1,128)} %copy-done.4), channel_id=1, source_target_pairs={{4,0},{8,4},{12,8},{16,12},{20,16},{24,20},{28,24},{32,28},{36,32}... | collective-permute-start | bytes 3080 | tf_op jit(solution)/shard_map/ppermute | solution.py:21
  75.0 0.0 collective-permute-done.3.prior_0
  75.0 0.0 collective-permute-done.5.after_0
  75.1 0.0 copy-done.1
  75.1 0.0 copy-done.3
  75.1 0.0 copy-done.7
  75.1 0.0 copy-start.5
  75.1 0.7 copy-done.5
  75.8 4.3 %first.1 = (f32[256,1152]{1,0:T(8,128)S(1)}, f32[256,1152]{1,0:T(8,128)S(1)}, f32[1,256]{1,0:T(1,128)S(1)}) custom-call(s32[4]{0:T(128)S(1)} %pad_add_fusion.firsts, f32[2]{0:T(128)S(1)} %pad_maximum_fusion.reals, bf16[256,1152]{1,0:T(8,128)(2,1)S(1)} %copy-done.1, bf16[256,1152]{1,0:T(8,128)(2,1)S(1)} %gate.1.image_1, bf16[256,1152]{1,0:T(8,128)(2,1)S(1)} %copy-done.3, ...), custom_call_target="tpu_custom_call" | custom-call | flops 1660944384 | bytes 1048576 | tf_op jit(solution)/shard_map/first/pallas_call | solution.py:223
  80.1 0.0 collective-permute-done.7.far_1
  80.1 0.0 collective-permute-done.6.after_1
  80.1 1.5 %text.1.sent = bf16[256,1152]{1,0:T(8,128)(2,1)S(1)} custom-call(s32[4]{0:T(128)S(1)} %pad_add_fusion.firsts, f32[2]{0:T(128)S(1)} %pad_maximum_fusion.reals, bf16[256,1152]{1,0:T(8,128)(2,1)S(1)} %collective-permute-done.2.text_1, bf16[256,1152]{1,0:T(8,128)(2,1)S(1)} %collective-permute-done.6.after_1, s32[1,256]{1,0:T(1,128)S(1)} %collective-permute-done.7.far_1, ...), custom_call_target="tpu_custom_call" | custom-call | flops 301989888 | bytes 1048576 | tf_op jit(solution)/shard_map/text/pallas_call | solution.py:226
  81.6 0.0 collective-permute-done.4.prior_1
  81.7 1.7 %image.1 = (bf16[256,1152]{1,0:T(8,128)(2,1)S(1)}, f32[1,256]{1,0:T(1,128)S(1)}) custom-call(s32[4]{0:T(128)S(1)} %pad_add_fusion.firsts, f32[2]{0:T(128)S(1)} %pad_maximum_fusion.reals, bf16[256,1152]{1,0:T(8,128)(2,1)S(1)} %gate.1.image_1, bf16[256,1152]{1,0:T(8,128)(2,1)S(1)} %collective-permute-done.4.prior_1, s32[1,256]{1,0:T(1,128)S(1)} %copy-done.5, ...), custom_call_target="tpu_custom_call" | custom-call | flops 301989888 | bytes 1048576 | tf_op jit(solution)/shard_map/image/pallas_call | solution.py:229
  83.4 1.9 %collective-permute-start.9 = (bf16[256,1152]{1,0:T(8,128)(2,1)S(1)}, bf16[256,1152]{1,0:T(8,128)(2,1)S(1)}, u32[]{:S(2)}, u32[]{:S(2)}) collective-permute-start(bf16[256,1152]{1,0:T(8,128)(2,1)S(1)} %get-tuple-element.18.image_sent), channel_id=1, source_target_pairs={{0,1},{1,0},{2,3},{3,2},{4,5},{5,4},{6,7},{7,6},{8,9},{9,8},{10,11... | collective-permute-start | bytes 1769480 | tf_op jit(solution)/shard_map/ppermute | solution.py:254
  85.3 4.9 %collective-permute-start.10 = (bf16[256,1152]{1,0:T(8,128)(2,1)S(1)}, bf16[256,1152]{1,0:T(8,128)(2,1)S(1)}, u32[]{:S(2)}, u32[]{:S(2)}) collective-permute-start(bf16[256,1152]{1,0:T(8,128)(2,1)S(1)} %text.1.sent), channel_id=1, source_target_pairs={{1,2},{2,1},{3,0},{0,3},{5,6},{6,5},{7,4},{4,7},{9,10},{10,9},{11,... | collective-permute-start | bytes 1769480 | tf_op jit(solution)/shard_map/ppermute | solution.py:255
  90.2 2.2 %collective-permute-start.8 = (f32[1,256]{1,0:T(1,128)S(1)}, f32[1,256]{1,0:T(1,128)S(1)}, u32[]{:S(2)}, u32[]{:S(2)}) collective-permute-start(f32[1,256]{1,0:T(1,128)S(1)} %get-tuple-element.20), channel_id=1, source_target_pairs={{0,1},{1,0},{2,3},{3,2},{4,5},{5,4},{6,7},{7,6},{8,9},{9,8},{10,11... | collective-permute-start | bytes 3080 | tf_op jit(solution)/shard_map/ppermute | solution.py:256
  92.4 5.4 %late.1 = (f32[256,1152]{1,0:T(8,128)S(1)}, f32[256,1152]{1,0:T(8,128)S(1)}, f32[1,256]{1,0:T(1,128)S(1)}) custom-call(s32[4]{0:T(128)S(1)} %pad_add_fusion.firsts, f32[2]{0:T(128)S(1)} %pad_maximum_fusion.reals, bf16[256,1152]{1,0:T(8,128)(2,1)S(1)} %copy-done.1, bf16[256,1152]{1,0:T(8,128)(2,1)S(1)} %gate.1.image_1, bf16[256,1152]{1,0:T(8,128)(2,1)S(1)} %copy-done.3, ...), custom_call_target="tpu_custom_call" | custom-call | flops 2264924160 | bytes 1048576 | tf_op jit(solution)/shard_map/late/pallas_call | solution.py:232
  97.8 27.2 %collective-permute-done.8 = f32[1,256]{1,0:T(1,128)S(1)} collective-permute-done((f32[1,256]{1,0:T(1,128)S(1)}, f32[1,256]{1,0:T(1,128)S(1)}, u32[]{:S(2)}, u32[]{:S(2)}) %collective-permute-start.8) | collective-permute-done | bytes 1056 | tf_op jit(solution)/shard_map/ppermute | solution.py:256
  125.0 0.6 add.37
  125.6 0.0 collective-permute-done.9
  125.6 1.0 multiply_convert_fusion.1
  126.6 0.0 collective-permute-done.10
  126.6 1.0 multiply_convert_fusion
  (1 shorter events, 0.0 us)
Async XLA Ops:
  0.6 44.6 %collective-permute-start = (bf16[256,1152]{1,0:T(8,128)(2,1)}, bf16[256,1152]{1,0:T(8,128)(2,1)S(1)}, u32[]{:S(2)}, u32[]{:S(2)}) collective-permute-start(bf16[256,1152]{1,0:T(8,128)(2,1)} %image_0.3), channel_id=1, source_target_pairs={{0,1},{1,0},{2,3},{3,2},{4,5},{5,4},{6,7},{7,6},{8,9},{9,8},{10,11... | collective-permute-start | bytes 1769480 | tf_op jit(solution)/shard_map/ppermute | solution.py:210
  9.1 53.5 %collective-permute-start.2 = (bf16[256,1152]{1,0:T(8,128)(2,1)}, bf16[256,1152]{1,0:T(8,128)(2,1)S(1)}, u32[]{:S(2)}, u32[]{:S(2)}) collective-permute-start(bf16[256,1152]{1,0:T(8,128)(2,1)} %text_0.3), channel_id=1, source_target_pairs={{1,2},{2,1},{3,0},{0,3},{5,6},{6,5},{7,4},{4,7},{9,10},{10,9},{11,... | collective-permute-start | bytes 1769480 | tf_op jit(solution)/shard_map/ppermute | solution.py:209
  20.0 1.1 copy-start
  21.1 1.1 copy-start.2
  22.1 0.7 copy-start.6
  22.8 52.2 %copy-start.1 = (bf16[256,1152]{1,0:T(8,128)(2,1)S(1)}, bf16[256,1152]{1,0:T(8,128)(2,1)}, u32[]{:S(2)}) copy-start(bf16[256,1152]{1,0:T(8,128)(2,1)} %image_0.3) | copy-start | bytes 1769476
  22.8 52.3 %copy-start.3 = (bf16[256,1152]{1,0:T(8,128)(2,1)S(1)}, bf16[256,1152]{1,0:T(8,128)(2,1)}, u32[]{:S(2)}) copy-start(bf16[256,1152]{1,0:T(8,128)(2,1)} %text_0.3) | copy-start | bytes 1769476
  22.8 52.3 %copy-start.7 = (s32[256]{0:T(256)S(1)}, s32[256]{0:T(256)}, u32[]{:S(2)}) copy-start(s32[256]{0:T(256)} %param.7) | copy-start | bytes 3076
  24.5 50.6 %collective-permute-start.5 = (bf16[272,1152]{1,0:T(8,128)(2,1)}, bf16[272,1152]{1,0:T(8,128)(2,1)S(1)}, u32[]{:S(2)}, u32[]{:S(2)}) collective-permute-start(bf16[272,1152]{1,0:T(8,128)(2,1)} %get-tuple-element.14), channel_id=1, source_target_pairs={{4,0},{8,4},{12,8},{16,12},{20,16},{24,20},{28,24},{32,28},{36,32}... | collective-permute-start | bytes 1880072 | tf_op jit(solution)/shard_map/ppermute | solution.py:21
  27.6 47.4 %collective-permute-start.3 = (bf16[256,1152]{1,0:T(8,128)(2,1)}, bf16[256,1152]{1,0:T(8,128)(2,1)}, u32[]{:S(2)}, u32[]{:S(2)}) collective-permute-start(bf16[256,1152]{1,0:T(8,128)(2,1)} %get-tuple-element.13), channel_id=1, source_target_pairs={{764,0},{0,4},{4,8},{8,12},{12,16},{16,20},{20,24},{24,28},{28,32}... | collective-permute-start | bytes 1769480 | tf_op jit(solution)/shard_map/ppermute | solution.py:21
  30.7 14.5 %collective-permute-start.1 = (s32[1,256]{1,0:T(1,128)S(1)}, s32[1,256]{1,0:T(1,128)S(1)}, u32[]{:S(2)}, u32[]{:S(2)}) collective-permute-start(s32[1,256]{1,0:T(1,128)S(1)} %bitcast.10), channel_id=1, source_target_pairs={{0,1},{1,0},{2,3},{3,2},{4,5},{5,4},{6,7},{7,6},{8,9},{9,8},{10,11... | collective-permute-start | bytes 3080 | tf_op jit(solution)/shard_map/ppermute | solution.py:215
  45.3 0.6 copy-start.4
  45.8 34.3 %collective-permute-start.6 = (bf16[256,1152]{1,0:T(8,128)(2,1)S(1)}, bf16[256,1152]{1,0:T(8,128)(2,1)S(1)}, u32[]{:S(2)}, u32[]{:S(2)}) collective-permute-start(bf16[256,1152]{1,0:T(8,128)(2,1)S(1)} %gate.1.image_1), channel_id=1, source_target_pairs={{4,0},{8,4},{12,8},{16,12},{20,16},{24,20},{28,24},{32,28},{36,32}... | collective-permute-start | bytes 1769480 | tf_op jit(solution)/shard_map/ppermute | solution.py:21
  62.6 19.0 %collective-permute-start.4 = (bf16[256,1152]{1,0:T(8,128)(2,1)S(1)}, bf16[256,1152]{1,0:T(8,128)(2,1)S(1)}, u32[]{:S(2)}, u32[]{:S(2)}) collective-permute-start(bf16[256,1152]{1,0:T(8,128)(2,1)S(1)} %collective-permute-done.2.text_1), channel_id=1, source_target_pairs={{764,0},{0,4},{4,8},{8,12},{12,16},{16,20},{20,24},{24,28},{28,32}... | collective-permute-start | bytes 1769480 | tf_op jit(solution)/shard_map/ppermute | solution.py:21
  64.6 15.5 %collective-permute-start.7 = (s32[1,256]{1,0:T(1,128)}, s32[1,256]{1,0:T(1,128)S(1)}, u32[]{:S(2)}, u32[]{:S(2)}) collective-permute-start(s32[1,256]{1,0:T(1,128)} %copy-done.4), channel_id=1, source_target_pairs={{4,0},{8,4},{12,8},{16,12},{20,16},{24,20},{28,24},{32,28},{36,32}... | collective-permute-start | bytes 3080 | tf_op jit(solution)/shard_map/ppermute | solution.py:21
  75.1 0.7 copy-start.5
  83.4 42.2 %collective-permute-start.9 = (bf16[256,1152]{1,0:T(8,128)(2,1)S(1)}, bf16[256,1152]{1,0:T(8,128)(2,1)S(1)}, u32[]{:S(2)}, u32[]{:S(2)}) collective-permute-start(bf16[256,1152]{1,0:T(8,128)(2,1)S(1)} %get-tuple-element.18.image_sent), channel_id=1, source_target_pairs={{0,1},{1,0},{2,3},{3,2},{4,5},{5,4},{6,7},{7,6},{8,9},{9,8},{10,11... | collective-permute-start | bytes 1769480 | tf_op jit(solution)/shard_map/ppermute | solution.py:254
  85.3 41.3 %collective-permute-start.10 = (bf16[256,1152]{1,0:T(8,128)(2,1)S(1)}, bf16[256,1152]{1,0:T(8,128)(2,1)S(1)}, u32[]{:S(2)}, u32[]{:S(2)}) collective-permute-start(bf16[256,1152]{1,0:T(8,128)(2,1)S(1)} %text.1.sent), channel_id=1, source_target_pairs={{1,2},{2,1},{3,0},{0,3},{5,6},{6,5},{7,4},{4,7},{9,10},{10,9},{11,... | collective-permute-start | bytes 1769480 | tf_op jit(solution)/shard_map/ppermute | solution.py:255
  90.2 34.8 %collective-permute-start.8 = (f32[1,256]{1,0:T(1,128)S(1)}, f32[1,256]{1,0:T(1,128)S(1)}, u32[]{:S(2)}, u32[]{:S(2)}) collective-permute-start(f32[1,256]{1,0:T(1,128)S(1)} %get-tuple-element.20), channel_id=1, source_target_pairs={{0,1},{1,0},{2,3},{3,2},{4,5},{5,4},{6,7},{7,6},{8,9},{9,8},{10,11... | collective-permute-start | bytes 3080 | tf_op jit(solution)/shard_map/ppermute | solution.py:256
